TPU v7x, 32 devices: a whole 2x2x4 slice. The times are simulated.
32 devices in a mesh: dp: 8 (over z, core), row: 2 (over x), col: 2 (over y).
Axes of the slice: x: 2, y: 2, z: 4, core: 2. Of those that a mesh axis runs over, the one named last changes fastest.
Arguments:
- hidden_in: float32 [25088, 768], P(('dp', 'row', 'col')), may hold values from -6 to 6
- qkv_weight: bfloat16 [2, 2, 768, 3, 768], P(None, None, ('dp', 'row'), None, 'col'), may hold values from -0.21875 to 0.21875
- out_weight: bfloat16 [2, 2, 768, 768], P(None, None, 'col', ('dp', 'row')), may hold values from -0.625 to 0.625
- up_weight: bfloat16 [2, 768, 3072], P(None, ('dp', 'row'), 'col'), may hold values from -0.21875 to 0.21875
- down_weight: bfloat16 [2, 3072, 768], P(None, 'col', ('dp', 'row')), may hold values from -0.109375 to 0.109375
- qv_bias: float32 [2, 2, 2, 768], P(None, None, None, 'col'), may hold values from -3 to 3
- out_bias: float32 [2, 2, 768], replicated, may hold values from -3 to 3
- up_bias: float32 [2, 3072], P(None, 'col'), may hold values from -3 to 3
- down_bias: float32 [2, 768], replicated, may hold values from -3 to 3
- norm_gain: float32 [2, 3, 768], replicated, may hold values from 0.25 to 1.75
- norm_shift: float32 [2, 3, 768], replicated, may hold values from -2 to 2
- cotangent: float32 [25088, 768], P(('dp', 'row', 'col')), may hold values from -6 to 6
Outputs:
- hidden_out: float32 [25088, 768], P(('dp', 'row', 'col'))
- grad_in: float32 [25088, 768], P(('dp', 'row', 'col'))
- grad_qkv_weight: float32 [2, 2, 768, 3, 768], P(None, None, ('dp', 'row'), None, 'col')
- grad_out_weight: float32 [2, 2, 768, 768], P(None, None, 'col', ('dp', 'row'))
- grad_up_weight: float32 [2, 768, 3072], P(None, ('dp', 'row'), 'col')
- grad_down_weight: float32 [2, 3072, 768], P(None, 'col', ('dp', 'row'))
- grad_qv_bias: float32 [2, 2, 2, 768], P(None, None, None, 'col')
- grad_out_bias: float32 [2, 2, 768], replicated
- grad_up_bias: float32 [2, 3072], P(None, 'col')
- grad_down_bias: float32 [2, 768], replicated
- grad_norm_gain: float32 [2, 3, 768], replicated
- grad_norm_shift: float32 [2, 3, 768], replicated
All inputs are finite; a program needn't handle non-finite values.
Results may differ from a plain program's by a relative error of at most 0.019.
Values may be sent and summed in bfloat16 or wider, within the bound.
No kernel may reach another device: no remote copies, remote signals or barrier semaphores. Data moves between devices by JAX's collectives and lax.ppermute only.
A program may use at most 320 MiB of HBM per device.

v0:
```python
import jax
import jax.numpy as jnp
from jax import lax
from jax.sharding import PartitionSpec as P

D = 768
FF = 3072
HEADS = 12
FRAMES = 16
PATCHES = 196


layer_eps = 1e-06


def partner(value, axis, apart):
    mask = 2**apart
    pairs = [(source, source ^ mask) for source in range(lax.axis_size(axis))]
    return lax.ppermute(value, axis, pairs)


def layer_norm(values, norm_gain, norm_shift):
    average = jnp.mean(values, axis=-1, keepdims=True)
    centred = values - average
    spread_sq = jnp.mean(centred * centred, axis=-1, keepdims=True)
    return centred * lax.rsqrt(spread_sq + layer_eps) * norm_gain + norm_shift


def exact_gelu(values):
    return jax.nn.gelu(values, approximate=False)


def pair_rows(rounded_value):
    return lax.all_gather(rounded_value, "col", axis=0, tiled=True)


def pair_sums(partial_rows):
    return lax.psum_scatter(
        partial_rows.astype(jnp.bfloat16), "col", scatter_dimension=0, tiled=True
    ).astype(jnp.float32)


def fetch_layer(qkv_weight, out_weight, up_weight, down_weight, layer_at):
    return (
        lax.all_gather(qkv_weight[layer_at], ("dp", "row"), axis=1, tiled=True),
        lax.all_gather(out_weight[layer_at], ("dp", "row"), axis=2, tiled=True),
        lax.all_gather(up_weight[layer_at], ("dp", "row"), axis=0, tiled=True),
        lax.all_gather(down_weight[layer_at], ("dp", "row"), axis=1, tiled=True),
    )


def split_heads(flat, head_count):
    return flat.reshape(flat.shape[:-1] + (head_count, flat.shape[-1] // head_count))


def merge_heads(heads_split):
    return heads_split.reshape(
        heads_split.shape[:-2] + (heads_split.shape[-2] * heads_split.shape[-1],)
    )


def to_patches(stacked):
    parity = lax.axis_index("row") % 2
    half_count = PATCHES // 2
    frame_grid = stacked.reshape(stacked.shape[0], FRAMES // 2, PATCHES, stacked.shape[-1])
    kept_part = lax.dynamic_slice_in_dim(frame_grid, parity * half_count, half_count, 2)
    sent_part = lax.dynamic_slice_in_dim(frame_grid, (1 - parity) * half_count, half_count, 2)
    received = partner(sent_part, "row", 0)
    assembled = jnp.where(
        parity == 0,
        jnp.concatenate([kept_part, received], 1),
        jnp.concatenate([received, kept_part], 1),
    )
    return jnp.swapaxes(assembled, 1, 2)


def to_frames(stacked):
    parity = lax.axis_index("row") % 2
    half_frames = FRAMES // 2
    patch_grid = jnp.swapaxes(stacked, 1, 2)
    kept_part = lax.dynamic_slice_in_dim(patch_grid, parity * half_frames, half_frames, 1)
    sent_part = lax.dynamic_slice_in_dim(patch_grid, (1 - parity) * half_frames, half_frames, 1)
    received = partner(sent_part, "row", 0)
    assembled = jnp.where(
        parity == 0,
        jnp.concatenate([kept_part, received], 2),
        jnp.concatenate([received, kept_part], 2),
    )
    return assembled.reshape(stacked.shape[0], half_frames * PATCHES, stacked.shape[-1])


def project_qkv(rows, weight, bias_pair):
    projected_output = jnp.einsum("nd,dte->tne", rows, weight, preferred_element_type=jnp.float32)
    offsets = jnp.stack([bias_pair[0], jnp.zeros_like(bias_pair[0]), bias_pair[1]], axis=0)
    return (projected_output + offsets[:, None, :]).astype(jnp.bfloat16)


def attend_core(queries, keys_all, values_all, score_scale):
    scores = (
        jnp.einsum("slhe,smhe->shlm", queries, keys_all, preferred_element_type=jnp.float32)
        * score_scale
    )
    row_max = jnp.max(scores, axis=-1, keepdims=True)
    log_total = row_max + jnp.log(jnp.sum(jnp.exp(scores - row_max), axis=-1, keepdims=True))
    weights_low = jnp.exp(scores - log_total).astype(jnp.bfloat16)
    attention_mixed = jnp.einsum(
        "shlm,smhe->slhe", weights_low, values_all, preferred_element_type=jnp.float32
    )
    return (attention_mixed.astype(jnp.bfloat16), log_total)


def attend_back(queries, keys_all, values_all, log_total, grad_mixed, score_scale):
    scores = (
        jnp.einsum("slhe,smhe->shlm", queries, keys_all, preferred_element_type=jnp.float32)
        * score_scale
    )
    probabilities = jnp.exp(scores - log_total)
    grad_weights = jnp.einsum(
        "slhe,smhe->shlm", grad_mixed, values_all, preferred_element_type=jnp.float32
    )
    grad_values = jnp.einsum(
        "shlm,slhe->smhe",
        probabilities.astype(jnp.bfloat16),
        grad_mixed,
        preferred_element_type=jnp.float32,
    )
    row_terms = jnp.sum(grad_weights * probabilities, axis=-1, keepdims=True)
    grad_scores = (probabilities * (grad_weights - row_terms)).astype(jnp.bfloat16)
    grad_queries = (
        jnp.einsum("shlm,smhe->slhe", grad_scores, keys_all, preferred_element_type=jnp.float32)
        * score_scale
    )
    grad_keys = (
        jnp.einsum("shlm,slhe->smhe", grad_scores, queries, preferred_element_type=jnp.float32)
        * score_scale
    )
    return jnp.stack(
        [
            grad_queries.astype(jnp.bfloat16),
            grad_keys.astype(jnp.bfloat16),
            grad_values.astype(jnp.bfloat16),
        ],
        axis=0,
    )


def project_back(rows, weight, grad_proj):
    weight_grad = jnp.einsum("nd,tne->dte", rows, grad_proj, preferred_element_type=jnp.float32)
    bias_grad = jnp.stack(
        [
            jnp.sum(grad_proj[0].astype(jnp.float32), axis=0),
            jnp.sum(grad_proj[2].astype(jnp.float32), axis=0),
        ],
        axis=0,
    )
    normed_grad = pair_sums(
        jnp.einsum("tne,dte->nd", grad_proj, weight, preferred_element_type=jnp.float32)
    )
    return (weight_grad, bias_grad, normed_grad)


def norm_back(values, norm_gain, norm_shift, grad_normed, grad_carry):
    normed_value, norm_pull = jax.vjp(layer_norm, values, norm_gain, norm_shift)
    grad_values, grad_gain, grad_shift = norm_pull(grad_normed)
    return (grad_carry + grad_values, grad_gain, grad_shift)


def layer_forward(hidden, weights, small_params):
    qkv_full, out_full, up_full, down_full = weights
    gains, shifts, bias_qv, bias_out, bias_up, bias_down = small_params
    head_count = HEADS // lax.axis_size("col")
    score_scale = (D // HEADS) ** (-0.5)
    normalised_input = layer_norm(hidden, gains[0], shifts[0])
    rows_one = pair_rows(normalised_input.astype(jnp.bfloat16))
    proj_one = project_qkv(rows_one, qkv_full[0], bias_qv[0])
    grids_one = split_heads(
        proj_one.reshape(3, FRAMES // 2, PATCHES, proj_one.shape[-1]), head_count
    )
    first_mixed_output, total_one = attend_core(
        grids_one[0], grids_one[1], grids_one[2], score_scale
    )
    flat_one = merge_heads(first_mixed_output).reshape(-1, proj_one.shape[-1])
    hidden_one = (
        hidden
        + pair_sums(jnp.dot(flat_one, out_full[0], preferred_element_type=jnp.float32))
        + bias_out[0]
    )
    normalised_input = layer_norm(hidden_one, gains[1], shifts[1])
    rows_two = pair_rows(normalised_input.astype(jnp.bfloat16))
    proj_two = project_qkv(rows_two, qkv_full[1], bias_qv[1])
    grids_two = split_heads(to_patches(proj_two), head_count)
    mixed_two, total_two = attend_core(grids_two[0], grids_two[1], grids_two[2], score_scale)
    flat_two = to_frames(merge_heads(mixed_two)[None])[0]
    hidden_two = (
        hidden_one
        + pair_sums(jnp.dot(flat_two, out_full[1], preferred_element_type=jnp.float32))
        + bias_out[1]
    )
    normalised_input = layer_norm(hidden_two, gains[2], shifts[2])
    rows_three = pair_rows(normalised_input.astype(jnp.bfloat16))
    inner_pre = jnp.dot(rows_three, up_full, preferred_element_type=jnp.float32) + bias_up
    activated = exact_gelu(inner_pre).astype(jnp.bfloat16)
    hidden_out = (
        hidden_two
        + pair_sums(jnp.dot(activated, down_full, preferred_element_type=jnp.float32))
        + bias_down
    )
    record = (
        hidden,
        hidden_one,
        hidden_two,
        rows_one,
        grids_one,
        total_one,
        flat_one,
        rows_two,
        grids_two,
        total_two,
        flat_two,
        rows_three,
        inner_pre,
        activated,
    )
    return (hidden_out, record)


def layer_backward(record, grad_out, weights, small_params):
    (
        hidden,
        hidden_one,
        hidden_two,
        rows_one,
        grids_one,
        total_one,
        flat_one,
        rows_two,
        grids_two,
        total_two,
        flat_two,
        rows_three,
        inner_pre,
        activated,
    ) = record
    qkv_full, out_full, up_full, down_full = weights
    gains, shifts, bias_qv, bias_out, bias_up, bias_down = small_params
    head_count = HEADS // lax.axis_size("col")
    score_scale = (D // HEADS) ** (-0.5)
    grad_down_bias = jnp.sum(grad_out, axis=0)
    grad_rows = pair_rows(grad_out.astype(jnp.bfloat16))
    grad_act = jnp.einsum("nd,fd->nf", grad_rows, down_full, preferred_element_type=jnp.float32)
    grad_down_w = jnp.einsum("nf,nd->fd", activated, grad_rows, preferred_element_type=jnp.float32)
    gelu_value, gelu_pull = jax.vjp(exact_gelu, inner_pre)
    grad_inner = gelu_pull(grad_act)[0].astype(jnp.bfloat16)
    grad_up_bias = jnp.sum(grad_inner.astype(jnp.float32), axis=0)
    grad_up_w = jnp.einsum("nd,nf->df", rows_three, grad_inner, preferred_element_type=jnp.float32)
    grad_normed = pair_sums(
        jnp.einsum("nf,df->nd", grad_inner, up_full, preferred_element_type=jnp.float32)
    )
    grad_two, gain_three, shift_three = norm_back(
        hidden_two, gains[2], shifts[2], grad_normed, grad_out
    )
    bias_grad_two = jnp.sum(grad_two, axis=0)
    grad_rows = pair_rows(grad_two.astype(jnp.bfloat16))
    grad_flat = jnp.einsum(
        "nd,cd->nc", grad_rows, out_full[1], preferred_element_type=jnp.float32
    ).astype(jnp.bfloat16)
    out_grad_two = jnp.einsum("nc,nd->cd", flat_two, grad_rows, preferred_element_type=jnp.float32)
    grad_mixed = split_heads(to_patches(grad_flat[None])[0], head_count)
    grads_moved = attend_back(
        grids_two[0], grids_two[1], grids_two[2], total_two, grad_mixed, score_scale
    )
    grad_proj_two = to_frames(merge_heads(grads_moved))
    qkv_grad_two, qv_grad_two, grad_normed = project_back(rows_two, qkv_full[1], grad_proj_two)
    grad_one, gain_two, shift_two = norm_back(
        hidden_one, gains[1], shifts[1], grad_normed, grad_two
    )
    bias_grad_one = jnp.sum(grad_one, axis=0)
    grad_rows = pair_rows(grad_one.astype(jnp.bfloat16))
    grad_flat = jnp.einsum(
        "nd,cd->nc", grad_rows, out_full[0], preferred_element_type=jnp.float32
    ).astype(jnp.bfloat16)
    out_grad_one = jnp.einsum("nc,nd->cd", flat_one, grad_rows, preferred_element_type=jnp.float32)
    grad_mixed = split_heads(
        grad_flat.reshape(FRAMES // 2, PATCHES, grad_flat.shape[-1]), head_count
    )
    grads_local = attend_back(
        grids_one[0], grids_one[1], grids_one[2], total_one, grad_mixed, score_scale
    )
    grad_proj_one = merge_heads(grads_local).reshape(3, -1, grad_flat.shape[-1])
    qkv_grad_one, qv_grad_one, grad_normed = project_back(rows_one, qkv_full[0], grad_proj_one)
    grad_input, gain_one, shift_one = norm_back(hidden, gains[0], shifts[0], grad_normed, grad_one)
    weight_part = (
        jnp.stack([qkv_grad_one, qkv_grad_two], axis=0),
        jnp.stack([out_grad_one, out_grad_two], axis=0),
        grad_up_w,
        grad_down_w,
    )
    small_part = (
        jnp.stack([gain_one, gain_two, gain_three], axis=0),
        jnp.stack([shift_one, shift_two, shift_three], axis=0),
        jnp.stack([qv_grad_one, qv_grad_two], axis=0),
        jnp.stack([bias_grad_one, bias_grad_two], axis=0),
        grad_up_bias,
        grad_down_bias,
    )
    return (grad_input, weight_part, small_part)


def rows_first(weight_part):
    qkv_term, out_term, up_term, down_term = weight_part
    model_rows = up_term.shape[0]
    return jnp.concatenate(
        [
            jnp.moveaxis(qkv_term, 1, 0).reshape(model_rows, -1),
            jnp.moveaxis(out_term, 2, 0).reshape(model_rows, -1),
            up_term,
            down_term.T,
        ],
        axis=1,
    )


def rows_back(summed_rows):
    own_rows = summed_rows.shape[0]
    head_cols = D // lax.axis_size("col")
    unit_cols = FF // lax.axis_size("col")
    qkv_cols = 6 * head_cols
    out_cols = 2 * head_cols
    qkv_shard = jnp.moveaxis(summed_rows[:, :qkv_cols].reshape(own_rows, 2, 3, head_cols), 0, 1)
    out_shard = jnp.moveaxis(
        summed_rows[:, qkv_cols : qkv_cols + out_cols].reshape(own_rows, 2, head_cols), 0, 2
    )
    up_shard = summed_rows[:, qkv_cols + out_cols : qkv_cols + out_cols + unit_cols]
    down_shard = summed_rows[:, qkv_cols + out_cols + unit_cols :].T
    return (qkv_shard, out_shard, up_shard, down_shard)


def shards(
    hidden_in,
    qkv_weight,
    out_weight,
    up_weight,
    down_weight,
    qv_bias,
    out_bias,
    up_bias,
    down_bias,
    norm_gain,
    norm_shift,
    cotangent,
):
    layer_total = qkv_weight.shape[0]
    hidden = hidden_in
    inputs_kept = []
    gathered = []
    for layer_at in range(layer_total):
        weights = fetch_layer(qkv_weight, out_weight, up_weight, down_weight, layer_at)
        gathered.append(weights)
        inputs_kept.append(hidden)
        small_params = (
            norm_gain[layer_at],
            norm_shift[layer_at],
            qv_bias[layer_at],
            out_bias[layer_at],
            up_bias[layer_at],
            down_bias[layer_at],
        )
        hidden, record = layer_forward(hidden, weights, small_params)
    grad_hidden = cotangent
    weight_shards = [None] * layer_total
    small_terms = [None] * layer_total
    for layer_at in reversed(range(layer_total)):
        weights = gathered[layer_at]
        small_params = (
            norm_gain[layer_at],
            norm_shift[layer_at],
            qv_bias[layer_at],
            out_bias[layer_at],
            up_bias[layer_at],
            down_bias[layer_at],
        )
        hidden_again, record = layer_forward(inputs_kept[layer_at], weights, small_params)
        grad_hidden, weight_part, small_part = layer_backward(
            record, grad_hidden, weights, small_params
        )
        small_terms[layer_at] = small_part
        moved = lax.all_to_all(
            rows_first(weight_part)[None].astype(jnp.bfloat16),
            ("dp", "row"),
            split_axis=1,
            concat_axis=0,
            tiled=True,
        ).astype(jnp.float32)
        weight_shards[layer_at] = rows_back(jnp.sum(moved, axis=0))
    grad_qkv = jnp.stack([weight_shards[layer_at][0] for layer_at in range(layer_total)], axis=0)
    grad_outw = jnp.stack([weight_shards[layer_at][1] for layer_at in range(layer_total)], axis=0)
    grad_upw = jnp.stack([weight_shards[layer_at][2] for layer_at in range(layer_total)], axis=0)
    grad_downw = jnp.stack([weight_shards[layer_at][3] for layer_at in range(layer_total)], axis=0)
    col_at = lax.axis_index("col")
    gain_terms = jnp.stack([small_terms[layer_at][0] for layer_at in range(layer_total)], axis=0)
    shift_terms = jnp.stack([small_terms[layer_at][1] for layer_at in range(layer_total)], axis=0)
    qv_terms = jnp.stack([small_terms[layer_at][2] for layer_at in range(layer_total)], axis=0)
    outb_terms = jnp.stack([small_terms[layer_at][3] for layer_at in range(layer_total)], axis=0)
    upb_terms = jnp.stack([small_terms[layer_at][4] for layer_at in range(layer_total)], axis=0)
    downb_terms = jnp.stack([small_terms[layer_at][5] for layer_at in range(layer_total)], axis=0)
    qv_width = qv_terms.shape[-1]
    up_width = upb_terms.shape[-1]
    qv_padded = lax.dynamic_update_slice_in_dim(
        jnp.zeros(qv_terms.shape[:-1] + (qv_width * lax.axis_size("col"),), jnp.float32),
        qv_terms,
        col_at * qv_width,
        3,
    )
    up_padded = lax.dynamic_update_slice_in_dim(
        jnp.zeros((layer_total, up_width * lax.axis_size("col")), jnp.float32),
        upb_terms,
        col_at * up_width,
        1,
    )
    summed = lax.psum(
        (gain_terms, shift_terms, qv_padded, outb_terms, up_padded, downb_terms),
        ("dp", "row", "col"),
    )
    grad_qv = lax.dynamic_slice_in_dim(summed[2], col_at * qv_width, qv_width, 3)
    grad_upb = lax.dynamic_slice_in_dim(summed[4], col_at * up_width, up_width, 1)
    return (
        hidden,
        grad_hidden,
        grad_qkv,
        grad_outw,
        grad_upw,
        grad_downw,
        grad_qv,
        summed[3],
        grad_upb,
        summed[5],
        summed[0],
        summed[1],
    )


def solution(mesh):
    return jax.shard_map(
        shards,
        mesh=mesh,
        in_specs=(
            P(("dp", "row", "col"), None),
            P(None, None, ("dp", "row"), None, "col"),
            P(None, None, "col", ("dp", "row")),
            P(None, ("dp", "row"), "col"),
            P(None, "col", ("dp", "row")),
            P(None, None, None, "col"),
            P(),
            P(None, "col"),
            P(),
            P(),
            P(),
            P(("dp", "row", "col"), None),
        ),
        out_specs=(
            P(("dp", "row", "col"), None),
            P(("dp", "row", "col"), None),
            P(None, None, ("dp", "row"), None, "col"),
            P(None, None, "col", ("dp", "row")),
            P(None, ("dp", "row"), "col"),
            P(None, "col", ("dp", "row")),
            P(None, None, None, "col"),
            P(),
            P(None, "col"),
            P(),
            P(),
            P(),
        ),
        check_vma=False,
    )
```

profile of v0, /device:TPU:0, one launch (start us, length us, event | category | flops | bytes accessed | tf_op | source)
XLA Modules:
  0.0 2562.4 jit_solution(12861056100415857821)
XLA Ops:
  15.9 37.0 %all-gather.29.cloned.1.call-done = bf16[1568,768]{1,0:T(8,128)(2,1)} async-done(((bf16[784,768]{1,0:T(8,128)(2,1)}), bf16[1568,768]{1,0:T(8,128)(2,1)}) %all-gather.29.cloned.1.call-update) | async-done | bytes 2408464 | tf_op jit(solution)/shard_map/all_gather | solution.py:34
  52.8 50.4 %all-gather.53.cloned.1.call-done = bf16[1,2,768,3,384]{4,2,3,1,0:T(8,128)(2,1)} async-done(((bf16[1,2,48,3,384]{4,2,3,1,0:T(8,128)(2,1)}), bf16[1,2,768,3,384]{4,2,3,1,0:T(8,128)(2,1)}) %all-gather.53.cloned.1.call-update) | async-done | bytes 3538960 | tf_op jit(solution)/shard_map/all_gather | solution.py:45
  159.7 32.9 %reduce-scatter.13.cloned.1.call-done = bf16[784,768]{1,0:T(8,128)(2,1)} async-done(((bf16[1568,768]{1,0:T(8,128)(2,1)}), bf16[784,768]{1,0:T(8,128)(2,1)}) %reduce-scatter.13.cloned.1.call-update) | async-done | bytes 1204240 | tf_op jit(solution)/shard_map/reduce_scatter | solution.py:38
  197.3 36.7 %all-gather.31.cloned.1.call-done = bf16[1568,768]{1,0:T(8,128)(2,1)} async-done(((bf16[784,768]{1,0:T(8,128)(2,1)}), bf16[1568,768]{1,0:T(8,128)(2,1)}) %all-gather.31.cloned.1.call-update) | async-done | bytes 2408464 | tf_op jit(solution)/shard_map/all_gather | solution.py:34
  254.1 40.0 %collective-permute-done = bf16[3,8,98,384]{3,1,2,0:T(8,128)(2,1)} collective-permute-done((bf16[3,8,98,384]{3,1,2,0:T(8,128)(2,1)}, bf16[3,8,98,384]{3,1,2,0:T(8,128)(2,1)}, u32[]{:S(2)}, u32[]{:S(2)}) %collective-permute-start) | collective-permute-done | bytes 1806368 | tf_op jit(solution)/shard_map/ppermute | solution.py:19
  342.0 13.0 collective-permute-done.1
  363.8 34.6 %reduce-scatter.15.cloned.1.call-done = bf16[784,768]{1,0:T(8,128)(2,1)} async-done(((bf16[1568,768]{1,0:T(8,128)(2,1)}), bf16[784,768]{1,0:T(8,128)(2,1)}) %reduce-scatter.15.cloned.1.call-update) | async-done | bytes 1204240 | tf_op jit(solution)/shard_map/reduce_scatter | solution.py:38
  404.5 39.0 %all-gather.57.cloned.1.call-done = bf16[1,768,1536]{2,1,0:T(8,128)(2,1)} async-done(((bf16[1,48,1536]{2,1,0:T(8,128)(2,1)}), bf16[1,768,1536]{2,1,0:T(8,128)(2,1)}) %all-gather.57.cloned.1.call-update) | async-done | bytes 2359312 | tf_op jit(solution)/shard_map/all_gather | solution.py:47
  443.5 37.6 %all-gather.33.cloned.1.call-done = bf16[1568,768]{1,0:T(8,128)(2,1)} async-done(((bf16[784,768]{1,0:T(8,128)(2,1)}), bf16[1568,768]{1,0:T(8,128)(2,1)}) %all-gather.33.cloned.1.call-update) | async-done | bytes 2408464 | tf_op jit(solution)/shard_map/all_gather | solution.py:34
  481.1 27.5 %multiply_convert_fusion.3 = (bf16[1568,1536]{1,0:T(8,128)(2,1)}, f32[1568,1536]{1,0:T(8,128)}, f32[1568,1536]{1,0:T(8,128)}) fusion(f32[1536]{0:T(1024)S(1)} %get-tuple-element.77, bf16[1568,768]{1,0:T(8,128)(2,1)} %all-gather.33.cloned.1.call-done, bf16[1,768,1536]{2,1,0:T(8,128)(2,1)} %all-gather.57.cloned.1.call-done), kind=kOutput, calls=%fused_computation.33 | convolution fusion | flops 3858333696 | bytes 28858368 | tf_op jit(solution)/shard_map/dot_general | solution.py:201
  508.6 17.1 all-gather.59.cloned.1.call-done
  525.7 8.5 convolution_convert_fusion.11
  535.6 32.8 %reduce-scatter.17.cloned.1.call-done = bf16[784,768]{1,0:T(8,128)(2,1)} async-done(((bf16[1568,768]{1,0:T(8,128)(2,1)}), bf16[784,768]{1,0:T(8,128)(2,1)}) %reduce-scatter.17.cloned.1.call-update) | async-done | bytes 1204240 | tf_op jit(solution)/shard_map/reduce_scatter | solution.py:38
  574.3 44.7 %all-gather.61.cloned.1.call-done = bf16[1,2,768,3,384]{4,2,3,1,0:T(8,128)(2,1)} async-done(((bf16[1,2,48,3,384]{4,2,3,1,0:T(8,128)(2,1)}), bf16[1,2,768,3,384]{4,2,3,1,0:T(8,128)(2,1)}) %all-gather.61.cloned.1.call-update) | async-done | bytes 3538960 | tf_op jit(solution)/shard_map/all_gather | solution.py:45
  619.1 37.6 %all-gather.35.cloned.1.call-done = bf16[1568,768]{1,0:T(8,128)(2,1)} async-done(((bf16[784,768]{1,0:T(8,128)(2,1)}), bf16[1568,768]{1,0:T(8,128)(2,1)}) %all-gather.35.cloned.1.call-update) | async-done | bytes 2408464 | tf_op jit(solution)/shard_map/all_gather | solution.py:34
  703.4 35.1 %reduce-scatter.19.cloned.1.call-done = bf16[784,768]{1,0:T(8,128)(2,1)} async-done(((bf16[1568,768]{1,0:T(8,128)(2,1)}), bf16[784,768]{1,0:T(8,128)(2,1)}) %reduce-scatter.19.cloned.1.call-update) | async-done | bytes 1204240 | tf_op jit(solution)/shard_map/reduce_scatter | solution.py:38
  747.0 36.7 %all-gather.37.cloned.1.call-done = bf16[1568,768]{1,0:T(8,128)(2,1)} async-done(((bf16[784,768]{1,0:T(8,128)(2,1)}), bf16[1568,768]{1,0:T(8,128)(2,1)}) %all-gather.37.cloned.1.call-update) | async-done | bytes 2408464 | tf_op jit(solution)/shard_map/all_gather | solution.py:34
  802.2 39.7 %collective-permute-done.2 = bf16[3,8,98,384]{3,1,2,0:T(8,128)(2,1)S(1)} collective-permute-done((bf16[3,8,98,384]{3,1,2,0:T(8,128)(2,1)S(1)}, bf16[3,8,98,384]{3,1,2,0:T(8,128)(2,1)S(1)}, u32[]{:S(2)}, u32[]{:S(2)}) %collective-permute-start.2) | collective-permute-done | bytes 1806368 | tf_op jit(solution)/shard_map/ppermute | solution.py:19
  888.2 13.0 collective-permute-done.3
  909.8 34.8 %reduce-scatter.21.cloned.1.call-done = bf16[784,768]{1,0:T(8,128)(2,1)} async-done(((bf16[1568,768]{1,0:T(8,128)(2,1)}), bf16[784,768]{1,0:T(8,128)(2,1)}) %reduce-scatter.21.cloned.1.call-update) | async-done | bytes 1204240 | tf_op jit(solution)/shard_map/reduce_scatter | solution.py:38
  950.6 39.2 %all-gather.65.cloned.1.call-done = bf16[1,768,1536]{2,1,0:T(8,128)(2,1)} async-done(((bf16[1,48,1536]{2,1,0:T(8,128)(2,1)}), bf16[1,768,1536]{2,1,0:T(8,128)(2,1)}) %all-gather.65.cloned.1.call-update) | async-done | bytes 2359312 | tf_op jit(solution)/shard_map/all_gather | solution.py:47
  989.8 37.5 %all-gather.39.cloned.1.call-done = bf16[1568,768]{1,0:T(8,128)(2,1)} async-done(((bf16[784,768]{1,0:T(8,128)(2,1)}), bf16[1568,768]{1,0:T(8,128)(2,1)}) %all-gather.39.cloned.1.call-update) | async-done | bytes 2408464 | tf_op jit(solution)/shard_map/all_gather | solution.py:34
  1027.3 27.8 %multiply_convert_fusion.2 = (bf16[1568,1536]{1,0:T(8,128)(2,1)}, f32[1568,1536]{1,0:T(8,128)}, f32[1568,1536]{1,0:T(8,128)}) fusion(f32[1536]{0:T(1024)S(1)} %copy-done.165, bf16[1568,768]{1,0:T(8,128)(2,1)} %all-gather.39.cloned.1.call-done, bf16[1,768,1536]{2,1,0:T(8,128)(2,1)} %all-gather.65.cloned.1.call-done), kind=kOutput, calls=%fused_computation.20 | convolution fusion | flops 3858333696 | bytes 28858368 | tf_op jit(solution)/shard_map/dot_general | solution.py:201
  1055.1 17.0 all-gather.67.cloned.1.call-done
  1072.1 36.9 %all-gather.41.cloned.1.call-done = bf16[1568,768]{1,0:T(8,128)(2,1)} async-done(((bf16[784,768]{1,0:T(8,128)(2,1)}), bf16[1568,768]{1,0:T(8,128)(2,1)}) %all-gather.41.cloned.1.call-update) | async-done | bytes 2408464 | tf_op jit(solution)/shard_map/all_gather | solution.py:34
  1109.1 13.7 convert_reduce_fusion.2
  1131.7 7.7 convolution_convert_fusion.10
  1139.5 26.0 %reduce-scatter.25.cloned.1.call-done = bf16[784,768]{1,0:T(8,128)(2,1)} async-done(((bf16[1568,768]{1,0:T(8,128)(2,1)}), bf16[784,768]{1,0:T(8,128)(2,1)}) %reduce-scatter.25.cloned.1.call-update) | async-done | bytes 1204240 | tf_op jit(solution)/shard_map/reduce_scatter | solution.py:38
  1170.2 32.8 %reduce-scatter.23.cloned.1.call-done = bf16[784,768]{1,0:T(8,128)(2,1)} async-done(((bf16[1568,768]{1,0:T(8,128)(2,1)}), bf16[784,768]{1,0:T(8,128)(2,1)}) %reduce-scatter.23.cloned.1.call-update) | async-done | bytes 1204240 | tf_op jit(solution)/shard_map/reduce_scatter | solution.py:38
  1210.4 36.7 %all-gather.43.cloned.1.call-done = bf16[1568,768]{1,0:T(8,128)(2,1)} async-done(((bf16[784,768]{1,0:T(8,128)(2,1)}), bf16[1568,768]{1,0:T(8,128)(2,1)}) %all-gather.43.cloned.1.call-update) | async-done | bytes 2408464 | tf_op jit(solution)/shard_map/all_gather | solution.py:34
  1252.6 13.9 collective-permute-done.4
  1309.6 39.1 %collective-permute-done.5 = bf16[3,8,98,384]{3,1,2,0:T(8,128)(2,1)} collective-permute-done((bf16[3,8,98,384]{3,1,2,0:T(8,128)(2,1)}, bf16[3,8,98,384]{3,1,2,0:T(8,128)(2,1)}, u32[]{:S(2)}, u32[]{:S(2)}) %collective-permute-start.5) | collective-permute-done | bytes 1806368 | tf_op jit(solution)/shard_map/ppermute | solution.py:19
  1353.0 7.5 maximum_select_fusion
  1380.0 35.3 %reduce-scatter.27.cloned.1.call-done = bf16[784,768]{1,0:T(8,128)(2,1)} async-done(((bf16[1568,768]{1,0:T(8,128)(2,1)}), bf16[784,768]{1,0:T(8,128)(2,1)}) %reduce-scatter.27.cloned.1.call-update) | async-done | bytes 1204240 | tf_op jit(solution)/shard_map/reduce_scatter | solution.py:38
  1424.4 36.7 %all-gather.45.cloned.1.call-done = bf16[1568,768]{1,0:T(8,128)(2,1)} async-done(((bf16[784,768]{1,0:T(8,128)(2,1)}), bf16[1568,768]{1,0:T(8,128)(2,1)}) %all-gather.45.cloned.1.call-update) | async-done | bytes 2408464 | tf_op jit(solution)/shard_map/all_gather | solution.py:34
  1471.3 7.7 convert_reduce_fusion.12
  1479.0 7.4 multiply_reduce_fusion.1
  1486.4 11.6 multiply_convert_fusion.1
  1535.2 35.3 %reduce-scatter.29.cloned.1.call-done = bf16[784,768]{1,0:T(8,128)(2,1)} async-done(((bf16[1568,768]{1,0:T(8,128)(2,1)}), bf16[784,768]{1,0:T(8,128)(2,1)}) %reduce-scatter.29.cloned.1.call-update) | async-done | bytes 1204240 | tf_op jit(solution)/shard_map/reduce_scatter | solution.py:38
  1579.6 36.7 %all-gather.47.cloned.1.call-done = bf16[1568,768]{1,0:T(8,128)(2,1)} async-done(((bf16[784,768]{1,0:T(8,128)(2,1)}), bf16[1568,768]{1,0:T(8,128)(2,1)}) %all-gather.47.cloned.1.call-update) | async-done | bytes 2408464 | tf_op jit(solution)/shard_map/all_gather | solution.py:34
  1616.4 12.0 convert_reduce_fusion.3
  1635.8 35.3 %reduce-scatter.31.cloned.1.call-done = bf16[784,768]{1,0:T(8,128)(2,1)} async-done(((bf16[1568,768]{1,0:T(8,128)(2,1)}), bf16[784,768]{1,0:T(8,128)(2,1)}) %reduce-scatter.31.cloned.1.call-update) | async-done | bytes 1204240 | tf_op jit(solution)/shard_map/reduce_scatter | solution.py:38
  1681.1 8.3 fusion.24
  1689.4 27.5 %all-gather.49.cloned.1.call-done = bf16[1568,768]{1,0:T(8,128)(2,1)} async-done(((bf16[784,768]{1,0:T(8,128)(2,1)}), bf16[1568,768]{1,0:T(8,128)(2,1)}) %all-gather.49.cloned.1.call-update) | async-done | bytes 2408464 | tf_op jit(solution)/shard_map/all_gather | solution.py:34
  1722.5 8.3 fusion.25
  1736.5 12.2 copy.273
  1806.4 13.8 copy.270
  1826.1 9.8 collective-permute-done.7
  1840.2 9.3 maximum_select_fusion.1
  1861.8 7.3 bitcast_convert_fusion.1
  1869.1 49.4 %fusion.145 = bf16[768,1,6144]{2,1,0:T(2,128)(2,1)} fusion(bf16[1,768,1536]{2,0,1:T(2,128)(2,1)} %copy.273, bf16[1,768,1536]{2,0,1:T(2,128)(2,1)} %copy.272, bf16[1,768,768]{2,0,1:T(2,128)(2,1)S(1)} %copy.271, bf16[1,768,2304]{2,0,1:T(2,128)(2,1)} %copy.270), kind=kLoop, calls=%fused_computation.415 | loop fusion | flops 37748736 | bytes 18874368
  1919.1 57.3 %reduce.56 = bf16[768,6144]{1,0:T(8,128)(2,1)} reduce(bf16[768,1,6144]{2,1,0:T(2,128)(2,1)} %fusion.145, bf16[]{:T(256)} %broadcast.694), dimensions={1}, to_apply=%fusion.145.reduce_sub_computation | reduce | bytes 18874370
  1976.3 15.2 reshape.897
  2067.1 7.5 multiply_reduce_fusion
  2074.6 11.7 multiply_convert_fusion
  2118.4 13.9 copy.265
  2138.2 49.4 %fusion.146 = bf16[768,1,6144]{2,1,0:T(2,128)(2,1)} fusion(bf16[1,768,1536]{2,0,1:T(2,128)(2,1)} %copy.268, bf16[1,768,1536]{2,0,1:T(2,128)(2,1)} %copy.267, bf16[1,768,768]{2,0,1:T(2,128)(2,1)S(1)} %copy.266, bf16[1,768,2304]{2,0,1:T(2,128)(2,1)} %copy.265), kind=kLoop, calls=%fused_computation.416 | loop fusion | flops 37748736 | bytes 18874368
  2187.6 57.2 %reduce.57 = bf16[768,6144]{1,0:T(8,128)(2,1)} reduce(bf16[768,1,6144]{2,1,0:T(2,128)(2,1)} %fusion.146, bf16[]{:T(256)} %broadcast.694), dimensions={1}, to_apply=%fusion.146.reduce_sub_computation | reduce | bytes 18874370
  2244.8 15.2 reshape.899
  2279.9 17.6 reshape.898
  2297.4 12.1 copy.274
  2324.5 188.5 %all-reduce.3.cloned.1.call-done = (f32[2,2,2,768]{3,2,1,0:T(2,128)}, f32[2,2,768]{2,1,0:T(2,128)}, f32[2,3072]{1,0:T(2,128)}, f32[2,768]{1,0:T(2,128)}, f32[2,3,768]{2,1,0:T(4,128)}, /*index=5*/f32[2,3,768]{2,1,0:T(4,128)}) async-done(((f32[2,2,2,768]{3,2,1,0:T(2,128)}, f32[2,2,768]{2,1,0:T(2,128)}, f32[2,3072]{1,0:T(2,128)}, f32[2,768]{1,0:T(2,128)}, f32[2,3,768]{2,1,0:T(4,128)}, ...) | async-done | bytes 104464 | tf_op jit(solution)/shard_map/psum | solution.py:420
  2518.4 17.4 reshape.900
  2535.8 12.3 copy.269
  (804 shorter events, 721.1 us)
Async XLA Ops:
  7.2 45.7 %all-gather.29.cloned.1.call-start = ((), (), s32[]{:S(2)}) async-start(), calls=%async_computation.14 | async-start | bytes 3612672 | tf_op jit(solution)/shard_map/all_gather | solution.py:34
  8.8 186.0 %copy-start.107 = (f32[768]{0:T(1024)}, f32[768]{0:T(1024)S(1)}, u32[]{:S(2)}) copy-start(f32[768]{0:T(1024)S(1)} %get-tuple-element.67) | copy-start | bytes 9220
  8.8 392.7 %copy-start.109 = (f32[768]{0:T(1024)}, f32[768]{0:T(1024)S(1)}, u32[]{:S(2)}) copy-start(f32[768]{0:T(1024)S(1)} %get-tuple-element.66) | copy-start | bytes 9220
  13.4 89.9 %all-gather.53.cloned.1.call-start = ((), (), s32[]{:S(2)}) async-start(), calls=%async_computation.38 | async-start | bytes 3760128 | tf_op jit(solution)/shard_map/all_gather | solution.py:45
  14.3 139.7 %all-gather.55.cloned.1.call-start = ((), (), s32[]{:S(2)}) async-start(), calls=%async_computation.39 | async-start | bytes 1253376 | tf_op jit(solution)/shard_map/all_gather | solution.py:46
  15.0 177.6 %reduce-scatter.13.cloned.1.call-start = ((), (), s32[]{:S(2)}) async-start(), calls=%async_computation.15 | async-start | bytes 3612672 | tf_op jit(solution)/shard_map/reduce_scatter | solution.py:38
  158.4 75.6 %all-gather.31.cloned.1.call-start = ((), (), s32[]{:S(2)}) async-start(), calls=%async_computation.16 | async-start | bytes 3612672 | tf_op jit(solution)/shard_map/all_gather | solution.py:34
  197.2 201.1 %reduce-scatter.15.cloned.1.call-start = ((), (), s32[]{:S(2)}) async-start(), calls=%async_computation.17 | async-start | bytes 3612672 | tf_op jit(solution)/shard_map/reduce_scatter | solution.py:38
  252.7 41.5 %collective-permute-start = (bf16[3,8,98,384]{3,1,2,0:T(8,128)(2,1)}, bf16[3,8,98,384]{3,1,2,0:T(8,128)(2,1)}, u32[]{:S(2)}, u32[]{:S(2)}) collective-permute-start(bf16[3,8,98,384]{3,1,2,0:T(8,128)(2,1)} %copy.163), channel_id=1, source_target_pairs={{0,2},{2,0},{1,3},{3,1},{4,6},{6,4},{5,7},{7,5},{8,10},{10,8},{9,1... | collective-permute-start | bytes 5419016 | tf_op jit(solution)/shard_map/ppermute | solution.py:19
  340.4 14.5 collective-permute-start.1
  363.0 80.6 %all-gather.57.cloned.1.call-start = ((), (), s32[]{:S(2)}) async-start(), calls=%async_computation.40 | async-start | bytes 2506752 | tf_op jit(solution)/shard_map/all_gather | solution.py:47
  363.8 117.3 %all-gather.33.cloned.1.call-start = ((), (), s32[]{:S(2)}) async-start(), calls=%async_computation.18 | async-start | bytes 3612672 | tf_op jit(solution)/shard_map/all_gather | solution.py:34
  403.0 122.6 %all-gather.59.cloned.1.call-start = ((), (), s32[]{:S(2)}) async-start(), calls=%async_computation.41 | async-start | bytes 2506752 | tf_op jit(solution)/shard_map/all_gather | solution.py:48
  403.8 164.5 %reduce-scatter.17.cloned.1.call-start = ((), (), s32[]{:S(2)}) async-start(), calls=%async_computation.19 | async-start | bytes 3612672 | tf_op jit(solution)/shard_map/reduce_scatter | solution.py:38
  534.2 84.9 %all-gather.61.cloned.1.call-start = ((), (), s32[]{:S(2)}) async-start(), calls=%async_computation.42 | async-start | bytes 3760128 | tf_op jit(solution)/shard_map/all_gather | solution.py:45
  534.9 121.7 %all-gather.35.cloned.1.call-start = ((), (), s32[]{:S(2)}) async-start(), calls=%async_computation.20 | async-start | bytes 3612672 | tf_op jit(solution)/shard_map/all_gather | solution.py:34
  572.1 84.6 %copy-start.170 = (f32[3,384]{1,0:T(4,128)S(1)}, f32[3,384]{1,0:T(4,128)}, u32[]{:S(2)}) copy-start(f32[3,384]{1,0:T(4,128)} %get-tuple-element.167) | copy-start | bytes 13828
  573.6 124.7 %all-gather.63.cloned.1.call-start = ((), (), s32[]{:S(2)}) async-start(), calls=%async_computation.43 | async-start | bytes 1253376 | tf_op jit(solution)/shard_map/all_gather | solution.py:46
  574.3 164.3 %reduce-scatter.19.cloned.1.call-start = ((), (), s32[]{:S(2)}) async-start(), calls=%async_computation.21 | async-start | bytes 3612672 | tf_op jit(solution)/shard_map/reduce_scatter | solution.py:38
  703.2 80.6 %all-gather.37.cloned.1.call-start = ((), (), s32[]{:S(2)}) async-start(), calls=%async_computation.22 | async-start | bytes 3612672 | tf_op jit(solution)/shard_map/all_gather | solution.py:34
  745.5 38.3 %copy-start.169 = (f32[3,384]{1,0:T(4,128)S(1)}, f32[3,384]{1,0:T(4,128)}, u32[]{:S(2)}) copy-start(f32[3,384]{1,0:T(4,128)} %get-tuple-element.165) | copy-start | bytes 13828
  745.5 38.3 %copy-start.173 = (bf16[1,2,768,3,384]{4,2,3,1,0:T(8,128)(2,1)S(1)}, bf16[1,2,768,3,384]{4,2,3,1,0:T(8,128)(2,1)}, u32[]{:S(2)}) copy-start(bf16[1,2,768,3,384]{4,2,3,1,0:T(8,128)(2,1)} %all-gather.61.cloned.1.call-done) | copy-start | bytes 10616836
  747.0 197.6 %reduce-scatter.21.cloned.1.call-start = ((), (), s32[]{:S(2)}) async-start(), calls=%async_computation.23 | async-start | bytes 3612672 | tf_op jit(solution)/shard_map/reduce_scatter | solution.py:38
  800.7 41.2 %collective-permute-start.2 = (bf16[3,8,98,384]{3,1,2,0:T(8,128)(2,1)S(1)}, bf16[3,8,98,384]{3,1,2,0:T(8,128)(2,1)S(1)}, u32[]{:S(2)}, u32[]{:S(2)}) collective-permute-start(bf16[3,8,98,384]{3,1,2,0:T(8,128)(2,1)S(1)} %copy.186), channel_id=1, source_target_pairs={{0,2},{2,0},{1,3},{3,1},{4,6},{6,4},{5,7},{7,5},{8,10},{10,8},{9,1... | collective-permute-start | bytes 5419016 | tf_op jit(solution)/shard_map/ppermute | solution.py:19
  886.7 14.5 collective-permute-start.3
  909.1 80.7 %all-gather.65.cloned.1.call-start = ((), (), s32[]{:S(2)}) async-start(), calls=%async_computation.44 | async-start | bytes 2506752 | tf_op jit(solution)/shard_map/all_gather | solution.py:47
  909.7 117.6 %all-gather.39.cloned.1.call-start = ((), (), s32[]{:S(2)}) async-start(), calls=%async_computation.24 | async-start | bytes 3612672 | tf_op jit(solution)/shard_map/all_gather | solution.py:34
  947.7 79.6 %copy-start.165 = (f32[1536]{0:T(1024)S(1)}, f32[1536]{0:T(1024)}, u32[]{:S(2)}) copy-start(f32[1536]{0:T(1024)} %get-tuple-element.76) | copy-start | bytes 18436
  949.2 122.9 %all-gather.67.cloned.1.call-start = ((), (), s32[]{:S(2)}) async-start(), calls=%async_computation.45 | async-start | bytes 2506752 | tf_op jit(solution)/shard_map/all_gather | solution.py:48
  950.0 159.1 %all-gather.41.cloned.1.call-start = ((), (), s32[]{:S(2)}) async-start(), calls=%async_computation.26 | async-start | bytes 3612672 | tf_op jit(solution)/shard_map/all_gather | solution.py:34
  950.6 214.9 %reduce-scatter.25.cloned.1.call-start = ((), (), s32[]{:S(2)}) async-start(), calls=%async_computation.27 | async-start | bytes 3612672 | tf_op jit(solution)/shard_map/reduce_scatter | solution.py:38
  1130.1 72.9 %reduce-scatter.23.cloned.1.call-start = ((), (), s32[]{:S(2)}) async-start(), calls=%async_computation.25 | async-start | bytes 3612672 | tf_op jit(solution)/shard_map/reduce_scatter | solution.py:38
  1139.5 107.6 %all-gather.43.cloned.1.call-start = ((), (), s32[]{:S(2)}) async-start(), calls=%async_computation.28 | async-start | bytes 3612672 | tf_op jit(solution)/shard_map/all_gather | solution.py:34
  1210.3 205.0 %reduce-scatter.27.cloned.1.call-start = ((), (), s32[]{:S(2)}) async-start(), calls=%async_computation.29 | async-start | bytes 3612672 | tf_op jit(solution)/shard_map/reduce_scatter | solution.py:38
  1251.0 15.4 collective-permute-start.4
  1308.1 44.8 %copy-start.63 = (bf16[3,8,98,384]{2,3,1,0:T(8,128)(2,1)S(1)}, bf16[3,8,98,384]{2,3,1,0:T(8,128)(2,1)}, u32[]{:S(2)}) copy-start(bf16[3,8,98,384]{2,3,1,0:T(8,128)(2,1)} %get-tuple-element.116) | copy-start | bytes 5419012
  1308.1 40.6 %collective-permute-start.5 = (bf16[3,8,98,384]{3,1,2,0:T(8,128)(2,1)}, bf16[3,8,98,384]{3,1,2,0:T(8,128)(2,1)}, u32[]{:S(2)}, u32[]{:S(2)}) collective-permute-start(bf16[3,8,98,384]{3,1,2,0:T(8,128)(2,1)} %copy.214), channel_id=1, source_target_pairs={{0,2},{2,0},{1,3},{3,1},{4,6},{6,4},{5,7},{7,5},{8,10},{10,8},{9,1... | collective-permute-start | bytes 5419016 | tf_op jit(solution)/shard_map/ppermute | solution.py:19
  1372.6 42.7 %copy-start.103 = (f32[784]{0:T(1024)S(1)}, f32[784]{0:T(1024)}, u32[]{:S(2)}) copy-start(f32[784]{0:T(1024)} %copy-done.102) | copy-start | bytes 9412
  1372.6 42.7 %copy-start.114 = (f32[768]{0:T(1024)S(1)}, f32[768]{0:T(1024)}, u32[]{:S(2)}) copy-start(f32[768]{0:T(1024)} %get-tuple-element.69) | copy-start | bytes 9220
  1379.9 38.2 %copy-start.137 = (f32[784]{0:T(1024)S(1)}, f32[784]{0:T(1024)}, u32[]{:S(2)}) copy-start(f32[784]{0:T(1024)} %copy-done.136) | copy-start | bytes 9412
  1379.9 38.2 %copy-start.127 = (f32[784]{0:T(1024)S(1)}, f32[784]{0:T(1024)}, u32[]{:S(2)}) copy-start(f32[784]{0:T(1024)} %copy-done.126) | copy-start | bytes 9412
  1379.9 81.2 %all-gather.45.cloned.1.call-start = ((), (), s32[]{:S(2)}) async-start(), calls=%async_computation.30 | async-start | bytes 3612672 | tf_op jit(solution)/shard_map/all_gather | solution.py:34
  1423.2 38.0 %copy-start.188 = (bf16[1,2,384,768]{2,3,1,0:T(8,128)(2,1)S(1)}, bf16[1,2,384,768]{2,3,1,0:T(8,128)(2,1)}, u32[]{:S(2)}) copy-start(bf16[1,2,384,768]{2,3,1,0:T(8,128)(2,1)} %all-gather.63.cloned.1.call-done) | copy-start | bytes 3538948
  1424.3 146.2 %reduce-scatter.29.cloned.1.call-start = ((), (), s32[]{:S(2)}) async-start(), calls=%async_computation.31 | async-start | bytes 3612672 | tf_op jit(solution)/shard_map/reduce_scatter | solution.py:38
  1530.5 40.0 %copy-start.101 = (f32[784]{0:T(1024)S(1)}, f32[784]{0:T(1024)}, u32[]{:S(2)}) copy-start(f32[784]{0:T(1024)} %copy-done.100) | copy-start | bytes 9412
  1530.5 40.0 %copy-start.112 = (f32[768]{0:T(1024)S(1)}, f32[768]{0:T(1024)}, u32[]{:S(2)}) copy-start(f32[768]{0:T(1024)} %get-tuple-element.65) | copy-start | bytes 9220
  1535.1 38.2 %copy-start.135 = (f32[784]{0:T(1024)S(1)}, f32[784]{0:T(1024)}, u32[]{:S(2)}) copy-start(f32[784]{0:T(1024)} %copy-done.134) | copy-start | bytes 9412
  1535.2 38.2 %copy-start.125 = (f32[784]{0:T(1024)S(1)}, f32[784]{0:T(1024)}, u32[]{:S(2)}) copy-start(f32[784]{0:T(1024)} %copy-done.124) | copy-start | bytes 9412
  1535.2 81.2 %all-gather.47.cloned.1.call-start = ((), (), s32[]{:S(2)}) async-start(), calls=%async_computation.32 | async-start | bytes 3612672 | tf_op jit(solution)/shard_map/all_gather | solution.py:34
  1578.4 38.0 %copy-start.183 = (bf16[1,1536,768]{1,2,0:T(8,128)(2,1)S(1)}, bf16[1,1536,768]{1,2,0:T(8,128)(2,1)}, u32[]{:S(2)}) copy-start(bf16[1,1536,768]{1,2,0:T(8,128)(2,1)} %all-gather.59.cloned.1.call-done) | copy-start | bytes 7077892
  1579.6 91.5 %reduce-scatter.31.cloned.1.call-start = ((), (), s32[]{:S(2)}) async-start(), calls=%async_computation.33 | async-start | bytes 3612672 | tf_op jit(solution)/shard_map/reduce_scatter | solution.py:38
  1630.5 40.6 %copy-start.99 = (f32[784]{0:T(1024)S(1)}, f32[784]{0:T(1024)}, u32[]{:S(2)}) copy-start(f32[784]{0:T(1024)} %copy-done.98) | copy-start | bytes 9412
  1630.5 40.6 %copy-start.110 = (f32[768]{0:T(1024)S(1)}, f32[768]{0:T(1024)}, u32[]{:S(2)}) copy-start(f32[768]{0:T(1024)} %copy-done.109) | copy-start | bytes 9220
  1635.7 38.2 %copy-start.133 = (f32[784]{0:T(1024)S(1)}, f32[784]{0:T(1024)}, u32[]{:S(2)}) copy-start(f32[784]{0:T(1024)} %copy-done.132) | copy-start | bytes 9412
  1635.7 38.2 %copy-start.123 = (f32[784]{0:T(1024)S(1)}, f32[784]{0:T(1024)}, u32[]{:S(2)}) copy-start(f32[784]{0:T(1024)} %copy-done.122) | copy-start | bytes 9412
  1635.7 81.2 %all-gather.49.cloned.1.call-start = ((), (), s32[]{:S(2)}) async-start(), calls=%async_computation.34 | async-start | bytes 3612672 | tf_op jit(solution)/shard_map/all_gather | solution.py:34
  1680.1 317.2 %reduce-scatter.33.cloned.1.call-start = ((), (), s32[]{:S(2)}) async-start(), calls=%async_computation.35 | async-start | bytes 3612672 | tf_op jit(solution)/shard_map/reduce_scatter | solution.py:38
  1721.0 31.6 %collective-permute-start.6 = (bf16[1,8,98,384]{3,1,2,0:T(8,128)(2,1)S(1)}, bf16[1,8,98,384]{3,1,2,0:T(8,128)(2,1)S(1)}, u32[]{:S(2)}, u32[]{:S(2)}) collective-permute-start(bf16[1,8,98,384]{3,1,2,0:T(8,128)(2,1)S(1)} %copy.233), channel_id=1, source_target_pairs={{0,2},{2,0},{1,3},{3,1},{4,6},{6,4},{5,7},{7,5},{8,10},{10,8},{9,1... | collective-permute-start | bytes 1806344 | tf_op jit(solution)/shard_map/ppermute | solution.py:19
  1794.6 41.2 %collective-permute-start.7 = (bf16[3,8,98,384]{3,1,2,0:T(8,128)(2,1)}, bf16[3,8,98,384]{3,1,2,0:T(8,128)(2,1)}, u32[]{:S(2)}, u32[]{:S(2)}) collective-permute-start(bf16[3,8,98,384]{3,1,2,0:T(8,128)(2,1)} %copy.246), channel_id=1, source_target_pairs={{0,2},{2,0},{1,3},{3,1},{4,6},{6,4},{5,7},{7,5},{8,10},{10,8},{9,1... | collective-permute-start | bytes 5419016 | tf_op jit(solution)/shard_map/ppermute | solution.py:19
  1991.6 268.4 %all-to-all-start.1 = ((bf16[16,2,147456]{2,1,0:T(2,128)(2,1)}), bf16[16,2,147456]{2,1,0:T(2,128)(2,1)}, u32[]{:S(2)}, u32[]{:S(2)}) async-start(bf16[16,2,147456]{2,1,0:T(2,128)(2,1)} %reshape.897), calls=%async_computation.13 | async-start | bytes 18874368 | tf_op jit(solution)/shard_map/all_to_all | solution.py:387
  1997.3 45.3 %all-gather.51.cloned.1.call-start = ((), (), s32[]{:S(2)}) async-start(), calls=%async_computation.36 | async-start | bytes 3612672 | tf_op jit(solution)/shard_map/all_gather | solution.py:34
  2260.0 258.3 %all-to-all-start = ((bf16[16,2,147456]{2,1,0:T(2,128)(2,1)}), bf16[16,2,147456]{2,1,0:T(2,128)(2,1)}, u32[]{:S(2)}, u32[]{:S(2)}) async-start(bf16[16,2,147456]{2,1,0:T(2,128)(2,1)} %reshape.899), calls=%async_computation.12 | async-start | bytes 18874368 | tf_op jit(solution)/shard_map/all_to_all | solution.py:387
  2265.9 50.1 %reduce-scatter.35.cloned.1.call-start = ((), (), s32[]{:S(2)}) async-start(), calls=%async_computation.37 | async-start | bytes 3612672 | tf_op jit(solution)/shard_map/reduce_scatter | solution.py:38
  2273.1 239.9 %all-reduce.3.cloned.1.call-start = ((), (), s32[]{:S(2)}) async-start(), calls=%async_computation.46 | async-start | bytes 233472 | tf_op jit(solution)/shard_map/psum | solution.py:420
  (174 other events, 1010.0 us)
Sparse Core Ops, SparseCore 0:
  13.5 39.3 all-gather.28
  55.7 47.5 all-gather.52
  106.1 37.2 all-gather.54
  158.5 34.0 reduce-scatter.12
  197.3 36.6 all-gather.30
  363.1 35.2 reduce-scatter.14
  401.2 42.2 all-gather.56
  445.6 35.4 all-gather.32
  483.4 42.2 all-gather.58
  534.3 34.0 reduce-scatter.16
  571.5 47.5 all-gather.60
  621.1 35.4 all-gather.34
  659.1 38.3 all-gather.62
  703.3 35.2 reduce-scatter.18
  747.1 36.6 all-gather.36
  909.3 35.2 reduce-scatter.20
  947.5 42.2 all-gather.64
  991.9 35.4 all-gather.38
  1029.9 42.2 all-gather.66
  1073.6 35.4 all-gather.40
  1130.2 35.2 reduce-scatter.24
  1167.8 35.2 reduce-scatter.22
  1210.4 36.6 all-gather.42
  1380.0 35.2 reduce-scatter.26
  1424.4 36.6 all-gather.44
  1535.3 35.2 reduce-scatter.28
  1579.7 36.6 all-gather.46
  1635.8 35.2 reduce-scatter.30
  1680.3 36.6 all-gather.48
  1869.3 35.0 reduce-scatter.32
  2005.5 36.9 all-gather.50
  2273.3 35.5 reduce-scatter.34
  2321.2 191.8 all-reduce.2
where the time goes:
time: 2570 us; the launch traced here: 2560 us
  waiting for transfers between devices  1300 us (51%)
  local copies, waits for them, and re-layouts  502 us (20%)
  other arithmetic  367 us (14%)
  matrix products  349 us (14%)
    all_gather x12, waiting for transfers between devices, pair_rows(): return lax.all_gather(rounded_value, 'col', axis=0, tiled=True)  399 us
    reduce_scatter x12, waiting for transfers between devices, pair_sums(): lax.psum_scatter(partial_rows.astype(jnp.bfloat16), 'col', scatter_dimens...  335 us
    unnamed x6, other arithmetic  213 us
    psum x1, waiting for transfers between devices, shards(): lax.psum((gain_terms, shift_terms, qv_padded, outb_terms, up_padded, down...  188 us
    ppermute x8, waiting for transfers between devices, partner(): return lax.ppermute(value, axis, pairs)  168 us
    unnamed x404, local copies, waits for them, and re-layouts  110 us
    all_gather x2, waiting for transfers between devices, fetch_layer(): lax.all_gather(qkv_weight[layer_at], ('dp', 'row'), axis=1, tiled=True)  95.1 us
    all_gather x2, waiting for transfers between devices, fetch_layer(): lax.all_gather(up_weight[layer_at], ('dp', 'row'), axis=0, tiled=True)  78.2 us
  transfers between devices with their start and end apart: 43, of which 36 were waited for; matrix products, arithmetic and copies ran while one was open for 27% of the time, Pallas kernels for 0%

commit v1 on v0

v1 whole, which is shorter than its diff:
```python
import jax
import jax.numpy as jnp
from jax import lax
from jax.sharding import PartitionSpec as P

D = 768
FF = 3072
HEADS = 12
FRAMES = 16
PATCHES = 196
ROWS_AXES = ("col", "dp", "row")
ALL_AXES = ("dp", "row", "col")
CLIP_AXES = ("row", "col")
HEAD = D // HEADS
SCALE = HEAD**-0.5

layer_eps = 1e-06


def layer_norm(values, norm_gain, norm_shift):
    average = jnp.mean(values, axis=-1, keepdims=True)
    centred = values - average
    spread_sq = jnp.mean(centred * centred, axis=-1, keepdims=True)
    return centred * lax.rsqrt(spread_sq + layer_eps) * norm_gain + norm_shift


def exact_gelu(values):
    return jax.nn.gelu(values, approximate=False)


def dot(left, right, dims):
    return jnp.einsum(dims, left, right, preferred_element_type=jnp.float32)


def clip_place():
    return lax.axis_index("row") * lax.axis_size("col") + lax.axis_index("col")


def clip_swap(value, apart):
    count = lax.axis_size("row") * lax.axis_size("col")
    return lax.ppermute(value, CLIP_AXES, [(at, at ^ apart) for at in range(count)])


def to_patches(rows, group):
    own_frames = FRAMES // group
    share = PATCHES // group
    place = clip_place() % group
    grid = rows.reshape(own_frames, PATCHES, rows.shape[-1])
    total = jnp.zeros((FRAMES, share, rows.shape[-1]), rows.dtype)
    for apart in range(group):
        other = place ^ apart
        piece = lax.dynamic_slice_in_dim(grid, other * share, share, 1)
        if apart:
            piece = clip_swap(piece, apart)
        total = lax.dynamic_update_slice_in_dim(total, piece, other * own_frames, 0)
    return jnp.swapaxes(total, 0, 1)


def to_frames(rows, group):
    own_frames = FRAMES // group
    share = PATCHES // group
    place = clip_place() % group
    grid = jnp.swapaxes(rows, 0, 1)
    total = jnp.zeros((own_frames, PATCHES, rows.shape[-1]), rows.dtype)
    for apart in range(group):
        other = place ^ apart
        piece = lax.dynamic_slice_in_dim(grid, other * own_frames, own_frames, 0)
        if apart:
            piece = clip_swap(piece, apart)
        total = lax.dynamic_update_slice_in_dim(total, piece, other * share, 1)
    return total.reshape(own_frames * PATCHES, rows.shape[-1])


def heads_of(flat):
    return flat.reshape(flat.shape[:-1] + (HEADS, HEAD))


def attend(qkv):
    q, k, v = heads_of(qkv[0]), heads_of(qkv[1]), heads_of(qkv[2])
    scores = dot(q, k, "slhe,smhe->shlm") * SCALE
    top = jnp.max(scores, axis=-1, keepdims=True)
    raised = jnp.exp(scores - top)
    weights = raised / jnp.sum(raised, axis=-1, keepdims=True)
    mixed = dot(weights.astype(jnp.bfloat16), v, "shlm,smhe->slhe").astype(jnp.bfloat16)
    return mixed.reshape(qkv.shape[1:]), weights


def attend_back(qkv, weights, grad_mixed):
    q, k, v = heads_of(qkv[0]), heads_of(qkv[1]), heads_of(qkv[2])
    dm = heads_of(grad_mixed)
    dp = dot(dm, v, "slhe,smhe->shlm")
    dv = dot(weights.astype(jnp.bfloat16), dm, "shlm,slhe->smhe")
    ds = (weights * (dp - jnp.sum(dp * weights, axis=-1, keepdims=True))).astype(jnp.bfloat16)
    dq = dot(ds, k, "shlm,smhe->slhe") * SCALE
    dk = dot(ds, q, "shlm,slhe->smhe") * SCALE
    return jnp.stack([dq, dk, dv]).astype(jnp.bfloat16).reshape(qkv.shape)


def project(rows, weight, bias_pair):
    out = dot(rows, weight, "nd,dte->tne")
    offsets = jnp.stack([bias_pair[0], jnp.zeros_like(bias_pair[0]), bias_pair[1]])
    return (out + offsets[:, None, :]).astype(jnp.bfloat16)


def norm_back(values, gain, shift, grad_normed, carry):
    _, pull = jax.vjp(layer_norm, values, gain, shift)
    grad_values, grad_gain, grad_shift = pull(grad_normed)
    return carry + grad_values, grad_gain, grad_shift


def pack_rows(qkv_weight, out_weight, up_weight, down_weight, at):
    rows = up_weight.shape[1]
    return jnp.concatenate(
        [
            jnp.moveaxis(qkv_weight[at], 1, 0).reshape(rows, -1),
            jnp.moveaxis(out_weight[at], 2, 0).reshape(rows, -1),
            up_weight[at],
            down_weight[at].T,
        ],
        axis=1,
    )


def unpack_full(full, cols):
    half, units = D // cols, FF // cols
    qkv = full[:, :, : 6 * half].reshape(cols, D, 2, 3, half)
    qkv = jnp.transpose(qkv, (2, 1, 3, 0, 4)).reshape(2, D, 3, D)
    out = full[:, :, 6 * half : 8 * half].reshape(cols, D, 2, half)
    out = jnp.transpose(out, (2, 0, 3, 1)).reshape(2, D, D)
    up = jnp.transpose(full[:, :, 8 * half : 8 * half + units], (1, 0, 2)).reshape(D, FF)
    down = jnp.transpose(full[:, :, 8 * half + units :], (0, 2, 1)).reshape(FF, D)
    return qkv, out, up, down


def pack_grads(qkv, out, up, down, cols):
    half, units = D // cols, FF // cols
    qkv = jnp.transpose(qkv.reshape(2, D, 3, cols, half), (3, 1, 0, 2, 4)).reshape(cols, D, 6 * half)
    out = jnp.transpose(out.reshape(2, cols, half, D), (1, 3, 0, 2)).reshape(cols, D, 2 * half)
    up = jnp.transpose(up.reshape(D, cols, units), (1, 0, 2))
    down = jnp.transpose(down.reshape(cols, units, D), (0, 2, 1))
    return jnp.concatenate([qkv, out, up, down], axis=2).astype(jnp.bfloat16)


def unpack_own(rows, half, units):
    count = rows.shape[0]
    qkv = jnp.moveaxis(rows[:, : 6 * half].reshape(count, 2, 3, half), 0, 1)
    out = jnp.moveaxis(rows[:, 6 * half : 8 * half].reshape(count, 2, half), 0, 2)
    up = rows[:, 8 * half : 8 * half + units]
    down = rows[:, 8 * half + units :].T
    return qkv, out, up, down


def layer_forward(hidden, weights, small, group):
    qkv_w, out_w, up_w, down_w = weights
    gains, shifts, bias_qv, bias_out, bias_up, bias_down = small
    own_frames = FRAMES // group
    x0 = layer_norm(hidden, gains[0], shifts[0]).astype(jnp.bfloat16)
    qkv0 = project(x0, qkv_w[0], bias_qv[0]).reshape(3, own_frames, PATCHES, D)
    mixed0, p0 = attend(qkv0)
    mixed0 = mixed0.reshape(-1, D)
    hidden1 = hidden + dot(mixed0, out_w[0], "nc,cd->nd") + bias_out[0]
    x1 = layer_norm(hidden1, gains[1], shifts[1]).astype(jnp.bfloat16)
    x1 = to_patches(x1, group)
    share = x1.shape[0]
    x1 = x1.reshape(-1, D)
    qkv1 = project(x1, qkv_w[1], bias_qv[1]).reshape(3, share, FRAMES, D)
    mixed1, p1 = attend(qkv1)
    mixed1 = to_frames(mixed1, group)
    hidden2 = hidden1 + dot(mixed1, out_w[1], "nc,cd->nd") + bias_out[1]
    x2 = layer_norm(hidden2, gains[2], shifts[2]).astype(jnp.bfloat16)
    inner = dot(x2, up_w, "nd,df->nf") + bias_up
    act = exact_gelu(inner).astype(jnp.bfloat16)
    hidden3 = hidden2 + dot(act, down_w, "nf,fd->nd") + bias_down
    return hidden3, (hidden, hidden1, hidden2, x0, qkv0, p0, mixed0, x1, qkv1, p1, mixed1, x2, inner, act)


def bias_sums(d):
    flat = d.reshape(3, -1, D).astype(jnp.float32)
    return jnp.stack([jnp.sum(flat[0], axis=0), jnp.sum(flat[2], axis=0)])


def layer_backward(record, grad, weights, small, group, cols):
    hidden, hidden1, hidden2, x0, qkv0, p0, mixed0, x1, qkv1, p1, mixed1, x2, inner, act = record
    qkv_w, out_w, up_w, down_w = weights
    gains, shifts, *_ = small
    down_bias = jnp.sum(grad, axis=0)
    gb = grad.astype(jnp.bfloat16)
    _, pull = jax.vjp(exact_gelu, inner)
    d_inner = pull(dot(gb, down_w, "nd,fd->nf"))[0].astype(jnp.bfloat16)
    down_g = dot(act, gb, "nf,nd->fd")
    up_bias = jnp.sum(d_inner.astype(jnp.float32), axis=0)
    up_g = dot(x2, d_inner, "nd,nf->df")
    grad, gain2, shift2 = norm_back(hidden2, gains[2], shifts[2], dot(d_inner, up_w, "nf,df->nd"), grad)

    out_bias1 = jnp.sum(grad, axis=0)
    gb = grad.astype(jnp.bfloat16)
    out_g1 = dot(mixed1, gb, "nc,nd->cd")
    dm = to_patches(dot(gb, out_w[1], "nd,cd->nc").astype(jnp.bfloat16), group)
    d1 = attend_back(qkv1, p1, dm).reshape(3, -1, D)
    qv1 = bias_sums(d1)
    qkv_g1 = dot(x1, d1, "nd,tne->dte")
    dx = dot(d1, qkv_w[1], "tne,dte->nd").astype(jnp.bfloat16)
    dx = to_frames(dx.reshape(-1, FRAMES, D), group).astype(jnp.float32)
    grad, gain1, shift1 = norm_back(hidden1, gains[1], shifts[1], dx, grad)

    out_bias0 = jnp.sum(grad, axis=0)
    gb = grad.astype(jnp.bfloat16)
    out_g0 = dot(mixed0, gb, "nc,nd->cd")
    dm = dot(gb, out_w[0], "nd,cd->nc").astype(jnp.bfloat16).reshape(qkv0.shape[1:])
    d0 = attend_back(qkv0, p0, dm).reshape(3, -1, D)
    qv0 = bias_sums(d0)
    qkv_g0 = dot(x0, d0, "nd,tne->dte")
    dx = dot(d0, qkv_w[0], "tne,dte->nd")
    grad, gain0, shift0 = norm_back(hidden, gains[0], shifts[0], dx, grad)
    packed = pack_grads(jnp.stack([qkv_g0, qkv_g1]), jnp.stack([out_g0, out_g1]), up_g, down_g, cols)
    small_g = (
        jnp.stack([gain0, gain1, gain2]),
        jnp.stack([shift0, shift1, shift2]),
        jnp.stack([qv0, qv1]),
        jnp.stack([out_bias0, out_bias1]),
        up_bias,
        down_bias,
    )
    return grad, packed, small_g


def shards(
    hidden_in,
    qkv_weight,
    out_weight,
    up_weight,
    down_weight,
    qv_bias,
    out_bias,
    up_bias,
    down_bias,
    norm_gain,
    norm_shift,
    cotangent,
):
    layers = qkv_weight.shape[0]
    cols = lax.axis_size("col")
    group = FRAMES * PATCHES // hidden_in.shape[0]
    half, units = D // cols, FF // cols
    qv_all = lax.all_gather(qv_bias, "col", axis=3, tiled=True)
    up_all = lax.all_gather(up_bias, "col", axis=1, tiled=True)
    hidden = hidden_in
    kept = []
    for at in range(layers):
        packed = pack_rows(qkv_weight, out_weight, up_weight, down_weight, at)
        full = lax.all_gather(packed, ROWS_AXES, axis=0, tiled=True).reshape(cols, D, -1)
        weights = unpack_full(full, cols)
        small = (norm_gain[at], norm_shift[at], qv_all[at], out_bias[at], up_all[at], down_bias[at])
        hidden, record = layer_forward(hidden, weights, small, group)
        kept.append((weights, small, record))
    grad = cotangent
    owned = [None] * layers
    smalls = [None] * layers
    for at in reversed(range(layers)):
        weights, small, record = kept[at]
        grad, packed, smalls[at] = layer_backward(record, grad, weights, small, group, cols)
        rows = lax.psum_scatter(
            packed.reshape(cols * D, -1), ROWS_AXES, scatter_dimension=0, tiled=True
        ).astype(jnp.float32)
        owned[at] = unpack_own(rows, half, units)
    grads = [jnp.stack([owned[at][i] for at in range(layers)]) for i in range(4)]
    terms = [jnp.stack([smalls[at][i] for at in range(layers)]) for i in range(6)]
    gain, shift, qv, outb, upb, downb = lax.psum(tuple(terms), ALL_AXES)
    col_at = lax.axis_index("col")
    qv = lax.dynamic_slice_in_dim(qv, col_at * half, half, 3)
    upb = lax.dynamic_slice_in_dim(upb, col_at * units, units, 1)
    return (hidden, grad, *grads, qv, outb, upb, downb, gain, shift)


def solution(mesh):
    return jax.shard_map(
        shards,
        mesh=mesh,
        in_specs=(
            P(("dp", "row", "col"), None),
            P(None, None, ("dp", "row"), None, "col"),
            P(None, None, "col", ("dp", "row")),
            P(None, ("dp", "row"), "col"),
            P(None, "col", ("dp", "row")),
            P(None, None, None, "col"),
            P(),
            P(None, "col"),
            P(),
            P(),
            P(),
            P(("dp", "row", "col"), None),
        ),
        out_specs=(
            P(("dp", "row", "col"), None),
            P(("dp", "row", "col"), None),
            P(None, None, ("dp", "row"), None, "col"),
            P(None, None, "col", ("dp", "row")),
            P(None, ("dp", "row"), "col"),
            P(None, "col", ("dp", "row")),
            P(None, None, None, "col"),
            P(),
            P(None, "col"),
            P(),
            P(),
            P(),
        ),
        check_vma=False,
    )
```

time: 2570 us -> 1770 us (0.69)
  waiting for transfers between devices: 1300 us -> 418 us
  local copies, waits for them, and re-layouts: 502 us -> 756 us
  other arithmetic: 367 us -> 162 us
    all_gather x20 -> x2, waiting for transfers between devices: 607 us -> 118 us  [shards(): lax.all_gather(packed, ROWS_AXES, axis=0, tiled=True).reshape(cols, D, -1)]
    reduce_scatter x12 -> x0, waiting for transfers between devices: 335 us -> none  [pair_sums(): lax.psum_scatter(partial_rows.astype(jnp.bfloat16), 'col', scatter_dimens...]
    unnamed x33 -> x7, waiting for transfers between devices: 3.6 us -> 287 us
    unnamed x6 -> x11, other arithmetic: 213 us -> 0.01 us
    psum x1, waiting for transfers between devices: 188 us -> 0.01 us  [shards(): gain, shift, qv, outb, upb, downb = lax.psum(tuple(terms), ALL_AXES)]
    ppermute x8 -> x24, waiting for transfers between devices: 168 us -> 13.1 us  [clip_swap(): lax.ppermute(value, CLIP_AXES, [(at, at ^ apart) for at in range(count)])]
    another operation x43 -> x79, local copies, waits for them, and re-layouts: 78.3 us -> 176 us  [the longest x22 86 us: heads_of(): return flat.reshape(flat.shape[:-1] + (HEADS, HEAD))]
    slice x24 -> x27, local copies, waits for them, and re-layouts: 28.1 us -> 112 us  [the longest x4 37 us: layer_forward(): qkv1 = project(x1, qkv_w[1], bias_qv[1]).reshape(3, share, FRAMES, D)]
  transfers between devices with their start and end apart: 43 -> 29, of which waited for: 36 -> 7; matrix products, arithmetic and copies ran while one was open for 27% -> 39% of each run, Pallas kernels for 0% -> 0%
where the time goes in v1:
time: 1770 us; the launch traced here: 1750 us
  local copies, waits for them, and re-layouts  756 us (43%)
  waiting for transfers between devices  418 us (24%)
  matrix products  358 us (20%)
  other arithmetic  162 us (9%)
  starting transfers between devices  29.5 us (2%)
    dot_general x58, matrix products, dot(): return jnp.einsum(dims, left, right, preferred_element_type=jnp.float32)  339 us
    unnamed x7, waiting for transfers between devices  287 us
    unnamed x456, local copies, waits for them, and re-layouts  176 us
    all_gather x2, waiting for transfers between devices, shards(): lax.all_gather(packed, ROWS_AXES, axis=0, tiled=True).reshape(cols, D, -1)  118 us
    another operation x22, local copies, waits for them, and re-layouts, heads_of(): return flat.reshape(flat.shape[:-1] + (HEADS, HEAD))  86 us
    concatenate x2, other arithmetic, pack_grads(): return jnp.concatenate([qkv, out, up, down], axis=2).astype(jnp.bfloat16)  74.4 us
    another operation x22, local copies, waits for them, and re-layouts, attend_back(): return jnp.stack([dq, dk, dv]).astype(jnp.bfloat16).reshape(qkv.shape)  60.1 us
    dynamic_update_slice x16, local copies, waits for them, and re-layouts, to_frames(): total = lax.dynamic_update_slice_in_dim(total, piece, other * share, 1)  53.4 us
  transfers between devices with their start and end apart: 29, of which 7 were waited for; matrix products, arithmetic and copies ran while one was open for 39% of the time, Pallas kernels for 0%

profile of v1, /device:TPU:0, one launch (start us, length us, event | category | flops | bytes accessed | tf_op | source)
XLA Modules:
  0.0 1748.9 jit_solution(14315268087133908395)
XLA Ops:
  25.9 113.0 %all-gather.3.cloned.1.call-done = bf16[1536,6144]{1,0:T(8,128)(2,1)} async-done(((bf16[48,6144]{1,0:T(8,128)(2,1)}), bf16[1536,6144]{1,0:T(8,128)(2,1)}) %all-gather.3.cloned.1.call-update) | async-done | bytes 18874384 | tf_op jit(solution)/shard_map/all_gather | solution.py:251
  138.9 6.3 slice.458
  148.4 10.4 copy.609
  158.8 6.4 fusion.184
  165.2 12.1 copy.403
  177.3 8.9 squeeze.36
  186.2 5.6 fusion.33
  215.1 9.4 fusion.192
  252.7 8.1 fusion.182
  265.3 6.3 slice.477
  271.6 10.7 copy.613
  282.3 6.5 fusion.183
  296.3 12.0 copy.413
  308.3 8.9 squeeze.38
  317.2 6.6 copy.611
  323.8 6.6 copy.612
  330.5 12.0 copy.432
  342.5 8.9 squeeze.88
  433.5 30.2 %multiply_convert_fusion.3 = (bf16[784,3072]{1,0:T(8,128)(2,1)S(1)}, f32[784,3072]{1,0:T(8,128)}, f32[784,3072]{1,0:T(8,128)}) fusion(f32[3072]{0:T(1024)S(1)} %bitcast.583, bf16[768,3072]{0,1:T(8,128)(2,1)S(1)} %bitcast.528, f32[784,768]{1,0:T(8,128)S(1)} %get-tuple-element.212, f32[768]{0:T(1024)S(1)} %get-tuple-element.80, ...), kind=kOutput, calls=%fused_computation.41 | convolution fusion | flops 3861344256 | bytes 31236224 | tf_op jit(solution)/shard_map/nd,df->nf/dot_general | solution.py:32
  495.7 9.3 fusion.197
  526.0 12.0 copy.442
  538.0 9.0 squeeze.90
  551.6 6.5 collective-permute-done.7
  558.4 5.6 collective-permute-done.8
  610.9 8.0 fusion.181
  618.9 6.6 copy.615
  625.5 6.7 copy.616
  655.7 30.1 %multiply_convert_fusion.2 = (bf16[784,3072]{1,0:T(8,128)(2,1)}, f32[784,3072]{1,0:T(8,128)}, f32[784,3072]{1,0:T(8,128)}) fusion(f32[3072]{0:T(1024)S(1)} %bitcast.585, bf16[768,3072]{0,1:T(8,128)(2,1)S(1)} %bitcast.540, f32[784,768]{1,0:T(8,128)S(1)} %get-tuple-element.223, f32[768]{0:T(1024)S(1)} %copy-done.183, f32[768]{0:T(1024)S(1)} %copy-done.145, ...), kind=kOutput, calls=%fused_computation.28 | convolution fusion | flops 3861344256 | bytes 31236224 | tf_op jit(solution)/shard_map/nd,df->nf/dot_general | solution.py:32
  685.8 13.4 convert_reduce_fusion
  699.2 6.9 multiply_reduce_fusion.8
  706.1 7.7 convolution_convert_fusion.1
  726.1 9.6 convolution_convert_fusion
  740.8 11.6 reshape.617
  752.4 16.1 copy.540
  768.5 5.6 copy.638
  866.2 7.3 fusion.99
  873.5 7.2 multiply_reduce_fusion.1
  880.7 11.2 multiply_convert_fusion.1
  935.1 6.0 convolution_convert_fusion.4
  943.5 14.5 convert_reduce_fusion.1
  958.1 6.6 multiply_reduce_fusion.10
  986.2 5.6 maximum_bitcast_fusion.1
  991.8 18.3 %copy.535 = bf16[2,768,2,3,384]{1,0,4,3,2:T(2,128)(2,1)} copy(bf16[2,768,2,3,384]{4,1,0,3,2:T(8,128)(2,1)} %maximum_bitcast_fusion.1) | data formatting | bytes 14155776 | tf_op jit(solution)/shard_map/transpose | solution.py:137
  1010.2 7.3 copy.636
  1110.8 7.3 fusion.105
  1118.1 7.3 multiply_reduce_fusion
  1125.5 11.1 multiply_convert_fusion
  1170.4 8.0 fusion.63
  1182.3 17.0 pad_maximum_fusion.1
  1199.3 24.7 %copy.583 = bf16[1536,6144]{1,0:T(8,128)(2,1)} copy(bf16[1536,6144]{0,1:T(8,128)(2,1)} %pad_maximum_fusion.1) | data formatting | bytes 37748736
  1224.7 10.0 convolution_convert_fusion.3
  1234.7 11.6 reshape.612
  1246.4 16.1 copy.529
  1262.4 5.5 copy.635
  1268.0 8.1 convolution_convert_fusion.2
  1287.7 6.3 convolution_convert_fusion.5
  1294.0 6.0 copy.523
  1300.0 6.8 maximum_bitcast_fusion
  1306.8 18.3 %copy.524 = bf16[2,768,2,3,384]{1,0,4,3,2:T(2,128)(2,1)} copy(bf16[2,768,2,3,384]{4,1,0,3,2:T(8,128)(2,1)} %maximum_bitcast_fusion) | data formatting | bytes 14155776 | tf_op jit(solution)/shard_map/transpose | solution.py:137
  1336.0 57.4 %pad_maximum_fusion = bf16[1536,6144]{0,1:T(8,128)(2,1)} fusion(bf16[1536,1536]{0,1:T(8,128)(2,1)S(1)} %bitcast.501, bf16[1536,1536]{0,1:T(8,128)(2,1)S(1)} %bitcast.498, bf16[1536,768]{0,1:T(8,128)(2,1)S(1)} %bitcast.513, bf16[1536,2304]{0,1:T(8,128)(2,1)S(1)} %bitcast.485), kind=kLoop, calls=%fused_computation.4 | loop fusion | flops 75497472 | bytes 37748736 | tf_op jit(solution)/shard_map/concatenate | solution.py:141
  1393.4 24.9 %copy.581 = bf16[1536,6144]{1,0:T(8,128)(2,1)} copy(bf16[1536,6144]{0,1:T(8,128)(2,1)} %pad_maximum_fusion) | data formatting | bytes 37748736
  1419.0 10.3 add_add_fusion.12
  1438.0 80.0 %reduce-scatter.9.cloned.1.call-done = bf16[48,6144]{1,0:T(8,128)(2,1)} async-done(((bf16[1536,6144]{1,0:T(8,128)(2,1)}), bf16[48,6144]{1,0:T(8,128)(2,1)}) %reduce-scatter.9.cloned.1.call-update) | async-done | bytes 589840
  1523.0 206.9 %reduce-scatter.7.cloned.1.call-done = bf16[48,6144]{1,0:T(8,128)(2,1)} async-done(((bf16[1536,6144]{1,0:T(8,128)(2,1)}), bf16[48,6144]{1,0:T(8,128)(2,1)}) %reduce-scatter.7.cloned.1.call-update) | async-done | bytes 589840
  (839 shorter events, 650.2 us)
Async XLA Ops:
  7.2 131.7 %all-gather.3.cloned.1.call-start = ((), (), s32[]{:S(2)}) async-start(), calls=%async_computation.2 | async-start | bytes 19464192 | tf_op jit(solution)/shard_map/all_gather | solution.py:251
  10.7 254.6 %all-gather.5.cloned.1.call-start = ((), (), s32[]{:S(2)}) async-start(), calls=%async_computation.3 | async-start | bytes 19464192 | tf_op jit(solution)/shard_map/all_gather | solution.py:251
  10.9 11.8 copy-start.147
  11.1 12.3 copy-start.129
  11.1 12.2 copy-start.130
  12.0 1420.6 %all-reduce.3.cloned.1.call-start = ((), (), s32[]{:S(2)}) async-start(), calls=%async_computation.6 | async-start | bytes 233472 | tf_op jit(solution)/shard_map/psum | solution.py:268
  24.0 162.2 %copy-start.138 = (f32[768]{0:T(1024)}, f32[768]{0:T(1024)S(1)}, u32[]{:S(2)}) copy-start(f32[768]{0:T(1024)S(1)} %get-tuple-element.242) | copy-start | bytes 9220
  24.0 162.2 %copy-start.177 = (f32[768]{0:T(1024)}, f32[768]{0:T(1024)S(1)}, u32[]{:S(2)}) copy-start(f32[768]{0:T(1024)S(1)} %get-tuple-element.82) | copy-start | bytes 9220
  24.0 219.9 %copy-start.108 = (f32[768]{0:T(1024)}, f32[768]{0:T(1024)S(1)}, u32[]{:S(2)}) copy-start(f32[768]{0:T(1024)S(1)} %get-tuple-element.243) | copy-start | bytes 9220
  24.1 409.4 %copy-start.140 = (f32[768]{0:T(1024)}, f32[768]{0:T(1024)S(1)}, u32[]{:S(2)}) copy-start(f32[768]{0:T(1024)S(1)} %get-tuple-element.244) | copy-start | bytes 9220
  24.1 409.4 %copy-start.179 = (f32[768]{0:T(1024)}, f32[768]{0:T(1024)S(1)}, u32[]{:S(2)}) copy-start(f32[768]{0:T(1024)S(1)} %get-tuple-element.80) | copy-start | bytes 9220
  24.1 162.2 %copy-start.112 = (f32[784]{0:T(1024)}, f32[784]{0:T(1024)S(1)}, u32[]{:S(2)}) copy-start(f32[784]{0:T(1024)S(1)} %broadcast_multiply_fusion.5) | copy-start | bytes 9412
  24.5 120.7 %copy-start.119 = (f32[784]{0:T(1024)}, f32[784]{0:T(1024)S(1)}, u32[]{:S(2)}) copy-start(f32[784]{0:T(1024)S(1)} %multiply_reduce_fusion.23) | copy-start | bytes 9412
  24.5 161.7 %copy-start.131 = (f32[784]{0:T(1024)}, f32[784]{0:T(1024)S(1)}, u32[]{:S(2)}) copy-start(f32[784]{0:T(1024)S(1)} %fusion.152) | copy-start | bytes 9412
  25.9 407.6 %copy-start.158 = (f32[1,3072]{1,0:T(1,128)}, f32[1,3072]{1,0:T(1,128)S(1)}, u32[]{:S(2)}) copy-start(f32[1,3072]{1,0:T(1,128)S(1)} %get-tuple-element.192) | copy-start | bytes 36868
  243.5 185.9 %copy-start.2 = (f32[784,768]{1,0:T(8,128)}, f32[784,768]{1,0:T(8,128)S(1)}, u32[]{:S(2)}) copy-start(f32[784,768]{1,0:T(8,128)S(1)} %get-tuple-element.208) | copy-start | bytes 7225348
  251.2 104.5 %collective-permute-start = (bf16[4,49,768]{2,1,0:T(8,128)(2,1)}, bf16[4,49,768]{2,1,0:T(8,128)(2,1)}, u32[]{:S(2)}, u32[]{:S(2)}) collective-permute-start(bf16[4,49,768]{2,1,0:T(8,128)(2,1)} %get-tuple-element.165), channel_id=1, source_target_pairs={{0,1},{1,0},{2,3},{3,2},{4,5},{5,4},{6,7},{7,6},{8,9},{9,8},{10,11... | collective-permute-start | bytes 903176 | tf_op jit(solution)/shard_map/ppermute | solution.py:41
  292.0 65.5 %collective-permute-start.1 = (bf16[4,49,768]{2,1,0:T(8,128)(2,1)S(1)}, bf16[4,49,768]{2,1,0:T(8,128)(2,1)}, u32[]{:S(2)}, u32[]{:S(2)}) collective-permute-start(bf16[4,49,768]{2,1,0:T(8,128)(2,1)S(1)} %get-tuple-element.164), channel_id=1, source_target_pairs={{0,2},{1,3},{2,0},{3,1},{4,6},{5,7},{6,4},{7,5},{8,10},{9,11},{10,... | collective-permute-start | bytes 903176 | tf_op jit(solution)/shard_map/ppermute | solution.py:41
  293.4 66.0 %collective-permute-start.2 = (bf16[4,49,768]{2,1,0:T(8,128)(2,1)S(1)}, bf16[4,49,768]{2,1,0:T(8,128)(2,1)}, u32[]{:S(2)}, u32[]{:S(2)}) collective-permute-start(bf16[4,49,768]{2,1,0:T(8,128)(2,1)S(1)} %get-tuple-element.163), channel_id=1, source_target_pairs={{0,3},{1,2},{2,1},{3,0},{4,7},{5,6},{6,5},{7,4},{8,11},{9,10},{10,... | collective-permute-start | bytes 903176 | tf_op jit(solution)/shard_map/ppermute | solution.py:41
  406.5 9.7 collective-permute-start.3
  407.1 13.6 collective-permute-start.4
  408.5 15.7 collective-permute-start.5
  429.3 34.4 %slice-start.14 = ((s8[4718592]{0:T(1024)(128)(4,1)}), s8[4194304]{0:T(1024)(128)(4,1)S(1)}, s32[]{:S(2)}) async-start(s8[4718592]{0:T(1024)(128)(4,1)} %bitcast.532), calls=%async_computation.21 | async-start | bytes 8388608
  432.3 31.3 %copy-start.15 = (f32[784,768]{1,0:T(8,128)}, f32[784,768]{1,0:T(8,128)S(1)}, u32[]{:S(2)}) copy-start(f32[784,768]{1,0:T(8,128)S(1)} %get-tuple-element.212) | copy-start | bytes 7225348
  432.4 31.3 %copy-start.114 = (f32[784]{0:T(1024)}, f32[784]{0:T(1024)S(1)}, u32[]{:S(2)}) copy-start(f32[784]{0:T(1024)S(1)} %broadcast_multiply_fusion.3) | copy-start | bytes 9412
  433.4 30.3 %copy-start.133 = (f32[784]{0:T(1024)}, f32[784]{0:T(1024)S(1)}, u32[]{:S(2)}) copy-start(f32[784]{0:T(1024)S(1)} %fusion.154) | copy-start | bytes 9412
  433.5 30.2 %slice-start.15 = ((s8[4718592]{0:T(1024)(128)(4,1)}), s8[524288]{0:T(1024)(128)(4,1)S(1)}, s32[]{:S(2)}) async-start(s8[4718592]{0:T(1024)(128)(4,1)} %bitcast.532), calls=%async_computation.22 | async-start | bytes 1048576
  433.5 30.2 %copy-start.176 = (f32[768]{0:T(1024)S(1)}, f32[768]{0:T(1024)}, u32[]{:S(2)}) copy-start(f32[768]{0:T(1024)} %get-tuple-element.89) | copy-start | bytes 9220
  517.1 133.8 %copy-start.4 = (f32[784,768]{1,0:T(8,128)}, f32[784,768]{1,0:T(8,128)S(1)}, u32[]{:S(2)}) copy-start(f32[784,768]{1,0:T(8,128)S(1)} %get-tuple-element.219) | copy-start | bytes 7225348
  525.4 25.0 %collective-permute-start.6 = (bf16[4,49,768]{2,1,0:T(8,128)(2,1)}, bf16[4,49,768]{2,1,0:T(8,128)(2,1)}, u32[]{:S(2)}, u32[]{:S(2)}) collective-permute-start(bf16[4,49,768]{2,1,0:T(8,128)(2,1)} %get-tuple-element.161), channel_id=1, source_target_pairs={{0,1},{1,0},{2,3},{3,2},{4,5},{5,4},{6,7},{7,6},{8,9},{9,8},{10,11... | collective-permute-start | bytes 903176 | tf_op jit(solution)/shard_map/ppermute | solution.py:41
  547.1 17.1 copy-start.53
  547.1 17.1 copy-start.148
  547.1 11.1 collective-permute-start.7
  549.0 15.0 collective-permute-start.8
  607.4 29.3 %collective-permute-start.9 = (bf16[4,49,768]{2,0,1:T(4,128)(2,1)}, bf16[4,49,768]{2,0,1:T(4,128)(2,1)}, u32[]{:S(2)}, u32[]{:S(2)}) collective-permute-start(bf16[4,49,768]{2,0,1:T(4,128)(2,1)} %get-tuple-element.177), channel_id=1, source_target_pairs={{0,1},{1,0},{2,3},{3,2},{4,5},{5,4},{6,7},{7,6},{8,9},{9,8},{10,11... | collective-permute-start | bytes 903176 | tf_op jit(solution)/shard_map/ppermute | solution.py:41
  608.0 33.3 %collective-permute-start.10 = (bf16[4,49,768]{2,0,1:T(4,128)(2,1)}, bf16[4,49,768]{2,0,1:T(4,128)(2,1)}, u32[]{:S(2)}, u32[]{:S(2)}) collective-permute-start(bf16[4,49,768]{2,0,1:T(4,128)(2,1)} %get-tuple-element.176), channel_id=1, source_target_pairs={{0,2},{1,3},{2,0},{3,1},{4,6},{5,7},{6,4},{7,5},{8,10},{9,11},{10,... | collective-permute-start | bytes 903176 | tf_op jit(solution)/shard_map/ppermute | solution.py:41
  609.4 36.3 %collective-permute-start.11 = (bf16[4,49,768]{2,0,1:T(4,128)(2,1)}, bf16[4,49,768]{2,0,1:T(4,128)(2,1)S(1)}, u32[]{:S(2)}, u32[]{:S(2)}) collective-permute-start(bf16[4,49,768]{2,0,1:T(4,128)(2,1)} %get-tuple-element.175), channel_id=1, source_target_pairs={{0,3},{1,2},{2,1},{3,0},{4,7},{5,6},{6,5},{7,4},{8,11},{9,10},{10,... | collective-permute-start | bytes 903176 | tf_op jit(solution)/shard_map/ppermute | solution.py:41
  650.9 34.9 %slice-start.8 = ((s8[4718592]{0:T(1024)(128)(4,1)}), s8[4194304]{0:T(1024)(128)(4,1)S(1)}, s32[]{:S(2)}) async-start(s8[4718592]{0:T(1024)(128)(4,1)} %bitcast.523), calls=%async_computation.15 | async-start | bytes 8388608
  653.9 59.8 %copy-start.17 = (f32[784,768]{1,0:T(8,128)}, f32[784,768]{1,0:T(8,128)S(1)}, u32[]{:S(2)}) copy-start(f32[784,768]{1,0:T(8,128)S(1)} %get-tuple-element.223) | copy-start | bytes 7225348
  655.6 30.1 %slice-start.9 = ((s8[4718592]{0:T(1024)(128)(4,1)}), s8[524288]{0:T(1024)(128)(4,1)S(1)}, s32[]{:S(2)}) async-start(s8[4718592]{0:T(1024)(128)(4,1)} %bitcast.523), calls=%async_computation.16 | async-start | bytes 1048576
  655.7 30.1 %copy-start.60 = (f32[784,768]{1,0:T(8,128)S(1)}, f32[784,768]{1,0:T(8,128)}, u32[]{:S(2)}) copy-start(f32[784,768]{1,0:T(8,128)} %param.23) | copy-start | bytes 7225348
  715.1 20.5 %copy-start.28 = (f32[784,768]{1,0:T(8,128)}, f32[784,768]{1,0:T(8,128)S(1)}, u32[]{:S(2)}) copy-start(f32[784,768]{1,0:T(8,128)S(1)} %get-tuple-element.105) | copy-start | bytes 7225348
  722.5 54.1 %collective-permute-start.12 = (bf16[4,49,768]{2,1,0:T(8,128)(2,1)S(1)}, bf16[4,49,768]{2,1,0:T(8,128)(2,1)}, u32[]{:S(2)}, u32[]{:S(2)}) collective-permute-start(bf16[4,49,768]{2,1,0:T(8,128)(2,1)S(1)} %get-tuple-element.157), channel_id=1, source_target_pairs={{0,1},{1,0},{2,3},{3,2},{4,5},{5,4},{6,7},{7,6},{8,9},{9,8},{10,11... | collective-permute-start | bytes 903176 | tf_op jit(solution)/shard_map/ppermute | solution.py:41
  723.1 54.7 %collective-permute-start.13 = (bf16[4,49,768]{2,1,0:T(8,128)(2,1)S(1)}, bf16[4,49,768]{2,1,0:T(8,128)(2,1)}, u32[]{:S(2)}, u32[]{:S(2)}) collective-permute-start(bf16[4,49,768]{2,1,0:T(8,128)(2,1)S(1)} %get-tuple-element.156), channel_id=1, source_target_pairs={{0,2},{1,3},{2,0},{3,1},{4,6},{5,7},{6,4},{7,5},{8,10},{9,11},{10,... | collective-permute-start | bytes 903176 | tf_op jit(solution)/shard_map/ppermute | solution.py:41
  724.5 54.5 %collective-permute-start.14 = (bf16[4,49,768]{2,1,0:T(8,128)(2,1)S(1)}, bf16[4,49,768]{2,1,0:T(8,128)(2,1)}, u32[]{:S(2)}, u32[]{:S(2)}) collective-permute-start(bf16[4,49,768]{2,1,0:T(8,128)(2,1)S(1)} %get-tuple-element.155), channel_id=1, source_target_pairs={{0,3},{1,2},{2,1},{3,0},{4,7},{5,6},{6,5},{7,4},{8,11},{9,10},{10,... | collective-permute-start | bytes 903176 | tf_op jit(solution)/shard_map/ppermute | solution.py:41
  823.9 14.0 collective-permute-start.15
  824.6 16.8 collective-permute-start.16
  826.1 18.9 %collective-permute-start.17 = (bf16[4,49,768]{2,1,0:T(8,128)(2,1)S(1)}, bf16[4,49,768]{2,1,0:T(8,128)(2,1)}, u32[]{:S(2)}, u32[]{:S(2)}) collective-permute-start(bf16[4,49,768]{2,1,0:T(8,128)(2,1)S(1)} %bitcast.578), channel_id=1, source_target_pairs={{0,3},{1,2},{2,1},{3,0},{4,7},{5,6},{6,5},{7,4},{8,11},{9,10},{10,... | collective-permute-start | bytes 903176 | tf_op jit(solution)/shard_map/ppermute | solution.py:41
  931.3 11.9 slice-start.16
  942.8 15.3 slice-start.12
  943.1 22.5 %copy-start.23 = (f32[784,768]{1,0:T(8,128)}, f32[784,768]{1,0:T(8,128)S(1)}, u32[]{:S(2)}) copy-start(f32[784,768]{1,0:T(8,128)S(1)} %get-tuple-element.97) | copy-start | bytes 7225348
  943.5 14.6 copy-start.16
  943.5 14.6 slice-start.13
  943.5 14.6 copy-start.115
  943.5 14.6 copy-start.134
  943.5 14.6 copy-start.141
  970.2 55.1 %collective-permute-start.18 = (bf16[4,49,768]{2,1,0:T(8,128)(2,1)}, bf16[4,49,768]{2,1,0:T(8,128)(2,1)}, u32[]{:S(2)}, u32[]{:S(2)}) collective-permute-start(bf16[4,49,768]{2,1,0:T(8,128)(2,1)} %get-tuple-element.153), channel_id=1, source_target_pairs={{0,1},{1,0},{2,3},{3,2},{4,5},{5,4},{6,7},{7,6},{8,9},{9,8},{10,11... | collective-permute-start | bytes 903176 | tf_op jit(solution)/shard_map/ppermute | solution.py:41
  970.7 55.8 %collective-permute-start.19 = (bf16[4,49,768]{2,1,0:T(8,128)(2,1)}, bf16[4,49,768]{2,1,0:T(8,128)(2,1)}, u32[]{:S(2)}, u32[]{:S(2)}) collective-permute-start(bf16[4,49,768]{2,1,0:T(8,128)(2,1)} %get-tuple-element.152), channel_id=1, source_target_pairs={{0,2},{1,3},{2,0},{3,1},{4,6},{5,7},{6,4},{7,5},{8,10},{9,11},{10,... | collective-permute-start | bytes 903176 | tf_op jit(solution)/shard_map/ppermute | solution.py:41
  972.1 55.6 %collective-permute-start.20 = (bf16[4,49,768]{2,1,0:T(8,128)(2,1)}, bf16[4,49,768]{2,1,0:T(8,128)(2,1)}, u32[]{:S(2)}, u32[]{:S(2)}) collective-permute-start(bf16[4,49,768]{2,1,0:T(8,128)(2,1)} %get-tuple-element.151), channel_id=1, source_target_pairs={{0,3},{1,2},{2,1},{3,0},{4,7},{5,6},{6,5},{7,4},{8,11},{9,10},{10,... | collective-permute-start | bytes 903176 | tf_op jit(solution)/shard_map/ppermute | solution.py:41
  1072.6 10.2 collective-permute-start.21
  1074.0 12.3 collective-permute-start.22
  1075.5 14.5 collective-permute-start.23
  1182.3 335.7 %reduce-scatter.9.cloned.1.call-start = ((), (), s32[]{:S(2)}) async-start(), calls=%async_computation.5 | async-start | bytes 19464192
  1224.0 505.9 %reduce-scatter.7.cloned.1.call-start = ((), (), s32[]{:S(2)}) async-start(), calls=%async_computation.4 | async-start | bytes 19464192
  (173 other events, 675.7 us)
Sparse Core Ops, SparseCore 0:
  11.5 127.3 all-gather.2
  142.4 122.8 all-gather.4
  1182.4 122.6 all-reduce.2
  1311.3 206.6 reduce-scatter.8
  1524.2 205.6 reduce-scatter.6

commit v2 on v1

v2 whole, which is shorter than its diff:
```python
import functools

import jax
import jax.numpy as jnp
from jax import lax
from jax.experimental import pallas as pl
from jax.experimental.pallas import tpu as pltpu
from jax.sharding import PartitionSpec as P

D = 768
FF = 3072
HEADS = 12
FRAMES = 16
PATCHES = 196
ROWS_AXES = ("col", "dp", "row")
ALL_AXES = ("dp", "row", "col")
CLIP_AXES = ("row", "col")
HEAD = D // HEADS
PAIR = 2 * HEAD
SCALE = HEAD**-0.5
LAYER_EPS = 1e-06
NEG = -1e30

TILE = 8
FRAME_PAD = -(-PATCHES // 16) * 16
KEY_PAD = -(-PATCHES // 128) * 128
CHUNK = 512

BF = jnp.bfloat16
F32 = jnp.float32
ANY = pl.BlockSpec(memory_space=pl.ANY)
SMEM = pl.BlockSpec(memory_space=pltpu.SMEM)


def dot_nn(left, right):
    return lax.dot_general(left, right, (((1,), (0,)), ((), ())), preferred_element_type=F32)


def dot_nt(left, right):
    return lax.dot_general(left, right, (((1,), (1,)), ((), ())), preferred_element_type=F32)


def dot_tn(left, right):
    return lax.dot_general(left, right, (((0,), (0,)), ((), ())), preferred_element_type=F32)


def whole(shape):
    return pl.BlockSpec(shape, lambda *_: (0,) * len(shape))


def shaped(shape, dtype):
    return jax.ShapeDtypeStruct(shape, dtype)


def normalise(values):
    average = jnp.mean(values, axis=-1, keepdims=True)
    centred = values - average
    spread = jnp.mean(centred * centred, axis=-1, keepdims=True)
    inverse = lax.rsqrt(spread + LAYER_EPS)
    return centred * inverse, inverse


def norm_rows(values, gain, shift):
    normed, _ = normalise(values)
    return normed * gain + shift


def norm_rows_back(values, gain, dx, carry):
    normed, inverse = normalise(values)
    e = dx * gain
    first = jnp.mean(e, axis=-1, keepdims=True)
    second = jnp.mean(e * normed, axis=-1, keepdims=True)
    grad = carry + (e - first - normed * second) * inverse
    return (
        grad,
        jnp.sum(dx * normed, axis=0, keepdims=True),
        jnp.sum(dx, axis=0, keepdims=True),
    )


def gelu_parts(u):
    size = jnp.abs(u) * (0.5**0.5)
    t = pl.reciprocal(1.0 + 0.3275911 * size, approx=False)
    poly = 1.421413741 + t * (-1.453152027 + t * 1.061405429)
    poly = t * (0.254829592 + t * (-0.284496736 + t * poly))
    bell = jnp.exp(-size * size)
    tail = 0.5 * poly * bell
    cdf = jnp.where(u >= 0, 1.0 - tail, tail)
    return u * cdf, cdf + u * bell * 0.3989422804014327


def halves(value):
    lane = lax.broadcasted_iota(jnp.int32, value.shape, 1)
    zero = jnp.zeros_like(value)
    return jnp.where(lane < HEAD, value, zero), jnp.where(lane < HEAD, zero, value)


def soft(scores, valid):
    scores = jnp.where(valid, scores, NEG)
    top = jnp.max(scores, axis=-1, keepdims=True)
    raised = jnp.exp((scores - top) * SCALE)
    return raised * (1.0 / jnp.sum(raised, axis=-1, keepdims=True))


def attend_pair(q, k, v, valid):
    total = 0.0
    for kh, vh in zip(halves(k), halves(v)):
        weights = soft(dot_nt(q, kh), valid)
        total = total + dot_nn(weights.astype(BF), vh)
    return total.astype(BF)


def attend_pair_back(q, k, v, dm, valid):
    dq = dk = dv = 0.0
    for qh, kh, vh, dmh in zip(halves(q), halves(k), halves(v), halves(dm)):
        weights = soft(dot_nt(q, kh), valid)
        dp = dot_nt(dm, vh)
        ds = (weights * (dp - jnp.sum(dp * weights, axis=-1, keepdims=True))).astype(BF)
        dv = dv + dot_tn(weights.astype(BF), dmh)
        dq = dq + dot_nn(ds, kh)
        dk = dk + dot_tn(ds, qh)
    return (dq * SCALE).astype(BF), (dk * SCALE).astype(BF), dv.astype(BF)


def frame_valid():
    return lax.broadcasted_iota(jnp.int32, (FRAME_PAD, KEY_PAD), 1) < PATCHES


def patch_valid(rows):
    key = lax.broadcasted_iota(jnp.int32, (rows, rows), 1)
    query = lax.broadcasted_iota(jnp.int32, (rows, rows), 0)
    return (key % TILE) == (query % TILE)


def key_rows(value):
    return jnp.concatenate([value, jnp.zeros((KEY_PAD - FRAME_PAD, value.shape[1]), value.dtype)], 0)


def weight_scratch(cols, width):
    return pltpu.VMEM((cols, D, width), BF)


def load_weights(sources, target, sem):
    return [pltpu.make_async_copy(sources[0], target, sem)]


def start_all(copies):
    for copy in copies:
        copy.start()


def wait_all(copies):
    for copy in copies:
        copy.wait()


class Sizes:
    def __init__(self, tokens, cols):
        self.members = FRAMES * PATCHES // tokens
        self.frames = FRAMES // self.members
        self.groups = -(-PATCHES // (self.members * TILE))
        self.share = self.groups * TILE
        self.span = self.members * self.share
        self.piece = self.frames * TILE
        self.group_rows = self.members * self.piece
        self.rows = self.frames * FRAME_PAD
        self.patch_rows = self.groups * self.group_rows
        self.cols = cols
        self.half = D // cols
        self.units = FF // cols


def send_pieces(z, place_ref, spread_ref, piece_refs):
    for apart in range(z.members):
        start = (place_ref[0] ^ apart) * z.share
        for g in range(z.groups):
            parts = [
                spread_ref[pl.ds(pl.multiple_of(f * z.span + start + g * TILE, TILE), TILE), :]
                for f in range(z.frames)
            ]
            piece_refs[apart][g] = jnp.concatenate(parts, 0).astype(BF)


def take_pieces(z, place_ref, spread_ref, apart, rows):
    start = (place_ref[0] ^ apart) * z.share
    for g in range(z.groups):
        for f in range(z.frames):
            at = g * z.piece + f * TILE
            spread_ref[pl.ds(pl.multiple_of(f * z.span + start + g * TILE, TILE), TILE), :] = rows[
                at : at + TILE
            ]


def gather_groups(z, piece_refs, rows_ref):
    for g in range(z.groups):
        for m in range(z.members):
            at = g * z.group_rows + m * z.piece
            rows_ref[at : at + z.piece, :] = piece_refs[m][g]


def call(body, name, grid, in_specs, out_specs, out_shape, scratch, args, flops):
    moved = sum(a.size * a.dtype.itemsize for a in args) + sum(
        s.size * s.dtype.itemsize for s in out_shape
    )
    return pl.pallas_call(
        body,
        name=name,
        grid=grid,
        in_specs=in_specs,
        out_specs=out_specs,
        out_shape=out_shape,
        scratch_shapes=scratch,
        compiler_params=pltpu.CompilerParams(
            vmem_limit_bytes=58 * 2**20, dimension_semantics=("arbitrary",) * len(grid)
        ),
        cost_estimate=pl.CostEstimate(flops=int(flops), bytes_accessed=int(moved), transcendentals=0),
    )(*args)


def spatial_forward(z, place, hidden, wq, wo, bias, out_bias, gains, shifts):
    wide = 3 * z.half

    def body(place_ref, h_ref, *refs):
        wq_refs, refs = refs[: len(wq)], refs[len(wq) :]
        wo_refs, refs = refs[: len(wo)], refs[len(wo) :]
        bias_ref, ob_ref, gain_ref, shift_ref, *refs = refs
        x_ref, qkv_ref, mixed_ref, h1_ref, *refs = refs
        piece_refs, refs = refs[: z.members], refs[z.members :]
        wq_s, wo_s, qkv_s, mixed_s, spread, sem = refs
        f = pl.program_id(0)

        @pl.when(f == 0)
        def _():
            first = load_weights(wq_refs, wq_s, sem.at[0])
            later = load_weights(wo_refs, wo_s, sem.at[1])
            start_all(first)
            start_all(later)
            for at in range(z.frames):
                x_ref[at] = norm_rows(h_ref[at], gain_ref[0:1], shift_ref[0:1]).astype(BF)
            spread[...] = jnp.zeros_like(spread)
            wait_all(first)
            x = x_ref[...].reshape(z.rows, D)
            for c in range(z.cols):
                out = dot_nn(x, wq_s[c]) + bias_ref[c]
                qkv_s[:, c * wide : (c + 1) * wide] = out.astype(BF)
            wait_all(later)

        valid = frame_valid()
        rows = pl.ds(pl.multiple_of(f * FRAME_PAD, 16), FRAME_PAD)
        qkv_ref[0] = qkv_s[rows, :]
        for c in range(z.cols):
            for pair in range(z.half // PAIR):
                q, k, v = [
                    qkv_s[rows, pl.ds(c * wide + t * z.half + pair * PAIR, PAIR)] for t in range(3)
                ]
                at = c * z.half + pair * PAIR
                mixed_s[rows, at : at + PAIR] = attend_pair(q, key_rows(k), key_rows(v), valid)

        @pl.when(f == z.frames - 1)
        def _():
            branch = ob_ref[0:1]
            for c in range(z.cols):
                branch = branch + dot_nt(mixed_s[:, c * z.half : (c + 1) * z.half], wo_s[c])
            mixed_ref[...] = mixed_s[...].reshape(mixed_ref.shape)
            for at in range(z.frames):
                h1 = h_ref[at] + branch[at * FRAME_PAD : (at + 1) * FRAME_PAD]
                h1_ref[at] = h1
                spread[at * z.span : at * z.span + FRAME_PAD, :] = norm_rows(
                    h1, gain_ref[1:2], shift_ref[1:2]
                )
            send_pieces(z, place_ref, spread, piece_refs)

    frame = (z.frames, FRAME_PAD, D)
    piece = (z.groups, z.piece, D)
    return call(
        body,
        "spatial_forward",
        (z.frames,),
        [SMEM, whole(frame)]
        + [ANY] * (len(wq) + len(wo))
        + [whole(bias.shape), whole(out_bias.shape), whole(gains.shape), whole(shifts.shape)],
        [
            whole(frame),
            pl.BlockSpec((1, FRAME_PAD, 3 * D), lambda f: (f, 0, 0)),
            whole(frame),
            whole(frame),
        ]
        + [whole(piece)] * z.members,
        [
            shaped(frame, BF),
            shaped((z.frames, FRAME_PAD, 3 * D), BF),
            shaped(frame, BF),
            shaped(frame, F32),
        ]
        + [shaped(piece, BF)] * z.members,
        [
            weight_scratch(z.cols, wide),
            weight_scratch(z.cols, z.half),
            pltpu.VMEM((z.rows, 3 * D), BF),
            pltpu.VMEM((z.rows, D), BF),
            pltpu.VMEM((z.frames * z.span, D), F32),
            pltpu.SemaphoreType.DMA((2,)),
        ],
        (place, hidden, *wq, *wo, bias, out_bias, gains, shifts),
        2 * z.rows * D * (4 * D + 2 * KEY_PAD),
    )


def temporal_forward(z, pieces, wq, bias):
    wide = 3 * z.half
    n = z.group_rows

    def body(*refs):
        in_refs, refs = refs[: z.members], refs[z.members :]
        wq_refs, refs = refs[: len(wq)], refs[len(wq) :]
        bias_ref, qkv_ref, *refs = refs
        out_refs, refs = refs[: z.members], refs[z.members :]
        wq_s, x_s, qkv_s, sem = refs
        g = pl.program_id(0)

        @pl.when(g == 0)
        def _():
            copies = load_weights(wq_refs, wq_s, sem.at[0])
            start_all(copies)
            gather_groups(z, in_refs, x_s)
            wait_all(copies)
            x = x_s[...]
            for c in range(z.cols):
                out = dot_nn(x, wq_s[c]) + bias_ref[c]
                qkv_s[:, c * wide : (c + 1) * wide] = out.astype(BF)

        valid = patch_valid(n)
        rows = pl.ds(pl.multiple_of(g * n, n), n)
        qkv_ref[0] = qkv_s[rows, :]
        for c in range(z.cols):
            for pair in range(z.half // PAIR):
                q, k, v = [
                    qkv_s[rows, pl.ds(c * wide + t * z.half + pair * PAIR, PAIR)] for t in range(3)
                ]
                out = attend_pair(q, k, v, valid)
                at = c * z.half + pair * PAIR
                for m in range(z.members):
                    out_refs[m][0, :, at : at + PAIR] = out[m * z.piece : (m + 1) * z.piece]

    piece = (z.groups, z.piece, D)
    step = pl.BlockSpec((1, z.piece, D), lambda g: (g, 0, 0))
    return call(
        body,
        "temporal_forward",
        (z.groups,),
        [whole(piece)] * z.members + [ANY] * len(wq) + [whole(bias.shape)],
        [pl.BlockSpec((1, n, 3 * D), lambda g: (g, 0, 0))] + [step] * z.members,
        [shaped((z.groups, n, 3 * D), BF)] + [shaped(piece, BF)] * z.members,
        [
            weight_scratch(z.cols, wide),
            pltpu.VMEM((z.patch_rows, D), BF),
            pltpu.VMEM((z.patch_rows, 3 * D), BF),
            pltpu.SemaphoreType.DMA((1,)),
        ],
        (*pieces, *wq, bias),
        2 * z.patch_rows * D * (3 * D + 2 * n),
    )


def hidden_forward(z, place, pieces, hidden, wo, wu, wd, out_bias, up_bias, down_bias, gains, shifts):
    steps = FF // CHUNK
    per = z.units // CHUNK

    def body(place_ref, *refs):
        in_refs, refs = refs[: z.members], refs[z.members :]
        h1_ref, *refs = refs
        wo_refs, refs = refs[: len(wo)], refs[len(wo) :]
        wu_refs, refs = refs[: len(wu)], refs[len(wu) :]
        wd_refs, refs = refs[: len(wd)], refs[len(wd) :]
        ob_ref, ub_ref, db_ref, gain_ref, shift_ref, *refs = refs
        h2_ref, x_ref, act_ref, slope_ref, h3_ref, *refs = refs
        wo_s, wu_s, wd_s, spread, sem = refs
        i = pl.program_id(0)

        @pl.when(i == 0)
        def _():
            first = load_weights(wo_refs, wo_s, sem.at[0])
            second = load_weights(wu_refs, wu_s, sem.at[1])
            third = load_weights(wd_refs, wd_s, sem.at[2])
            start_all(first)
            start_all(second)
            start_all(third)
            wait_all(first)
            for m in range(z.members):
                mixed = in_refs[m][...].reshape(z.groups * z.piece, D)
                branch = 0.0
                for c in range(z.cols):
                    branch = branch + dot_nt(mixed[:, c * z.half : (c + 1) * z.half], wo_s[c])
                take_pieces(z, place_ref, spread, m, branch)
            for f in range(z.frames):
                rows = slice(f * FRAME_PAD, (f + 1) * FRAME_PAD)
                h2 = h1_ref[f] + spread[f * z.span : f * z.span + FRAME_PAD, :] + ob_ref[1:2]
                h2_ref[f] = h2
                x_ref[rows, :] = norm_rows(h2, gain_ref[2:3], shift_ref[2:3]).astype(BF)
                h3_ref[f] = h2 + db_ref[...]
            wait_all(second)
            wait_all(third)

        c = i // per
        cut = pl.ds(pl.multiple_of((i % per) * CHUNK, CHUNK), CHUNK)
        up = wu_s[c, :, cut]
        down = wd_s[c, :, cut]
        bias = ub_ref[...]
        for f in range(z.frames):
            rows = slice(f * FRAME_PAD, (f + 1) * FRAME_PAD)
            act, slope = gelu_parts(dot_nn(x_ref[rows, :], up) + bias)
            act = act.astype(BF)
            act_ref[rows, :] = act
            slope_ref[rows, :] = slope.astype(slope_ref.dtype)
            h3_ref[f] += dot_nt(act, down)

    frame = (z.frames, FRAME_PAD, D)
    piece = (z.groups, z.piece, D)
    step = pl.BlockSpec((z.rows, CHUNK), lambda i: (0, i))
    return call(
        body,
        "hidden_forward",
        (steps,),
        [SMEM]
        + [whole(piece)] * z.members
        + [whole(frame)]
        + [ANY] * (len(wo) + len(wu) + len(wd))
        + [
            whole(out_bias.shape),
            pl.BlockSpec((1, CHUNK), lambda i: (0, i)),
            whole(down_bias.shape),
            whole(gains.shape),
            whole(shifts.shape),
        ],
        [whole(frame), whole((z.rows, D)), step, step, whole(frame)],
        [
            shaped(frame, F32),
            shaped((z.rows, D), BF),
            shaped((z.rows, FF), BF),
            shaped((z.rows, FF), F32),
            shaped(frame, F32),
        ],
        [
            weight_scratch(z.cols, z.half),
            weight_scratch(z.cols, z.units),
            weight_scratch(z.cols, z.units),
            pltpu.VMEM((z.frames * z.span, D), F32),
            pltpu.SemaphoreType.DMA((3,)),
        ],
        (place, *pieces, hidden, *wo, *wu, *wd, out_bias, up_bias, down_bias, gains, shifts),
        2 * z.rows * D * (D + 2 * FF),
    )


def hidden_backward(z, place, grad, h2, slope, wu, wd, gains):
    steps = FF // CHUNK
    per = z.units // CHUNK

    def body(place_ref, g_ref, h2_ref, slope_ref, *refs):
        wu_refs, refs = refs[: len(wu)], refs[len(wu) :]
        wd_refs, refs = refs[: len(wd)], refs[len(wd) :]
        gain_ref, di_ref, gb_ref, g2_ref, sums_ref, *refs = refs
        piece_refs, refs = refs[: z.members], refs[z.members :]
        wu_s, wd_s, dx_s, spread, sem = refs
        i = pl.program_id(0)

        @pl.when(i == 0)
        def _():
            first = load_weights(wd_refs, wd_s, sem.at[0])
            second = load_weights(wu_refs, wu_s, sem.at[1])
            start_all(first)
            start_all(second)
            total = 0.0
            for f in range(z.frames):
                rows = slice(f * FRAME_PAD, (f + 1) * FRAME_PAD)
                g = g_ref[f]
                gb_ref[rows, :] = g.astype(BF)
                total = total + jnp.sum(g, axis=0, keepdims=True)
            sums_ref[0:1] = total
            dx_s[...] = jnp.zeros_like(dx_s)
            spread[...] = jnp.zeros_like(spread)
            wait_all(first)
            wait_all(second)

        c = i // per
        cut = pl.ds(pl.multiple_of((i % per) * CHUNK, CHUNK), CHUNK)
        up = wu_s[c, :, cut]
        down = wd_s[c, :, cut]
        for f in range(z.frames):
            rows = slice(f * FRAME_PAD, (f + 1) * FRAME_PAD)
            di = (dot_nn(gb_ref[rows, :], down) * slope_ref[rows, :]).astype(BF)
            di_ref[rows, :] = di
            dx_s[rows, :] += dot_nt(di, up)

        @pl.when(i == steps - 1)
        def _():
            out_b = gain_g = shift_g = 0.0
            for f in range(z.frames):
                rows = slice(f * FRAME_PAD, (f + 1) * FRAME_PAD)
                g2, gg, sg = norm_rows_back(h2_ref[f], gain_ref[2:3], dx_s[rows, :], g_ref[f])
                g2_ref[f] = g2
                spread[f * z.span : f * z.span + FRAME_PAD, :] = g2
                gain_g, shift_g = gain_g + gg, shift_g + sg
                out_b = out_b + jnp.sum(g2, axis=0, keepdims=True)
            sums_ref[1:2] = gain_g
            sums_ref[2:3] = shift_g
            sums_ref[3:4] = out_b
            send_pieces(z, place_ref, spread, piece_refs)

    frame = (z.frames, FRAME_PAD, D)
    piece = (z.groups, z.piece, D)
    step = pl.BlockSpec((z.rows, CHUNK), lambda i: (0, i))
    return call(
        body,
        "hidden_backward",
        (steps,),
        [SMEM, whole(frame), whole(frame), step]
        + [ANY] * (len(wu) + len(wd))
        + [whole(gains.shape)],
        [step, whole((z.rows, D)), whole(frame), whole((4, D))] + [whole(piece)] * z.members,
        [
            shaped((z.rows, FF), BF),
            shaped((z.rows, D), BF),
            shaped(frame, F32),
            shaped((4, D), F32),
        ]
        + [shaped(piece, BF)] * z.members,
        [
            weight_scratch(z.cols, z.units),
            weight_scratch(z.cols, z.units),
            pltpu.VMEM((z.rows, D), F32),
            pltpu.VMEM((z.frames * z.span, D), F32),
            pltpu.SemaphoreType.DMA((2,)),
        ],
        (place, grad, h2, slope, *wu, *wd, gains),
        2 * z.rows * D * 2 * FF,
    )


def temporal_backward(z, grad_pieces, qkv, wq, wo):
    wide = 3 * z.half
    n = z.group_rows

    def body(*refs):
        in_refs, refs = refs[: z.members], refs[z.members :]
        qkv_ref, *refs = refs
        wq_refs, refs = refs[: len(wq)], refs[len(wq) :]
        wo_refs, refs = refs[: len(wo)], refs[len(wo) :]
        d_ref, *refs = refs
        out_refs, refs = refs[: z.members], refs[z.members :]
        wq_s, wo_s, gb_s, dm_s, d_s, sem = refs
        g = pl.program_id(0)

        @pl.when(g == 0)
        def _():
            first = load_weights(wo_refs, wo_s, sem.at[0])
            start_all(first)
            start_all(load_weights(wq_refs, wq_s, sem.at[1]))
            gather_groups(z, in_refs, gb_s)
            wait_all(first)
            gb = gb_s[...]
            for c in range(z.cols):
                dm_s[:, c * z.half : (c + 1) * z.half] = dot_nn(gb, wo_s[c]).astype(BF)

        valid = patch_valid(n)
        rows = pl.ds(pl.multiple_of(g * n, n), n)
        for c in range(z.cols):
            for pair in range(z.half // PAIR):
                at = c * z.half + pair * PAIR
                q, k, v = [
                    qkv_ref[0, :, pl.ds(c * wide + t * z.half + pair * PAIR, PAIR)] for t in range(3)
                ]
                grads = attend_pair_back(q, k, v, dm_s[rows, at : at + PAIR], valid)
                for t in range(3):
                    col = c * wide + t * z.half + pair * PAIR
                    d_s[rows, col : col + PAIR] = grads[t]
        d_ref[...] = d_s[rows, :]

        @pl.when(g == z.groups - 1)
        def _():
            wait_all(load_weights(wq_refs, wq_s, sem.at[1]))
            dx = 0.0
            for c in range(z.cols):
                dx = dx + dot_nt(d_s[:, c * wide : (c + 1) * wide], wq_s[c])
            dx = dx.astype(BF)
            for gg in range(z.groups):
                for m in range(z.members):
                    at = gg * n + m * z.piece
                    out_refs[m][gg] = dx[at : at + z.piece]

    piece = (z.groups, z.piece, D)
    return call(
        body,
        "temporal_backward",
        (z.groups,),
        [whole(piece)] * z.members
        + [pl.BlockSpec((1, n, 3 * D), lambda g: (g, 0, 0))]
        + [ANY] * (len(wq) + len(wo)),
        [pl.BlockSpec((n, 3 * D), lambda g: (g, 0))] + [whole(piece)] * z.members,
        [shaped((z.patch_rows, 3 * D), BF)] + [shaped(piece, BF)] * z.members,
        [
            weight_scratch(z.cols, wide),
            weight_scratch(z.cols, z.half),
            pltpu.VMEM((z.patch_rows, D), BF),
            pltpu.VMEM((z.patch_rows, D), BF),
            pltpu.VMEM((z.patch_rows, 3 * D), BF),
            pltpu.SemaphoreType.DMA((2,)),
        ],
        (*grad_pieces, qkv, *wq, *wo),
        2 * z.patch_rows * D * (4 * D + 5 * n),
    )


def spatial_backward(z, place, dx_pieces, grad, h1, qkv, wo, gains):
    wide = 3 * z.half

    def body(place_ref, *refs):
        in_refs, refs = refs[: z.members], refs[z.members :]
        g_ref, h1_ref, qkv_ref, *refs = refs
        wo_refs, refs = refs[: len(wo)], refs[len(wo) :]
        gain_ref, gb_ref, d_ref, g1_ref, sums_ref, *refs = refs
        wo_s, spread, dm_s, sem = refs
        f = pl.program_id(0)

        @pl.when(f == 0)
        def _():
            first = load_weights(wo_refs, wo_s, sem.at[0])
            start_all(first)
            for m in range(z.members):
                rows = in_refs[m][...].reshape(z.groups * z.piece, D).astype(F32)
                take_pieces(z, place_ref, spread, m, rows)
            out_b = gain_g = shift_g = 0.0
            for at in range(z.frames):
                rows = slice(at * FRAME_PAD, (at + 1) * FRAME_PAD)
                dx = spread[at * z.span : at * z.span + FRAME_PAD, :]
                g1, gg, sg = norm_rows_back(h1_ref[at], gain_ref[1:2], dx, g_ref[at])
                g1_ref[at] = g1
                gb_ref[rows, :] = g1.astype(BF)
                gain_g, shift_g = gain_g + gg, shift_g + sg
                out_b = out_b + jnp.sum(g1, axis=0, keepdims=True)
            sums_ref[0:1] = gain_g
            sums_ref[1:2] = shift_g
            sums_ref[2:3] = out_b
            wait_all(first)
            gb = gb_ref[...]
            for c in range(z.cols):
                dm_s[:, c * z.half : (c + 1) * z.half] = dot_nn(gb, wo_s[c]).astype(BF)

        valid = frame_valid()
        rows = pl.ds(pl.multiple_of(f * FRAME_PAD, 16), FRAME_PAD)
        for c in range(z.cols):
            for pair in range(z.half // PAIR):
                at = c * z.half + pair * PAIR
                q, k, v = [
                    qkv_ref[0, :, pl.ds(c * wide + t * z.half + pair * PAIR, PAIR)] for t in range(3)
                ]
                dq, dk, dv = attend_pair_back(
                    q, key_rows(k), key_rows(v), dm_s[rows, at : at + PAIR], valid
                )
                for t, value in enumerate((dq, dk[:FRAME_PAD], dv[:FRAME_PAD])):
                    col = c * wide + t * z.half + pair * PAIR
                    d_ref[:, col : col + PAIR] = value

    frame = (z.frames, FRAME_PAD, D)
    piece = (z.groups, z.piece, D)
    return call(
        body,
        "spatial_backward",
        (z.frames,),
        [SMEM]
        + [whole(piece)] * z.members
        + [whole(frame), whole(frame), pl.BlockSpec((1, FRAME_PAD, 3 * D), lambda f: (f, 0, 0))]
        + [ANY] * len(wo)
        + [whole(gains.shape)],
        [
            whole((z.rows, D)),
            pl.BlockSpec((FRAME_PAD, 3 * D), lambda f: (f, 0)),
            whole(frame),
            whole((3, D)),
        ],
        [
            shaped((z.rows, D), BF),
            shaped((z.rows, 3 * D), BF),
            shaped(frame, F32),
            shaped((3, D), F32),
        ],
        [
            weight_scratch(z.cols, z.half),
            pltpu.VMEM((z.frames * z.span, D), F32),
            pltpu.VMEM((z.rows, D), BF),
            pltpu.SemaphoreType.DMA((1,)),
        ],
        (place, *dx_pieces, grad, h1, qkv, *wo, gains),
        2 * z.rows * D * (D + 5 * KEY_PAD),
    )


def input_backward(z, d, grad, hidden, wq, gains):
    wide = 3 * z.half

    def body(d_ref, g_ref, h_ref, *refs):
        wq_refs, refs = refs[: len(wq)], refs[len(wq) :]
        gain_ref, g0_ref, sums_ref, wq_s, sem = refs
        f = pl.program_id(0)

        @pl.when(f == 0)
        def _():
            copies = load_weights(wq_refs, wq_s, sem.at[0])
            start_all(copies)
            wait_all(copies)
            sums_ref[...] = jnp.zeros_like(sums_ref)

        dx = 0.0
        for c in range(z.cols):
            dx = dx + dot_nt(d_ref[:, c * wide : (c + 1) * wide], wq_s[c])
        for at in range(2):
            rows = slice(at * FRAME_PAD, (at + 1) * FRAME_PAD)
            g0, gg, sg = norm_rows_back(h_ref[at], gain_ref[0:1], dx[rows], g_ref[at])
            g0_ref[at] = g0
            sums_ref[0:1] += gg
            sums_ref[1:2] += sg

    frame = (z.frames, FRAME_PAD, D)
    step = pl.BlockSpec((2, FRAME_PAD, D), lambda f: (f, 0, 0))
    return call(
        body,
        "input_backward",
        (z.frames // 2,),
        [pl.BlockSpec((2 * FRAME_PAD, 3 * D), lambda f: (f, 0)), step, step]
        + [ANY] * len(wq)
        + [whole(gains.shape)],
        [step, whole((2, D))],
        [shaped(frame, F32), shaped((2, D), F32)],
        [weight_scratch(z.cols, wide), pltpu.SemaphoreType.DMA((1,))],
        (d, grad, hidden, *wq, gains),
        2 * z.rows * D * 3 * D,
    )


def weight_grad(z, name, left, right, step):
    total = right[0].shape[-1]
    width = total // z.cols
    per = width // step
    rows = sum(a.shape[0] for a in left)

    def body(*refs):
        left_refs, refs = refs[: len(left)], refs[len(left) :]
        right_refs, refs = refs[: len(right)], refs[len(right) :]
        out_ref, sums_ref, turned = refs

        @pl.when(pl.program_id(0) == 0)
        def _():
            parts = [r[...] for r in left_refs]
            value = parts[0] if len(parts) == 1 else jnp.concatenate(parts, 0)
            turned[...] = value.T

        parts = [r[...] for r in right_refs]
        value = parts[0] if len(parts) == 1 else jnp.concatenate(parts, 0)
        sums_ref[...] = jnp.sum(value.astype(F32), axis=0, keepdims=True)
        out_ref[0] = dot_nn(turned[...], value).astype(BF)

    return call(
        body,
        name,
        (total // step,),
        [whole(a.shape) for a in left]
        + [pl.BlockSpec((a.shape[0], step), lambda i: (0, i)) for a in right],
        [
            pl.BlockSpec((1, D, step), lambda i: (i // per, 0, i % per)),
            pl.BlockSpec((1, step), lambda i: (0, i)),
        ],
        [shaped((z.cols, D, width), BF), shaped((1, total), F32)],
        [pltpu.VMEM((D, rows), BF)],
        (*left, *right),
        2 * rows * D * total,
    )


def clip_swap(value, apart):
    count = lax.axis_size("row") * lax.axis_size("col")
    return lax.ppermute(value, CLIP_AXES, [(at, at ^ apart) for at in range(count)])


def swap_pieces(pieces):
    return [pieces[0]] + [clip_swap(pieces[apart], apart) for apart in range(1, len(pieces))]


def flat(pieces):
    return [p.reshape(-1, D) for p in pieces]


def pad_frames(z, rows):
    grid = rows.reshape(z.frames, PATCHES, D)
    return jnp.pad(grid, ((0, 0), (0, FRAME_PAD - PATCHES), (0, 0)))


def cut_frames(z, grid):
    return grid[:, :PATCHES].reshape(z.frames * PATCHES, D)


def layer_forward(z, place, hidden, w, small):
    gains, shifts, bias_qkv, bias_out, bias_up, bias_down = small
    x0, qkv0, mixed0, h1, *send = spatial_forward(
        z, place, hidden, w["qkv0"], w["out0"], bias_qkv[0], bias_out, gains, shifts
    )
    pieces = swap_pieces(send)
    qkv1, *back = temporal_forward(z, pieces, w["qkv1"], bias_qkv[1])
    mixed1 = swap_pieces(back)
    h2, x2, act, slope, h3 = hidden_forward(
        z, place, mixed1, h1, w["out1"], w["up"], w["down"], bias_out, bias_up, bias_down, gains, shifts
    )
    return h3, (hidden, x0, qkv0, mixed0, h1, pieces, qkv1, mixed1, h2, x2, act, slope)


def group_rows(z, pieces):
    stacked = jnp.stack(pieces, axis=1)
    return stacked.reshape(z.patch_rows, D)


def layer_backward(z, place, grad, record, w, small, spend):
    gains, *_ = small
    hidden, x0, qkv0, mixed0, h1, pieces, qkv1, mixed1, h2, x2, act, slope = record
    di, gb, g2, sums_h, *send = hidden_backward(z, place, grad, h2, slope, w["up"], w["down"], gains)
    got = swap_pieces(send)
    down_g, _ = weight_grad(z, "down_grad", [gb], [act], CHUNK)
    spend("down", down_g)
    up_g, up_b = weight_grad(z, "up_grad", [x2], [di], CHUNK)
    spend("up", up_g)
    out1_g, _ = weight_grad(z, "out1_grad", flat(send), flat(mixed1), z.half)
    spend("out1", out1_g)
    d1, *back = temporal_backward(z, got, qkv1, w["qkv1"], w["out1"])
    dx = swap_pieces(back)
    qkv1_g, qkv1_b = weight_grad(z, "qkv1_grad", [group_rows(z, pieces)], [d1], z.half)
    spend("qkv1", qkv1_g)
    gb, d0, g1, sums_s = spatial_backward(z, place, dx, g2, h1, qkv0, w["out0"], gains)
    out0_g, _ = weight_grad(z, "out0_grad", [gb], [mixed0.reshape(z.rows, D)], z.half)
    spend("out0", out0_g)
    qkv0_g, qkv0_b = weight_grad(z, "qkv0_grad", [x0.reshape(z.rows, D)], [d0], z.half)
    spend("qkv0", qkv0_g)
    g0, sums_i = input_backward(z, d0, g1, hidden, w["qkv0"], gains)

    def qv(sums):
        parts = sums.reshape(z.cols, 3, z.half)
        return jnp.stack([parts[:, 0].reshape(D), parts[:, 2].reshape(D)])

    small_g = (
        jnp.stack([sums_i[0], sums_s[0], sums_h[1]]),
        jnp.stack([sums_i[1], sums_s[1], sums_h[2]]),
        jnp.stack([qv(qkv0_b), qv(qkv1_b)]),
        jnp.stack([sums_s[2], sums_h[3]]),
        up_b[0],
        sums_h[0],
    )
    return g0, small_g


def own_parts(qkv_weight, out_weight, up_weight, down_weight, at):
    rows = up_weight.shape[1]
    return {
        "qkv0": qkv_weight[at, 0].reshape(rows, -1),
        "out0": out_weight[at, 0].T,
        "qkv1": qkv_weight[at, 1].reshape(rows, -1),
        "out1": out_weight[at, 1].T,
        "up": up_weight[at],
        "down": down_weight[at].T,
    }


PARTS = ("qkv0", "out0", "qkv1", "out1", "up", "down")


def fetch(parts, cols):
    packed = jnp.concatenate([parts[name] for name in PARTS], axis=1)
    full = lax.all_gather(packed, ROWS_AXES, axis=0, tiled=True).reshape(cols, D, -1)
    result, at = {}, 0
    for name in PARTS:
        width = parts[name].shape[1]
        result[name] = [full[:, :, at : at + width]]
        at += width
    return result


def scatter(grads, cols):
    packed = jnp.concatenate([grads[name] for name in PARTS], axis=2)
    own = lax.psum_scatter(packed.reshape(cols * D, -1), ROWS_AXES, scatter_dimension=0, tiled=True)
    result, at = {}, 0
    for name in PARTS:
        width = grads[name].shape[2]
        result[name] = own[:, at : at + width].astype(F32)
        at += width
    return result


def shards(
    hidden_in,
    qkv_weight,
    out_weight,
    up_weight,
    down_weight,
    qv_bias,
    out_bias,
    up_bias,
    down_bias,
    norm_gain,
    norm_shift,
    cotangent,
):
    layers = qkv_weight.shape[0]
    cols = lax.axis_size("col")
    z = Sizes(hidden_in.shape[0], cols)
    place = lax.axis_index("row") * cols + lax.axis_index("col")
    place = (place % z.members).astype(jnp.int32).reshape(1)
    qv_all = lax.all_gather(qv_bias, "col", axis=3)
    up_all = lax.all_gather(up_bias, "col", axis=1, tiled=True)
    zero = jnp.zeros_like(qv_all[:, :, 0])
    bias_qkv = jnp.stack([qv_all[:, :, 0], zero, qv_all[:, :, 1]], axis=3)
    bias_qkv = bias_qkv.reshape(layers, 2, cols, 1, 3 * z.half)
    hidden = pad_frames(z, hidden_in)
    kept = []
    for at in range(layers):
        w = fetch(own_parts(qkv_weight, out_weight, up_weight, down_weight, at), cols)
        small = (
            norm_gain[at],
            norm_shift[at],
            bias_qkv[at],
            out_bias[at],
            up_all[at][None],
            down_bias[at][None],
        )
        hidden, record = layer_forward(z, place, hidden, w, small)
        kept.append((w, small, record))
    grad = pad_frames(z, cotangent)
    owned = [None] * layers
    smalls = [None] * layers
    for at in reversed(range(layers)):
        w, small, record = kept[at]
        grads = {}
        grad, smalls[at] = layer_backward(z, place, grad, record, w, small, grads.__setitem__)
        owned[at] = scatter(grads, cols)
    rows = up_weight.shape[1]

    def both(make):
        return jnp.stack([make(owned[at]) for at in range(layers)])

    grad_qkv = both(
        lambda o: jnp.stack([o["qkv0"].reshape(rows, 3, -1), o["qkv1"].reshape(rows, 3, -1)])
    )
    grad_out = both(lambda o: jnp.stack([o["out0"].T, o["out1"].T]))
    grad_up = both(lambda o: o["up"])
    grad_down = both(lambda o: o["down"].T)
    terms = [jnp.stack([smalls[at][i] for at in range(layers)]) for i in range(6)]
    gain, shift, qv, outb, upb, downb = lax.psum(tuple(terms), ALL_AXES)
    col_at = lax.axis_index("col")
    qv = lax.dynamic_slice_in_dim(qv, col_at * z.half, z.half, 3)
    upb = lax.dynamic_slice_in_dim(upb, col_at * z.units, z.units, 1)
    return (
        cut_frames(z, hidden),
        cut_frames(z, grad),
        grad_qkv,
        grad_out,
        grad_up,
        grad_down,
        qv,
        outb,
        upb,
        downb,
        gain,
        shift,
    )


def solution(mesh):
    return jax.shard_map(
        shards,
        mesh=mesh,
        in_specs=(
            P(("dp", "row", "col"), None),
            P(None, None, ("dp", "row"), None, "col"),
            P(None, None, "col", ("dp", "row")),
            P(None, ("dp", "row"), "col"),
            P(None, "col", ("dp", "row")),
            P(None, None, None, "col"),
            P(),
            P(None, "col"),
            P(),
            P(),
            P(),
            P(("dp", "row", "col"), None),
        ),
        out_specs=(
            P(("dp", "row", "col"), None),
            P(("dp", "row", "col"), None),
            P(None, None, ("dp", "row"), None, "col"),
            P(None, None, "col", ("dp", "row")),
            P(None, ("dp", "row"), "col"),
            P(None, "col", ("dp", "row")),
            P(None, None, None, "col"),
            P(),
            P(None, "col"),
            P(),
            P(),
            P(),
        ),
        check_vma=False,
    )
```

time: 1770 us -> 1320 us (0.75); the launches traced: 1750 us -> 1320 us
  local copies, waits for them, and re-layouts: 756 us -> 116 us
  Pallas kernels: 0 us -> 431 us
  matrix products: 358 us -> 0 us
  waiting for transfers between devices: 418 us -> 705 us
  other arithmetic: 162 us -> 11.9 us
    pallas_call x0 -> x26, Pallas kernels: none -> 431 us  [call(): pl.pallas_call(body, name=name, grid=grid, in_specs=in_specs, out_specs=o...]
    reduce_scatter x0 -> x2, waiting for transfers between devices: none -> 416 us  [scatter(): lax.psum_scatter(packed.reshape(cols * D, -1), ROWS_AXES, scatter_dimensi...]
    dot_general x58 -> x0, matrix products: 339 us -> none  [dot(): return jnp.einsum(dims, left, right, preferred_element_type=jnp.float32)]
    unnamed x7 -> x5, waiting for transfers between devices: 287 us -> 0.64 us
    another operation x79 -> x12, local copies, waits for them, and re-layouts: 176 us -> 4.43 us  [the longest x2 2.37 us: group_rows(): stacked = jnp.stack(pieces, axis=1)]
    unnamed x456 -> x153, local copies, waits for them, and re-layouts: 176 us -> 36.5 us
    psum x1, waiting for transfers between devices: 0.01 us -> 78.1 us  [shards(): gain, shift, qv, outb, upb, downb = lax.psum(tuple(terms), ALL_AXES)]
    concatenate x4 -> x0, other arithmetic: 76.1 us -> none  [the longest x2 74.4 us: pack_grads(): return jnp.concatenate([qkv, out, up, down], axis=2).astype(jnp.bfloat16)]
  transfers between devices with their start and end apart: 29 -> 29, of which waited for: 7 -> 13; matrix products, arithmetic and copies ran while one was open for 39% -> 8% of each run, Pallas kernels for 0% -> 10%
where the time goes in v2:
time: 1320 us
  waiting for transfers between devices  705 us (53%)
  Pallas kernels  431 us (33%)
  local copies, waits for them, and re-layouts  116 us (9%)
  starting transfers between devices  28.7 us (2%)
  between operations  15.3 us (1%)
    pallas_call x26, Pallas kernels, call(): pl.pallas_call(body, name=name, grid=grid, in_specs=in_specs, out_specs=o...  431 us
    reduce_scatter x2, waiting for transfers between devices, scatter(): lax.psum_scatter(packed.reshape(cols * D, -1), ROWS_AXES, scatter_dimensi...  416 us
    all_gather x2, waiting for transfers between devices, fetch(): lax.all_gather(packed, ROWS_AXES, axis=0, tiled=True).reshape(cols, D, -1)  171 us
    psum x1, waiting for transfers between devices, shards(): gain, shift, qv, outb, upb, downb = lax.psum(tuple(terms), ALL_AXES)  78.1 us
    ppermute x24, waiting for transfers between devices, clip_swap(): lax.ppermute(value, CLIP_AXES, [(at, at ^ apart) for at in range(count)])  38.5 us
    unnamed x153, local copies, waits for them, and re-layouts  36.5 us
    slice x6, local copies, waits for them, and re-layouts, fetch(): result[name] = [full[:, :, at:at + width]]  35.7 us
    ppermute x24, starting transfers between devices, clip_swap(): lax.ppermute(value, CLIP_AXES, [(at, at ^ apart) for at in range(count)])  28.5 us
  transfers between devices with their start and end apart: 29, of which 13 were waited for; matrix products, arithmetic and copies ran while one was open for 8% of the time, Pallas kernels for 10%

profile of v2, /device:TPU:0, one launch (start us, length us, event | category | flops | bytes accessed | tf_op | source)
XLA Modules:
  0.0 1317.2 jit_solution(13370087644338059910)
XLA Ops:
  11.4 1.8 reshape.143
  13.3 1.7 pad.7.h_ref
  15.1 5.3 all-gather
  22.4 4.4 all_gather.18
  29.9 109.0 %all-gather.4.cloned.1.call-done = bf16[1536,6144]{1,0:T(8,128)(2,1)} async-done(((bf16[48,6144]{1,0:T(8,128)(2,1)}), bf16[1536,6144]{1,0:T(8,128)(2,1)}) %all-gather.4.cloned.1.call-update) | async-done | bytes 18874384 | tf_op jit(solution)/shard_map/all_gather | solution.py:874
  138.9 3.3 fusion.4
  142.2 6.6 fusion.5
  148.8 20.1 %spatial_forward.2 = (bf16[4,208,768]{2,1,0:T(8,128)(2,1)}, bf16[4,208,2304]{2,1,0:T(8,128)(2,1)}, bf16[4,208,768]{2,1,0:T(8,128)(2,1)}, f32[4,208,768]{2,1,0:T(...) custom-call(s32[1]{0:T(128)} %bitcast.place_ref, ...), custom_call_target="tpu_custom_call" | custom-call | flops 4580179968 | bytes 17630212 | tf_op jit(solution)/shard_map/spatial_forward/pallas_call | solution.py:205
  172.5 8.0 fusion.3
  180.5 6.2 collective-permute-done.refs_1_
  186.7 1.9 collective-permute-done.1.refs_2_
  188.6 14.2 %collective-permute-done.2.refs_3_ = bf16[7,32,768]{2,1,0:T(8,128)(2,1)S(1)} collective-permute-done((bf16[7,32,768]{2,1,0:T(8,128)(2,1)}, bf16[7,32,768]{2,1,0:T(8,128)(2,1)S(1)}, u32[]{:S(2)}, u32[]{:S(2)}) %collective-permute-start.2) | collective-permute-done | bytes 344096 | tf_op jit(solution)/shard_map/ppermute | solution.py:781
  203.5 24.7 %temporal_forward.2 = (bf16[7,128,2304]{2,1,0:T(8,128)(2,1)}, bf16[7,32,768]{2,1,0:T(8,128)(2,1)}, bf16[7,32,768]{2,1,0:T(8,128)(2,1)}, bf16[7,32,768]{2,1,0:T(8,128)(2,1)}, bf16[7,32,768]{2,1,0:T(8,128)(2,1)}) custom-call(bf16[7,32,768]{2,1,0:T(8,128)(2,1)} %get-tuple-element.104.refs_0_, bf16[7,32,768]{2,1,0:T(8,128)(2,1)} %copy-done.16, ...), custom_call_target="tpu_custom_call" | custom-call | flops 3523215360 | bytes 10429440 | tf_op jit(solution)/shard_map/temporal_forward/pallas_call | solution.py:205
  228.2 1.8 collective-permute-start.3
  231.7 62.3 %all-gather.6.cloned.1.call-done = bf16[1536,6144]{1,0:T(8,128)(2,1)} async-done(((bf16[48,6144]{1,0:T(8,128)(2,1)}), bf16[1536,6144]{1,0:T(8,128)(2,1)}) %all-gather.6.cloned.1.call-update) | async-done | bytes 18874384 | tf_op jit(solution)/shard_map/all_gather | solution.py:874
  294.0 6.5 fusion.2
  300.5 3.3 fusion.1
  304.8 27.3 %hidden_forward.2 = (f32[4,208,768]{2,1,0:T(8,128)}, bf16[832,768]{1,0:T(8,128)(2,1)}, bf16[832,3072]{1,0:T(8,128)(2,1)}, f32[832,3072]{1,0:T(8,128)}, f32[4,208,768]{2,1,0:T(8,128)}) custom-call(s32[1]{0:T(128)} %bitcast.place_ref, bf16[7,32,768]{2,1,0:T(8,128)(2,1)} %get-tuple-element.108.refs_0_, bf16[7,32,768]{2,1,0:T(8,128)(2,1)} %copy-done.49, ...), custom_call_target="tpu_custom_call" | custom-call | flops 8833204224 | bytes 36314116 | tf_op jit(solution)/shard_map/hidden_forward/pallas_call | solution.py:205
  332.2 19.9 %spatial_forward.3 = (bf16[4,208,768]{2,1,0:T(8,128)(2,1)}, bf16[4,208,2304]{2,1,0:T(8,128)(2,1)}, bf16[4,208,768]{2,1,0:T(8,128)(2,1)}, f32[4,208,768]{2,1,0:T(...) custom-call(s32[1]{0:T(128)} %bitcast.place_ref, ...), custom_call_target="tpu_custom_call" | custom-call | flops 4580179968 | bytes 17630212 | tf_op jit(solution)/shard_map/spatial_forward/pallas_call | solution.py:205
  356.3 1.9 reshape.147
  358.2 1.7 pad.8.g_ref
  360.0 2.6 collective-permute-done.6.refs_1_
  362.6 2.0 collective-permute-done.7.refs_2_
  364.6 6.5 collective-permute-done.8.refs_3_
  371.9 24.6 %temporal_forward.3 = (bf16[7,128,2304]{2,1,0:T(8,128)(2,1)}, bf16[7,32,768]{2,1,0:T(8,128)(2,1)}, bf16[7,32,768]{2,1,0:T(8,128)(2,1)}, bf16[7,32,768]{2,1,0:T(8,128)(2,1)}, bf16[7,32,768]{2,1,0:T(8,128)(2,1)}) custom-call(bf16[7,32,768]{2,1,0:T(8,128)(2,1)} %get-tuple-element.114.refs_0_, bf16[7,32,768]{2,1,0:T(8,128)(2,1)} %copy-done.23, ...), custom_call_target="tpu_custom_call" | custom-call | flops 3523215360 | bytes 10429440 | tf_op jit(solution)/shard_map/temporal_forward/pallas_call | solution.py:205
  398.6 1.6 collective-permute-start.11
  400.2 8.0 fusion
  411.0 3.5 collective-permute-done.11.refs_3_
  415.2 27.2 %hidden_forward.3 = (f32[4,208,768]{2,1,0:T(8,128)}, bf16[832,768]{1,0:T(8,128)(2,1)}, bf16[832,3072]{1,0:T(8,128)(2,1)}, f32[832,3072]{1,0:T(8,128)}, f32[4,208,768]{2,1,0:T(8,128)}) custom-call(s32[1]{0:T(128)} %bitcast.place_ref, bf16[7,32,768]{2,1,0:T(8,128)(2,1)} %get-tuple-element.118.refs_0_, bf16[7,32,768]{2,1,0:T(8,128)(2,1)} %copy-done.52, ...), custom_call_target="tpu_custom_call" | custom-call | flops 8833204224 | bytes 36314116 | tf_op jit(solution)/shard_map/hidden_forward/pallas_call | solution.py:205
  442.4 24.0 %hidden_backward.2 = (bf16[832,3072]{1,0:T(8,128)(2,1)}, bf16[832,768]{1,0:T(8,128)(2,1)}, f32[4,208,768]{2,1,0:T(8,128)}, f32[4,768]{1,0:T(4,128)}, bf16[7,32,7...) custom-call(s32[1]{0:T(128)} %bitcast.place_ref, ...), custom_call_target="tpu_custom_call" | custom-call | flops 7851737088 | bytes 35116036 | tf_op jit(solution)/shard_map/hidden_backward/pallas_call | solution.py:205
  471.3 10.0 up_grad.3
  481.3 4.9 out1_grad.3
  486.1 10.1 down_grad.3
  497.2 32.7 %temporal_backward.2 = (bf16[896,2304]{1,0:T(8,128)(2,1)}, bf16[7,32,768]{2,1,0:T(8,128)(2,1)}, bf16[7,32,768]{2,1,0:T(8,128)(2,1)}, bf16[7,32,768]{2,1,0:T(8,128)(2,1)}, bf16[7,32,768]{2,1,0:T(8,128)(2,1)}) custom-call(bf16[7,32,768]{2,1,0:T(8,128)(2,1)} %get-tuple-element.126.refs_0_, bf16[7,32,768]{2,1,0:T(8,128)(2,1)} %copy-done.55, ...), custom_call_target="tpu_custom_call" | custom-call | flops 5108662272 | bytes 15728640 | tf_op jit(solution)/shard_map/temporal_backward/pallas_call | solution.py:205
  533.5 9.4 qkv1_grad.3
  544.2 1.6 collective-permute-done.17.refs_3_
  546.5 28.3 %spatial_backward.2 = (bf16[832,768]{1,0:T(8,128)(2,1)}, bf16[832,2304]{1,0:T(8,128)(2,1)}, f32[4,208,768]{2,1,0:T(8,128)}, f32[3,768]{1,0:T(4,128)}) custom-call(s32[1]{0:T(128)} %bitcast.place_ref, bf16[7,32,768]{2,1,0:T(8,128)(2,1)} %get-tuple-element.131.refs_0_, bf16[7,32,768]{2,1,0:T(8,128)(2,1)} %copy-done.9, bf16[7,32,768]{2,1,0:T(8,128)(2,1)} %copy-done.11, ...), custom_call_target="tpu_custom_call" | custom-call | flops 2617245696 | bytes 19187716 | tf_op jit(solution)/shard_map/spatial_backward/pallas_call | solution.py:205
  574.8 10.4 input_backward.2
  585.2 23.9 %hidden_backward.3 = (bf16[832,3072]{1,0:T(8,128)(2,1)}, bf16[832,768]{1,0:T(8,128)(2,1)}, f32[4,208,768]{2,1,0:T(8,128)}, f32[4,768]{1,0:T(4,128)}, bf16[7,32,7...) custom-call(s32[1]{0:T(128)} %bitcast.place_ref, ...), custom_call_target="tpu_custom_call" | custom-call | flops 7851737088 | bytes 35116036 | tf_op jit(solution)/shard_map/hidden_backward/pallas_call | solution.py:205
  612.7 9.3 qkv0_grad.3
  621.9 4.1 constant_dynamic-update-slice_fusion.19
  631.3 4.6 out0_grad.3
  636.0 2.5 constant_dynamic-update-slice_fusion.18
  638.5 2.1 constant_dynamic-update-slice_fusion.17
  642.8 2.6 constant_dynamic-update-slice_fusion.15
  645.4 10.0 up_grad.2
  657.6 32.7 %temporal_backward.3 = (bf16[896,2304]{1,0:T(8,128)(2,1)}, bf16[7,32,768]{2,1,0:T(8,128)(2,1)}, bf16[7,32,768]{2,1,0:T(8,128)(2,1)}, bf16[7,32,768]{2,1,0:T(8,128)(2,1)}, bf16[7,32,768]{2,1,0:T(8,128)(2,1)}) custom-call(bf16[7,32,768]{2,1,0:T(8,128)(2,1)} %get-tuple-element.142.refs_0_, bf16[7,32,768]{2,1,0:T(8,128)(2,1)} %collective-permute-done.18.refs_1_, ...), custom_call_target="tpu_custom_call" | custom-call | flops 5108662272 | bytes 15728640 | tf_op jit(solution)/shard_map/temporal_backward/pallas_call | solution.py:205
  693.8 9.4 qkv1_grad.2
  705.0 28.1 %spatial_backward.3 = (bf16[832,768]{1,0:T(8,128)(2,1)}, bf16[832,2304]{1,0:T(8,128)(2,1)}, f32[4,208,768]{2,1,0:T(8,128)}, f32[3,768]{1,0:T(4,128)}) custom-call(s32[1]{0:T(128)} %bitcast.place_ref, bf16[7,32,768]{2,1,0:T(8,128)(2,1)} %get-tuple-element.147.refs_0_, bf16[7,32,768]{2,1,0:T(8,128)(2,1)} %copy-done.10, bf16[7,32,768]{2,1,0:T(8,128)(2,1)} %copy-done.12, ...), custom_call_target="tpu_custom_call" | custom-call | flops 2617245696 | bytes 19187716 | tf_op jit(solution)/shard_map/spatial_backward/pallas_call | solution.py:205
  733.1 10.4 input_backward.3
  743.5 9.3 qkv0_grad.2
  756.2 4.8 constant_dynamic-update-slice_fusion.14
  761.1 5.1 out1_grad.2
  766.2 10.0 down_grad.2
  776.2 4.8 out0_grad.2
  781.0 2.1 constant_dynamic-update-slice_fusion.13
  785.1 2.1 constant_dynamic-update-slice_fusion.11
  788.8 2.5 constant_dynamic-update-slice_fusion.9
  791.4 2.6 constant_dynamic-update-slice_fusion.8
  793.9 1.9 slice.292
  797.4 1.9 slice.293
  800.8 78.1 %all-reduce.5.cloned.1.call-done = (f32[2,2,2,768]{3,2,1,0:T(2,128)}, f32[2,2,768]{2,1,0:T(2,128)}, f32[2,3072]{1,0:T(2,128)}, f32[2,768]{1,0:T(2,128)}, f32[2,3,768]{2,1,0:T(4,128)}, /*index=5*/f32[2,3,768]{2,1,0:T(4,128)}) async-done(((f32[2,2,2,768]{3,2,1,0:T(2,128)}, f32[2,2,768]{2,1,0:T(2,128)}, f32[2,3072]{1,0:T(2,128)}, f32[2,768]{1,0:T(2,128)}, f32[2,3,768]{2,1,0:T(4,128)}, ...) | async-done | bytes 104464 | tf_op jit(solution)/shard_map/psum | solution.py:952
  884.2 207.6 %reduce-scatter.5.cloned.1.call-done = bf16[48,6144]{1,0:T(8,128)(2,1)} async-done(((bf16[1536,6144]{1,0:T(8,128)(2,1)}), bf16[48,6144]{1,0:T(8,128)(2,1)}) %reduce-scatter.5.cloned.1.call-update) | async-done | bytes 589840 | tf_op jit(solution)/shard_map/reduce_scatter | solution.py:885
  1094.9 208.8 %reduce-scatter.3.cloned.1.call-done = bf16[48,6144]{1,0:T(8,128)(2,1)} async-done(((bf16[1536,6144]{1,0:T(8,128)(2,1)}), bf16[48,6144]{1,0:T(8,128)(2,1)}) %reduce-scatter.3.cloned.1.call-update) | async-done | bytes 589840 | tf_op jit(solution)/shard_map/reduce_scatter | solution.py:885
  (280 shorter events, 81.4 us)
Async XLA Ops:
  7.2 131.7 %all-gather.4.cloned.1.call-start = ((), (), s32[]{:S(2)}) async-start(), calls=%async_computation.2 | async-start | bytes 19464192 | tf_op jit(solution)/shard_map/all_gather | solution.py:874
  10.6 283.4 %all-gather.6.cloned.1.call-start = ((), (), s32[]{:S(2)}) async-start(), calls=%async_computation.3 | async-start | bytes 19464192 | tf_op jit(solution)/shard_map/all_gather | solution.py:874
  11.4 867.5 %all-reduce.5.cloned.1.call-start = ((), (), s32[]{:S(2)}) async-start(), calls=%async_computation.6 | async-start | bytes 233472 | tf_op jit(solution)/shard_map/psum | solution.py:952
  13.2 9.1 copy-start.39
  13.2 13.5 %copy-start.46 = (f32[2,768]{1,0:T(2,128)S(1)}, f32[2,768]{1,0:T(2,128)}, u32[]{:S(2)}) copy-start(f32[2,768]{1,0:T(2,128)} %param.20) | copy-start | bytes 18436
  13.3 14.1 %copy-start.35 = (f32[2,2,768]{2,1,0:T(2,128)S(1)}, f32[2,2,768]{2,1,0:T(2,128)}, u32[]{:S(2)}) copy-start(f32[2,2,768]{2,1,0:T(2,128)} %param.18) | copy-start | bytes 36868
  13.3 14.7 %copy-start.33 = (f32[2,3,768]{2,0,1:T(2,128)S(1)}, f32[2,3,768]{2,0,1:T(2,128)}, u32[]{:S(2)}) copy-start(f32[2,3,768]{2,0,1:T(2,128)} %param.22) | copy-start | bytes 55300
  13.3 14.7 %copy-start.34 = (f32[2,3,768]{2,0,1:T(2,128)S(1)}, f32[2,3,768]{2,0,1:T(2,128)}, u32[]{:S(2)}) copy-start(f32[2,3,768]{2,0,1:T(2,128)} %param.21) | copy-start | bytes 55300
  169.0 17.7 %collective-permute-start = (bf16[7,32,768]{2,1,0:T(8,128)(2,1)}, bf16[7,32,768]{2,1,0:T(8,128)(2,1)S(1)}, u32[]{:S(2)}, u32[]{:S(2)}) collective-permute-start(bf16[7,32,768]{2,1,0:T(8,128)(2,1)} %get-tuple-element.105), channel_id=1, source_target_pairs={{0,1},{1,0},{2,3},{3,2},{4,5},{5,4},{6,7},{7,6},{8,9},{9,8},{10,11... | collective-permute-start | bytes 1032200 | tf_op jit(solution)/shard_map/ppermute | solution.py:781
  170.5 18.1 %collective-permute-start.1 = (bf16[7,32,768]{2,1,0:T(8,128)(2,1)}, bf16[7,32,768]{2,1,0:T(8,128)(2,1)S(1)}, u32[]{:S(2)}, u32[]{:S(2)}) collective-permute-start(bf16[7,32,768]{2,1,0:T(8,128)(2,1)} %get-tuple-element.106), channel_id=1, source_target_pairs={{0,2},{1,3},{2,0},{3,1},{4,6},{5,7},{6,4},{7,5},{8,10},{9,11},{10,... | collective-permute-start | bytes 1032200 | tf_op jit(solution)/shard_map/ppermute | solution.py:781
  171.2 31.5 %collective-permute-start.2 = (bf16[7,32,768]{2,1,0:T(8,128)(2,1)}, bf16[7,32,768]{2,1,0:T(8,128)(2,1)S(1)}, u32[]{:S(2)}, u32[]{:S(2)}) collective-permute-start(bf16[7,32,768]{2,1,0:T(8,128)(2,1)} %get-tuple-element.107), channel_id=1, source_target_pairs={{0,3},{1,2},{2,1},{3,0},{4,7},{5,6},{6,5},{7,4},{8,11},{9,10},{10,... | collective-permute-start | bytes 1032200 | tf_op jit(solution)/shard_map/ppermute | solution.py:781
  186.7 16.1 %copy-start.16 = (bf16[7,32,768]{2,1,0:T(8,128)(2,1)}, bf16[7,32,768]{2,1,0:T(8,128)(2,1)S(1)}, u32[]{:S(2)}) copy-start(bf16[7,32,768]{2,1,0:T(8,128)(2,1)S(1)} %collective-permute-done.refs_1_) | copy-start | bytes 1032196
  188.6 14.2 %copy-start.18 = (bf16[7,32,768]{2,1,0:T(8,128)(2,1)}, bf16[7,32,768]{2,1,0:T(8,128)(2,1)S(1)}, u32[]{:S(2)}) copy-start(bf16[7,32,768]{2,1,0:T(8,128)(2,1)S(1)} %collective-permute-done.1.refs_2_) | copy-start | bytes 1032196
  228.2 75.7 %collective-permute-start.3 = (bf16[7,32,768]{2,1,0:T(8,128)(2,1)}, bf16[7,32,768]{2,1,0:T(8,128)(2,1)S(1)}, u32[]{:S(2)}, u32[]{:S(2)}) collective-permute-start(bf16[7,32,768]{2,1,0:T(8,128)(2,1)} %get-tuple-element.109), channel_id=1, source_target_pairs={{0,1},{1,0},{2,3},{3,2},{4,5},{5,4},{6,7},{7,6},{8,9},{9,8},{10,11... | collective-permute-start | bytes 1032200 | tf_op jit(solution)/shard_map/ppermute | solution.py:781
  230.0 73.9 %collective-permute-start.4 = (bf16[7,32,768]{2,1,0:T(8,128)(2,1)}, bf16[7,32,768]{2,1,0:T(8,128)(2,1)S(1)}, u32[]{:S(2)}, u32[]{:S(2)}) collective-permute-start(bf16[7,32,768]{2,1,0:T(8,128)(2,1)} %get-tuple-element.110), channel_id=1, source_target_pairs={{0,2},{1,3},{2,0},{3,1},{4,6},{5,7},{6,4},{7,5},{8,10},{9,11},{10,... | collective-permute-start | bytes 1032200 | tf_op jit(solution)/shard_map/ppermute | solution.py:781
  230.8 73.0 %collective-permute-start.5 = (bf16[7,32,768]{2,1,0:T(8,128)(2,1)}, bf16[7,32,768]{2,1,0:T(8,128)(2,1)S(1)}, u32[]{:S(2)}, u32[]{:S(2)}) collective-permute-start(bf16[7,32,768]{2,1,0:T(8,128)(2,1)} %get-tuple-element.111), channel_id=1, source_target_pairs={{0,3},{1,2},{2,1},{3,0},{4,7},{5,6},{6,5},{7,4},{8,11},{9,10},{10,... | collective-permute-start | bytes 1032200 | tf_op jit(solution)/shard_map/ppermute | solution.py:781
  352.1 10.5 collective-permute-start.6
  353.5 11.1 collective-permute-start.7
  354.1 17.1 %collective-permute-start.8 = (bf16[7,32,768]{2,1,0:T(8,128)(2,1)}, bf16[7,32,768]{2,1,0:T(8,128)(2,1)S(1)}, u32[]{:S(2)}, u32[]{:S(2)}) collective-permute-start(bf16[7,32,768]{2,1,0:T(8,128)(2,1)} %get-tuple-element.117), channel_id=1, source_target_pairs={{0,3},{1,2},{2,1},{3,0},{4,7},{5,6},{6,5},{7,4},{8,11},{9,10},{10,... | collective-permute-start | bytes 1032200 | tf_op jit(solution)/shard_map/ppermute | solution.py:781
  362.6 8.6 copy-start.23
  364.6 6.6 copy-start.25
  396.5 14.5 %collective-permute-start.9 = (bf16[7,32,768]{2,1,0:T(8,128)(2,1)}, bf16[7,32,768]{2,1,0:T(8,128)(2,1)S(1)}, u32[]{:S(2)}, u32[]{:S(2)}) collective-permute-start(bf16[7,32,768]{2,1,0:T(8,128)(2,1)} %get-tuple-element.119), channel_id=1, source_target_pairs={{0,1},{1,0},{2,3},{3,2},{4,5},{5,4},{6,7},{7,6},{8,9},{9,8},{10,11... | collective-permute-start | bytes 1032200 | tf_op jit(solution)/shard_map/ppermute | solution.py:781
  397.9 13.1 collective-permute-start.10
  398.5 9.7 copy-start.15
  398.6 9.7 copy-start.17
  398.6 9.7 copy-start.19
  398.6 9.7 copy-start.21
  398.6 15.9 %collective-permute-start.11 = (bf16[7,32,768]{2,1,0:T(8,128)(2,1)}, bf16[7,32,768]{2,1,0:T(8,128)(2,1)S(1)}, u32[]{:S(2)}, u32[]{:S(2)}) collective-permute-start(bf16[7,32,768]{2,1,0:T(8,128)(2,1)} %get-tuple-element.121), channel_id=1, source_target_pairs={{0,3},{1,2},{2,1},{3,0},{4,7},{5,6},{6,5},{7,4},{8,11},{9,10},{10,... | collective-permute-start | bytes 1032200 | tf_op jit(solution)/shard_map/ppermute | solution.py:781
  411.0 3.5 copy-start.52
  411.0 3.5 copy-start.53
  466.3 29.9 %collective-permute-start.12 = (bf16[7,32,768]{2,1,0:T(8,128)(2,1)}, bf16[7,32,768]{2,1,0:T(8,128)(2,1)S(1)}, u32[]{:S(2)}, u32[]{:S(2)}) collective-permute-start(bf16[7,32,768]{2,1,0:T(8,128)(2,1)} %get-tuple-element.127), channel_id=1, source_target_pairs={{0,1},{1,0},{2,3},{3,2},{4,5},{5,4},{6,7},{7,6},{8,9},{9,8},{10,11... | collective-permute-start | bytes 1032200 | tf_op jit(solution)/shard_map/ppermute | solution.py:781
  467.7 28.5 %collective-permute-start.13 = (bf16[7,32,768]{2,1,0:T(8,128)(2,1)}, bf16[7,32,768]{2,1,0:T(8,128)(2,1)S(1)}, u32[]{:S(2)}, u32[]{:S(2)}) collective-permute-start(bf16[7,32,768]{2,1,0:T(8,128)(2,1)} %get-tuple-element.128), channel_id=1, source_target_pairs={{0,2},{1,3},{2,0},{3,1},{4,6},{5,7},{6,4},{7,5},{8,10},{9,11},{10,... | collective-permute-start | bytes 1032200 | tf_op jit(solution)/shard_map/ppermute | solution.py:781
  468.3 27.9 %collective-permute-start.14 = (bf16[7,32,768]{2,1,0:T(8,128)(2,1)}, bf16[7,32,768]{2,1,0:T(8,128)(2,1)S(1)}, u32[]{:S(2)}, u32[]{:S(2)}) collective-permute-start(bf16[7,32,768]{2,1,0:T(8,128)(2,1)} %get-tuple-element.129), channel_id=1, source_target_pairs={{0,3},{1,2},{2,1},{3,0},{4,7},{5,6},{6,5},{7,4},{8,11},{9,10},{10,... | collective-permute-start | bytes 1032200 | tf_op jit(solution)/shard_map/ppermute | solution.py:781
  529.9 14.3 %collective-permute-start.15 = (bf16[7,32,768]{2,1,0:T(8,128)(2,1)}, bf16[7,32,768]{2,1,0:T(8,128)(2,1)S(1)}, u32[]{:S(2)}, u32[]{:S(2)}) collective-permute-start(bf16[7,32,768]{2,1,0:T(8,128)(2,1)} %get-tuple-element.132), channel_id=1, source_target_pairs={{0,1},{1,0},{2,3},{3,2},{4,5},{5,4},{6,7},{7,6},{8,9},{9,8},{10,11... | collective-permute-start | bytes 1032200 | tf_op jit(solution)/shard_map/ppermute | solution.py:781
  531.3 12.9 collective-permute-start.16
  531.9 13.9 %collective-permute-start.17 = (bf16[7,32,768]{2,1,0:T(8,128)(2,1)}, bf16[7,32,768]{2,1,0:T(8,128)(2,1)S(1)}, u32[]{:S(2)}, u32[]{:S(2)}) collective-permute-start(bf16[7,32,768]{2,1,0:T(8,128)(2,1)} %get-tuple-element.134), channel_id=1, source_target_pairs={{0,3},{1,2},{2,1},{3,0},{4,7},{5,6},{6,5},{7,4},{8,11},{9,10},{10,... | collective-permute-start | bytes 1032200 | tf_op jit(solution)/shard_map/ppermute | solution.py:781
  609.1 48.5 %collective-permute-start.18 = (bf16[7,32,768]{2,1,0:T(8,128)(2,1)}, bf16[7,32,768]{2,1,0:T(8,128)(2,1)}, u32[]{:S(2)}, u32[]{:S(2)}) collective-permute-start(bf16[7,32,768]{2,1,0:T(8,128)(2,1)} %get-tuple-element.143), channel_id=1, source_target_pairs={{0,1},{1,0},{2,3},{3,2},{4,5},{5,4},{6,7},{7,6},{8,9},{9,8},{10,11... | collective-permute-start | bytes 1032200 | tf_op jit(solution)/shard_map/ppermute | solution.py:781
  610.5 47.1 %collective-permute-start.19 = (bf16[7,32,768]{2,1,0:T(8,128)(2,1)}, bf16[7,32,768]{2,1,0:T(8,128)(2,1)}, u32[]{:S(2)}, u32[]{:S(2)}) collective-permute-start(bf16[7,32,768]{2,1,0:T(8,128)(2,1)} %get-tuple-element.144), channel_id=1, source_target_pairs={{0,2},{1,3},{2,0},{3,1},{4,6},{5,7},{6,4},{7,5},{8,10},{9,11},{10,... | collective-permute-start | bytes 1032200 | tf_op jit(solution)/shard_map/ppermute | solution.py:781
  611.1 46.5 %collective-permute-start.20 = (bf16[7,32,768]{2,1,0:T(8,128)(2,1)}, bf16[7,32,768]{2,1,0:T(8,128)(2,1)}, u32[]{:S(2)}, u32[]{:S(2)}) collective-permute-start(bf16[7,32,768]{2,1,0:T(8,128)(2,1)} %get-tuple-element.145), channel_id=1, source_target_pairs={{0,3},{1,2},{2,1},{3,0},{4,7},{5,6},{6,5},{7,4},{8,11},{9,10},{10,... | collective-permute-start | bytes 1032200 | tf_op jit(solution)/shard_map/ppermute | solution.py:781
  626.0 12.5 copy-start.1
  638.5 4.2 slice-start.2
  638.5 4.4 slice-start.3
  645.4 10.1 copy-start.32
  645.4 10.1 copy-start.37
  645.4 10.1 copy-start.42
  645.4 10.2 copy-start.41
  645.4 10.8 copy-start.40
  690.3 13.8 %collective-permute-start.21 = (bf16[7,32,768]{2,1,0:T(8,128)(2,1)}, bf16[7,32,768]{2,1,0:T(8,128)(2,1)S(1)}, u32[]{:S(2)}, u32[]{:S(2)}) collective-permute-start(bf16[7,32,768]{2,1,0:T(8,128)(2,1)} %get-tuple-element.148), channel_id=1, source_target_pairs={{0,1},{1,0},{2,3},{3,2},{4,5},{5,4},{6,7},{7,6},{8,9},{9,8},{10,11... | collective-permute-start | bytes 1032200 | tf_op jit(solution)/shard_map/ppermute | solution.py:781
  691.6 12.4 collective-permute-start.22
  692.3 11.8 collective-permute-start.23
  743.5 10.1 copy-start.45
  743.5 10.1 copy-start.48
  743.5 11.4 copy-start.44
  743.5 12.0 copy-start.43
  756.2 335.6 %reduce-scatter.5.cloned.1.call-start = ((), (), s32[]{:S(2)}) async-start(), calls=%async_computation.5 | async-start | bytes 19464192 | tf_op jit(solution)/shard_map/reduce_scatter | solution.py:885
  761.0 542.7 %reduce-scatter.3.cloned.1.call-start = ((), (), s32[]{:S(2)}) async-start(), calls=%async_computation.4 | async-start | bytes 19464192 | tf_op jit(solution)/shard_map/reduce_scatter | solution.py:885
  776.2 4.8 copy-start.2
  781.0 4.1 copy-start
  784.3 4.5 slice-start
  785.1 3.7 slice-start.1
  787.6 3.8 slice-start.4
  1303.7 2.7 copy-start.8
  1305.1 3.9 copy-start.36
  1305.1 4.5 copy-start.47
  (29 other events, 40.0 us)
Sparse Core Ops, SparseCore 0:
  11.5 127.3 all-gather.3
  142.4 151.6 all-gather.5
  756.3 122.5 all-reduce.4
  885.1 206.6 reduce-scatter.4
  1098.0 205.6 reduce-scatter.2

commit v3 on v2

v3 whole, which is shorter than its diff:
```python
import math

import functools

import jax
import jax.numpy as jnp
from jax import lax
from jax.experimental import pallas as pl
from jax.experimental.pallas import tpu as pltpu
from jax.sharding import PartitionSpec as P

D = 768
FF = 3072
HEADS = 12
FRAMES = 16
PATCHES = 196
ROWS_AXES = ("col", "dp", "row")
ALL_AXES = ("dp", "row", "col")
CLIP_AXES = ("row", "col")
HEAD = D // HEADS
PAIR = 2 * HEAD
SCALE = HEAD**-0.5
LAYER_EPS = 1e-06
NEG = -1e30

TILE = 8
FRAME_PAD = -(-PATCHES // 16) * 16
KEY_PAD = -(-PATCHES // 128) * 128
CHUNK = 512

BF = jnp.bfloat16
F32 = jnp.float32
HBM = pl.BlockSpec(memory_space=pltpu.HBM)
SMEM = pl.BlockSpec(memory_space=pltpu.SMEM)


def dot_nn(left, right):
    return lax.dot_general(left, right, (((1,), (0,)), ((), ())), preferred_element_type=F32)


def dot_nt(left, right):
    return lax.dot_general(left, right, (((1,), (1,)), ((), ())), preferred_element_type=F32)


def dot_tn(left, right):
    return lax.dot_general(left, right, (((0,), (0,)), ((), ())), preferred_element_type=F32)


def whole(shape):
    return pl.BlockSpec(shape, lambda *_: (0,) * len(shape))


def shaped(shape, dtype):
    return jax.ShapeDtypeStruct(shape, dtype)


def normalise(values):
    average = jnp.mean(values, axis=-1, keepdims=True)
    centred = values - average
    spread = jnp.mean(centred * centred, axis=-1, keepdims=True)
    inverse = lax.rsqrt(spread + LAYER_EPS)
    return centred * inverse, inverse


def norm_rows(values, gain, shift):
    normed, _ = normalise(values)
    return normed * gain + shift


def norm_rows_back(values, gain, dx, carry):
    normed, inverse = normalise(values)
    e = dx * gain
    first = jnp.mean(e, axis=-1, keepdims=True)
    second = jnp.mean(e * normed, axis=-1, keepdims=True)
    grad = carry + (e - first - normed * second) * inverse
    return (
        grad,
        jnp.sum(dx * normed, axis=0, keepdims=True),
        jnp.sum(dx, axis=0, keepdims=True),
    )


def gelu_parts(u):
    size = jnp.abs(u) * (0.5**0.5)
    t = pl.reciprocal(1.0 + 0.3275911 * size, approx=False)
    poly = 1.421413741 + t * (-1.453152027 + t * 1.061405429)
    poly = t * (0.254829592 + t * (-0.284496736 + t * poly))
    bell = jnp.exp(-size * size)
    tail = 0.5 * poly * bell
    cdf = jnp.where(u >= 0, 1.0 - tail, tail)
    return u * cdf, cdf + u * bell * 0.3989422804014327


def halves(value):
    lane = lax.broadcasted_iota(jnp.int32, value.shape, 1)
    zero = jnp.zeros_like(value)
    return jnp.where(lane < HEAD, value, zero), jnp.where(lane < HEAD, zero, value)


def soft(scores, valid):
    scores = jnp.where(valid, scores, NEG)
    top = jnp.max(scores, axis=-1, keepdims=True)
    raised = jnp.exp((scores - top) * SCALE)
    return raised * (1.0 / jnp.sum(raised, axis=-1, keepdims=True))


def split_all(values):
    return [half for value in values for half in halves(value)]


def attend_all(q, k, v, valid):
    keys, values = split_all(k), split_all(v)
    scores = [dot_nt(q[h // 2], keys[h]) for h in range(len(keys))]
    weights = [soft(s, valid).astype(BF) for s in scores]
    mixed = [dot_nn(w, value) for w, value in zip(weights, values)]
    return [(mixed[h] + mixed[h + 1]).astype(BF) for h in range(0, len(mixed), 2)]


def attend_all_back(q, k, v, dm, valid):
    queries, keys, values, grads = split_all(q), split_all(k), split_all(v), split_all(dm)
    heads = range(len(keys))
    scores = [dot_nt(q[h // 2], keys[h]) for h in heads]
    dps = [dot_nt(dm[h // 2], values[h]) for h in heads]
    weights = [soft(s, valid) for s in scores]
    ds = [
        (w * (dp - jnp.sum(dp * w, axis=-1, keepdims=True))).astype(BF)
        for w, dp in zip(weights, dps)
    ]
    weights = [w.astype(BF) for w in weights]
    result = []
    for h in range(0, len(keys), 2):
        dv = dot_tn(weights[h], grads[h]) + dot_tn(weights[h + 1], grads[h + 1])
        dq = dot_nn(ds[h], keys[h]) + dot_nn(ds[h + 1], keys[h + 1])
        dk = dot_tn(ds[h], queries[h]) + dot_tn(ds[h + 1], queries[h + 1])
        result.append(((dq * SCALE).astype(BF), (dk * SCALE).astype(BF), dv.astype(BF)))
    return result


def pair_columns(z):
    for c in range(z.cols):
        for pair in range(z.half // PAIR):
            at = c * z.half + pair * PAIR
            starts = [(3 * c + t) * z.half + pair * PAIR for t in range(3)] + [at]
            yield [slice(start, start + PAIR) for start in starts]


def frame_valid():
    return lax.broadcasted_iota(jnp.int32, (FRAME_PAD, KEY_PAD), 1) < PATCHES


def patch_valid(rows):
    key = lax.broadcasted_iota(jnp.int32, (rows, rows), 1)
    query = lax.broadcasted_iota(jnp.int32, (rows, rows), 0)
    return (key % TILE) == (query % TILE)


def key_rows(value):
    return jnp.concatenate([value, jnp.zeros((KEY_PAD - FRAME_PAD, value.shape[1]), value.dtype)], 0)


class Weight:
    def __init__(self, packed, at, width):
        self.arrays = [packed]
        self.at = at
        self.width = width

    def scratch(self):
        return pltpu.VMEM((self.arrays[0].shape[0], D, self.width), BF)

    def step(self, size):
        per, first = self.width // size, self.at // size
        return pl.BlockSpec((1, D, size), lambda i: (i // per, 0, first + i % per))

    def copies(self, refs, target, sem):
        window = refs[0].at[:, :, pl.ds(self.at, self.width)]
        return [pltpu.make_async_copy(window, target, sem)]


def start_all(copies):
    for copy in copies:
        copy.start()


def wait_all(copies):
    for copy in copies:
        copy.wait()


class Sizes:
    def __init__(self, tokens, block, depth, row_count, cols):
        self.members = FRAMES * PATCHES // tokens
        self.frames = FRAMES // self.members
        self.groups = -(-PATCHES // (self.members * TILE))
        self.share = self.groups * TILE
        self.span = self.members * self.share
        self.piece = self.frames * TILE
        self.group_rows = self.members * self.piece
        self.rows = self.frames * FRAME_PAD
        self.patch_rows = self.groups * self.group_rows
        self.cols = cols
        self.half = D // cols
        self.units = FF // cols
        self.block = block
        self.depth = depth
        self.direct = block % 16 == 0 and cols == 2 and row_count == 2 and depth >= 2


def send_pieces(z, place_ref, spread_ref, piece_refs):
    for apart in range(z.members):
        start = (place_ref[0] ^ apart) * z.share
        for g in range(z.groups):
            parts = [
                spread_ref[pl.ds(pl.multiple_of(f * z.span + start + g * TILE, TILE), TILE), :]
                for f in range(z.frames)
            ]
            piece_refs[apart][g] = jnp.concatenate(parts, 0).astype(BF)


def take_pieces(z, place_ref, spread_ref, apart, rows):
    start = (place_ref[0] ^ apart) * z.share
    for g in range(z.groups):
        for f in range(z.frames):
            at = g * z.piece + f * TILE
            spread_ref[pl.ds(pl.multiple_of(f * z.span + start + g * TILE, TILE), TILE), :] = rows[
                at : at + TILE
            ]


def gather_groups(z, piece_refs, rows_ref):
    for g in range(z.groups):
        for m in range(z.members):
            at = g * z.group_rows + m * z.piece
            rows_ref[at : at + z.piece, :] = piece_refs[m][g]


def vmem_bytes(specs, arrays, scratch):
    total = 16 * 2**20
    for spec, array in zip(specs, arrays):
        if spec.block_shape is not None:
            total += 2 * math.prod(spec.block_shape) * array.dtype.itemsize
    for held in scratch:
        if held.memory_space == pltpu.VMEM:
            total += math.prod(held.shape) * jnp.dtype(held.dtype).itemsize
    return min(total, 58 * 2**20)


def call(body, name, grid, in_specs, out_specs, out_shape, scratch, args, flops):
    limit = vmem_bytes([*in_specs, *out_specs], [*args, *out_shape], scratch)
    moved = sum(a.size * a.dtype.itemsize for a in args) + sum(
        s.size * s.dtype.itemsize for s in out_shape
    )
    return pl.pallas_call(
        body,
        name=name,
        grid=grid,
        in_specs=in_specs,
        out_specs=out_specs,
        out_shape=out_shape,
        scratch_shapes=scratch,
        compiler_params=pltpu.CompilerParams(
            vmem_limit_bytes=limit, dimension_semantics=("arbitrary",) * len(grid)
        ),
        cost_estimate=pl.CostEstimate(flops=int(flops), bytes_accessed=int(moved), transcendentals=0),
    )(*args)


def spatial_forward(z, place, hidden, wq, wo, bias, out_bias, gains, shifts):
    wide = 3 * z.half

    def body(place_ref, h_ref, *refs):
        wq_refs, refs = refs[: len(wq.arrays)], refs[len(wq.arrays) :]
        wo_refs, refs = refs[: len(wo.arrays)], refs[len(wo.arrays) :]
        bias_ref, ob_ref, gain_ref, shift_ref, *refs = refs
        x_ref, qkv_ref, mixed_ref, h1_ref, *refs = refs
        piece_refs, refs = refs[: z.members], refs[z.members :]
        wq_s, wo_s, qkv_s, mixed_s, spread, sem = refs
        f = pl.program_id(0)

        @pl.when(f == 0)
        def _():
            first = wq.copies(wq_refs, wq_s, sem.at[0])
            later = wo.copies(wo_refs, wo_s, sem.at[1])
            start_all(first)
            start_all(later)
            for at in range(z.frames):
                x_ref[at] = norm_rows(h_ref[at], gain_ref[0:1], shift_ref[0:1]).astype(BF)
            spread[...] = jnp.zeros_like(spread)
            wait_all(first)
            x = x_ref[...].reshape(z.rows, D)
            for c in range(z.cols):
                out = dot_nn(x, wq_s[c]) + bias_ref[c]
                qkv_s[:, c * wide : (c + 1) * wide] = out.astype(BF)
            wait_all(later)

        rows = pl.ds(pl.multiple_of(f * FRAME_PAD, 16), FRAME_PAD)
        q, k, v = [[qkv_s[rows, at[t]] for at in pair_columns(z)] for t in range(3)]
        mixed = attend_all(q, [key_rows(x) for x in k], [key_rows(x) for x in v], frame_valid())
        qkv_ref[0] = qkv_s[rows, :]
        for at, value in zip(pair_columns(z), mixed):
            mixed_s[rows, at[3]] = value

        @pl.when(f == z.frames - 1)
        def _():
            branch = ob_ref[0:1]
            for c in range(z.cols):
                branch = branch + dot_nt(mixed_s[:, c * z.half : (c + 1) * z.half], wo_s[c])
            mixed_ref[...] = mixed_s[...].reshape(mixed_ref.shape)
            for at in range(z.frames):
                h1 = h_ref[at] + branch[at * FRAME_PAD : (at + 1) * FRAME_PAD]
                h1_ref[at] = h1
                spread[at * z.span : at * z.span + FRAME_PAD, :] = norm_rows(
                    h1, gain_ref[1:2], shift_ref[1:2]
                )
            send_pieces(z, place_ref, spread, piece_refs)

    frame = (z.frames, FRAME_PAD, D)
    piece = (z.groups, z.piece, D)
    return call(
        body,
        "spatial_forward",
        (z.frames,),
        [SMEM, whole(frame)]
        + [HBM] * (len(wq.arrays) + len(wo.arrays))
        + [whole(bias.shape), whole(out_bias.shape), whole(gains.shape), whole(shifts.shape)],
        [
            whole(frame),
            pl.BlockSpec((1, FRAME_PAD, 3 * D), lambda f: (f, 0, 0)),
            whole(frame),
            whole(frame),
        ]
        + [whole(piece)] * z.members,
        [
            shaped(frame, BF),
            shaped((z.frames, FRAME_PAD, 3 * D), BF),
            shaped(frame, BF),
            shaped(frame, F32),
        ]
        + [shaped(piece, BF)] * z.members,
        [
            wq.scratch(),
            wo.scratch(),
            pltpu.VMEM((z.rows, 3 * D), BF),
            pltpu.VMEM((z.rows, D), BF),
            pltpu.VMEM((z.frames * z.span, D), F32),
            pltpu.SemaphoreType.DMA((2,)),
        ],
        (place, hidden, *wq.arrays, *wo.arrays, bias, out_bias, gains, shifts),
        2 * z.rows * D * (4 * D + 2 * KEY_PAD),
    )


def temporal_forward(z, pieces, wq, bias):
    wide = 3 * z.half
    n = z.group_rows

    def body(*refs):
        in_refs, refs = refs[: z.members], refs[z.members :]
        wq_refs, refs = refs[: len(wq.arrays)], refs[len(wq.arrays) :]
        bias_ref, qkv_ref, *refs = refs
        out_refs, refs = refs[: z.members], refs[z.members :]
        wq_s, x_s, qkv_s, sem = refs
        g = pl.program_id(0)

        @pl.when(g == 0)
        def _():
            copies = wq.copies(wq_refs, wq_s, sem.at[0])
            start_all(copies)
            gather_groups(z, in_refs, x_s)
            wait_all(copies)
            x = x_s[...]
            for c in range(z.cols):
                out = dot_nn(x, wq_s[c]) + bias_ref[c]
                qkv_s[:, c * wide : (c + 1) * wide] = out.astype(BF)

        rows = pl.ds(pl.multiple_of(g * n, n), n)
        q, k, v = [[qkv_s[rows, at[t]] for at in pair_columns(z)] for t in range(3)]
        mixed = attend_all(q, k, v, patch_valid(n))
        qkv_ref[0] = qkv_s[rows, :]
        for at, value in zip(pair_columns(z), mixed):
            for m in range(z.members):
                out_refs[m][0, :, at[3]] = value[m * z.piece : (m + 1) * z.piece]

    piece = (z.groups, z.piece, D)
    step = pl.BlockSpec((1, z.piece, D), lambda g: (g, 0, 0))
    return call(
        body,
        "temporal_forward",
        (z.groups,),
        [whole(piece)] * z.members + [HBM] * len(wq.arrays) + [whole(bias.shape)],
        [pl.BlockSpec((1, n, 3 * D), lambda g: (g, 0, 0))] + [step] * z.members,
        [shaped((z.groups, n, 3 * D), BF)] + [shaped(piece, BF)] * z.members,
        [
            wq.scratch(),
            pltpu.VMEM((z.patch_rows, D), BF),
            pltpu.VMEM((z.patch_rows, 3 * D), BF),
            pltpu.SemaphoreType.DMA((1,)),
        ],
        (*pieces, *wq.arrays, bias),
        2 * z.patch_rows * D * (3 * D + 2 * n),
    )


def hidden_forward(z, place, pieces, hidden, wo, wu, wd, out_bias, up_bias, down_bias, gains, shifts):
    steps = FF // CHUNK

    def body(place_ref, *refs):
        in_refs, refs = refs[: z.members], refs[z.members :]
        h1_ref, *refs = refs
        wo_refs, refs = refs[: len(wo.arrays)], refs[len(wo.arrays) :]
        up_ref, down_ref, ob_ref, ub_ref, db_ref, gain_ref, shift_ref, *refs = refs
        h2_ref, x_ref, act_ref, slope_ref, h3_ref, *refs = refs
        wo_s, spread, sem = refs
        i = pl.program_id(0)

        @pl.when(i == 0)
        def _():
            first = wo.copies(wo_refs, wo_s, sem.at[0])
            start_all(first)
            wait_all(first)
            for m in range(z.members):
                mixed = in_refs[m][...].reshape(z.groups * z.piece, D)
                branch = 0.0
                for c in range(z.cols):
                    branch = branch + dot_nt(mixed[:, c * z.half : (c + 1) * z.half], wo_s[c])
                take_pieces(z, place_ref, spread, m, branch)
            for f in range(z.frames):
                rows = slice(f * FRAME_PAD, (f + 1) * FRAME_PAD)
                h2 = h1_ref[f] + spread[f * z.span : f * z.span + FRAME_PAD, :] + ob_ref[1:2]
                h2_ref[f] = h2
                x_ref[rows, :] = norm_rows(h2, gain_ref[2:3], shift_ref[2:3]).astype(BF)
                h3_ref[f] = h2 + db_ref[...]

        up, down, bias = up_ref[0], down_ref[0], ub_ref[...]
        blocks = [slice(f * FRAME_PAD, (f + 1) * FRAME_PAD) for f in range(z.frames)]
        inner = dot_nn(x_ref[blocks[0], :], up) + bias
        results = []
        for f in range(z.frames):
            later = dot_nn(x_ref[blocks[f + 1], :], up) + bias if f + 1 < z.frames else None
            act, slope = gelu_parts(inner)
            act = act.astype(BF)
            results.append((act, slope, dot_nt(act, down)))
            inner = later
        for f, (act, slope, out) in enumerate(results):
            act_ref[blocks[f], :] = act
            slope_ref[blocks[f], :] = slope
            h3_ref[f] += out

    frame = (z.frames, FRAME_PAD, D)
    piece = (z.groups, z.piece, D)
    step = pl.BlockSpec((z.rows, CHUNK), lambda i: (0, i))
    return call(
        body,
        "hidden_forward",
        (steps,),
        [SMEM]
        + [whole(piece)] * z.members
        + [whole(frame)]
        + [HBM] * len(wo.arrays)
        + [
            wu.step(CHUNK),
            wd.step(CHUNK),
            whole(out_bias.shape),
            pl.BlockSpec((1, CHUNK), lambda i: (0, i)),
            whole(down_bias.shape),
            whole(gains.shape),
            whole(shifts.shape),
        ],
        [whole(frame), whole((z.rows, D)), step, step, whole(frame)],
        [
            shaped(frame, F32),
            shaped((z.rows, D), BF),
            shaped((z.rows, FF), BF),
            shaped((z.rows, FF), F32),
            shaped(frame, F32),
        ],
        [
            wo.scratch(),
            pltpu.VMEM((z.frames * z.span, D), F32),
            pltpu.SemaphoreType.DMA((1,)),
        ],
        (place, *pieces, hidden, *wo.arrays, *wu.arrays, *wd.arrays, out_bias, up_bias, down_bias, gains, shifts),
        2 * z.rows * D * (D + 2 * FF),
    )


def hidden_backward(z, place, grad, h2, slope, wu, wd, gains):
    steps = FF // CHUNK

    def body(place_ref, g_ref, h2_ref, slope_ref, *refs):
        up_ref, down_ref, gain_ref, di_ref, gb_ref, g2_ref, sums_ref, *refs = refs
        piece_refs, refs = refs[: z.members], refs[z.members :]
        dx_s, spread = refs
        i = pl.program_id(0)

        @pl.when(i == 0)
        def _():
            total = 0.0
            for f in range(z.frames):
                rows = slice(f * FRAME_PAD, (f + 1) * FRAME_PAD)
                g = g_ref[f]
                gb_ref[rows, :] = g.astype(BF)
                total = total + jnp.sum(g, axis=0, keepdims=True)
            sums_ref[0:1] = total
            dx_s[...] = jnp.zeros_like(dx_s)
            spread[...] = jnp.zeros_like(spread)

        up, down = up_ref[0], down_ref[0]
        blocks = [slice(f * FRAME_PAD, (f + 1) * FRAME_PAD) for f in range(z.frames)]
        products = [dot_nn(gb_ref[rows, :], down) for rows in blocks]
        inner = [(p * slope_ref[rows, :]).astype(BF) for p, rows in zip(products, blocks)]
        outs = [dot_nt(di, up) for di in inner]
        for rows, di, out in zip(blocks, inner, outs):
            di_ref[rows, :] = di
            dx_s[rows, :] += out

        @pl.when(i == steps - 1)
        def _():
            out_b = gain_g = shift_g = 0.0
            for f in range(z.frames):
                rows = slice(f * FRAME_PAD, (f + 1) * FRAME_PAD)
                g2, gg, sg = norm_rows_back(h2_ref[f], gain_ref[2:3], dx_s[rows, :], g_ref[f])
                g2_ref[f] = g2
                spread[f * z.span : f * z.span + FRAME_PAD, :] = g2
                gain_g, shift_g = gain_g + gg, shift_g + sg
                out_b = out_b + jnp.sum(g2, axis=0, keepdims=True)
            sums_ref[1:2] = gain_g
            sums_ref[2:3] = shift_g
            sums_ref[3:4] = out_b
            send_pieces(z, place_ref, spread, piece_refs)

    frame = (z.frames, FRAME_PAD, D)
    piece = (z.groups, z.piece, D)
    step = pl.BlockSpec((z.rows, CHUNK), lambda i: (0, i))
    return call(
        body,
        "hidden_backward",
        (steps,),
        [SMEM, whole(frame), whole(frame), step]
        + [wu.step(CHUNK), wd.step(CHUNK), whole(gains.shape)],
        [step, whole((z.rows, D)), whole(frame), whole((4, D))] + [whole(piece)] * z.members,
        [
            shaped((z.rows, FF), BF),
            shaped((z.rows, D), BF),
            shaped(frame, F32),
            shaped((4, D), F32),
        ]
        + [shaped(piece, BF)] * z.members,
        [
            pltpu.VMEM((z.rows, D), F32),
            pltpu.VMEM((z.frames * z.span, D), F32),
        ],
        (place, grad, h2, slope, *wu.arrays, *wd.arrays, gains),
        2 * z.rows * D * 2 * FF,
    )


def temporal_backward(z, grad_pieces, qkv, wq, wo):
    wide = 3 * z.half
    n = z.group_rows

    def body(*refs):
        in_refs, refs = refs[: z.members], refs[z.members :]
        qkv_ref, *refs = refs
        wq_refs, refs = refs[: len(wq.arrays)], refs[len(wq.arrays) :]
        wo_refs, refs = refs[: len(wo.arrays)], refs[len(wo.arrays) :]
        d_ref, *refs = refs
        out_refs, refs = refs[: z.members], refs[z.members :]
        wq_s, wo_s, gb_s, dm_s, d_s, sem = refs
        g = pl.program_id(0)

        @pl.when(g == 0)
        def _():
            first = wo.copies(wo_refs, wo_s, sem.at[0])
            start_all(first)
            start_all(wq.copies(wq_refs, wq_s, sem.at[1]))
            gather_groups(z, in_refs, gb_s)
            wait_all(first)
            gb = gb_s[...]
            for c in range(z.cols):
                dm_s[:, c * z.half : (c + 1) * z.half] = dot_nn(gb, wo_s[c]).astype(BF)

        rows = pl.ds(pl.multiple_of(g * n, n), n)
        q, k, v = [[qkv_ref[0, :, at[t]] for at in pair_columns(z)] for t in range(3)]
        dm = [dm_s[rows, at[3]] for at in pair_columns(z)]
        grads = attend_all_back(q, k, v, dm, patch_valid(n))
        for at, values in zip(pair_columns(z), grads):
            for t in range(3):
                d_s[rows, at[t]] = values[t]
        d_ref[...] = d_s[rows, :]

        @pl.when(g == z.groups - 1)
        def _():
            wait_all(wq.copies(wq_refs, wq_s, sem.at[1]))
            dx = 0.0
            for c in range(z.cols):
                dx = dx + dot_nt(d_s[:, c * wide : (c + 1) * wide], wq_s[c])
            dx = dx.astype(BF)
            for gg in range(z.groups):
                for m in range(z.members):
                    at = gg * n + m * z.piece
                    out_refs[m][gg] = dx[at : at + z.piece]

    piece = (z.groups, z.piece, D)
    return call(
        body,
        "temporal_backward",
        (z.groups,),
        [whole(piece)] * z.members
        + [pl.BlockSpec((1, n, 3 * D), lambda g: (g, 0, 0))]
        + [HBM] * (len(wq.arrays) + len(wo.arrays)),
        [pl.BlockSpec((n, 3 * D), lambda g: (g, 0))] + [whole(piece)] * z.members,
        [shaped((z.patch_rows, 3 * D), BF)] + [shaped(piece, BF)] * z.members,
        [
            wq.scratch(),
            wo.scratch(),
            pltpu.VMEM((z.patch_rows, D), BF),
            pltpu.VMEM((z.patch_rows, D), BF),
            pltpu.VMEM((z.patch_rows, 3 * D), BF),
            pltpu.SemaphoreType.DMA((2,)),
        ],
        (*grad_pieces, qkv, *wq.arrays, *wo.arrays),
        2 * z.patch_rows * D * (4 * D + 5 * n),
    )


def spatial_backward(z, place, dx_pieces, grad, h1, qkv, wo, gains):
    wide = 3 * z.half

    def body(place_ref, *refs):
        in_refs, refs = refs[: z.members], refs[z.members :]
        g_ref, h1_ref, qkv_ref, *refs = refs
        wo_refs, refs = refs[: len(wo.arrays)], refs[len(wo.arrays) :]
        gain_ref, gb_ref, d_ref, g1_ref, sums_ref, *refs = refs
        wo_s, spread, dm_s, sem = refs
        f = pl.program_id(0)

        @pl.when(f == 0)
        def _():
            first = wo.copies(wo_refs, wo_s, sem.at[0])
            start_all(first)
            for m in range(z.members):
                rows = in_refs[m][...].reshape(z.groups * z.piece, D).astype(F32)
                take_pieces(z, place_ref, spread, m, rows)
            out_b = gain_g = shift_g = 0.0
            for at in range(z.frames):
                rows = slice(at * FRAME_PAD, (at + 1) * FRAME_PAD)
                dx = spread[at * z.span : at * z.span + FRAME_PAD, :]
                g1, gg, sg = norm_rows_back(h1_ref[at], gain_ref[1:2], dx, g_ref[at])
                g1_ref[at] = g1
                gb_ref[rows, :] = g1.astype(BF)
                gain_g, shift_g = gain_g + gg, shift_g + sg
                out_b = out_b + jnp.sum(g1, axis=0, keepdims=True)
            sums_ref[0:1] = gain_g
            sums_ref[1:2] = shift_g
            sums_ref[2:3] = out_b
            wait_all(first)
            gb = gb_ref[...]
            for c in range(z.cols):
                dm_s[:, c * z.half : (c + 1) * z.half] = dot_nn(gb, wo_s[c]).astype(BF)

        rows = pl.ds(pl.multiple_of(f * FRAME_PAD, 16), FRAME_PAD)
        q, k, v = [[qkv_ref[0, :, at[t]] for at in pair_columns(z)] for t in range(3)]
        dm = [dm_s[rows, at[3]] for at in pair_columns(z)]
        grads = attend_all_back(
            q, [key_rows(x) for x in k], [key_rows(x) for x in v], dm, frame_valid()
        )
        for at, values in zip(pair_columns(z), grads):
            for t in range(3):
                d_ref[:, at[t]] = values[t][:FRAME_PAD]

    frame = (z.frames, FRAME_PAD, D)
    piece = (z.groups, z.piece, D)
    return call(
        body,
        "spatial_backward",
        (z.frames,),
        [SMEM]
        + [whole(piece)] * z.members
        + [whole(frame), whole(frame), pl.BlockSpec((1, FRAME_PAD, 3 * D), lambda f: (f, 0, 0))]
        + [HBM] * len(wo.arrays)
        + [whole(gains.shape)],
        [
            whole((z.rows, D)),
            pl.BlockSpec((FRAME_PAD, 3 * D), lambda f: (f, 0)),
            whole(frame),
            whole((3, D)),
        ],
        [
            shaped((z.rows, D), BF),
            shaped((z.rows, 3 * D), BF),
            shaped(frame, F32),
            shaped((3, D), F32),
        ],
        [
            wo.scratch(),
            pltpu.VMEM((z.frames * z.span, D), F32),
            pltpu.VMEM((z.rows, D), BF),
            pltpu.SemaphoreType.DMA((1,)),
        ],
        (place, *dx_pieces, grad, h1, qkv, *wo.arrays, gains),
        2 * z.rows * D * (D + 5 * KEY_PAD),
    )


def input_backward(z, d, grad, hidden, wq, gains):
    wide = 3 * z.half

    def body(d_ref, g_ref, h_ref, *refs):
        wq_refs, refs = refs[: len(wq.arrays)], refs[len(wq.arrays) :]
        gain_ref, g0_ref, sums_ref, wq_s, sem = refs
        f = pl.program_id(0)

        @pl.when(f == 0)
        def _():
            copies = wq.copies(wq_refs, wq_s, sem.at[0])
            start_all(copies)
            wait_all(copies)
            sums_ref[...] = jnp.zeros_like(sums_ref)

        dx = 0.0
        for c in range(z.cols):
            dx = dx + dot_nt(d_ref[:, c * wide : (c + 1) * wide], wq_s[c])
        for at in range(2):
            rows = slice(at * FRAME_PAD, (at + 1) * FRAME_PAD)
            g0, gg, sg = norm_rows_back(h_ref[at], gain_ref[0:1], dx[rows], g_ref[at])
            g0_ref[at] = g0
            sums_ref[0:1] += gg
            sums_ref[1:2] += sg

    frame = (z.frames, FRAME_PAD, D)
    step = pl.BlockSpec((2, FRAME_PAD, D), lambda f: (f, 0, 0))
    return call(
        body,
        "input_backward",
        (z.frames // 2,),
        [pl.BlockSpec((2 * FRAME_PAD, 3 * D), lambda f: (f, 0)), step, step]
        + [HBM] * len(wq.arrays)
        + [whole(gains.shape)],
        [step, whole((2, D))],
        [shaped(frame, F32), shaped((2, D), F32)],
        [wq.scratch(), pltpu.SemaphoreType.DMA((1,))],
        (d, grad, hidden, *wq.arrays, gains),
        2 * z.rows * D * 3 * D,
    )


def weight_grads(z, place, name, jobs, direct, room=0, into=None, start_at=0):
    halves_ = [job[1][0].shape[-1] // z.cols for job in jobs]
    width = sum(halves_)
    even = len(set(halves_)) == 1
    starts = [sum(halves_[:k]) for k in range(len(jobs))]
    total = jobs[0][1][0].shape[-1]
    rows = [sum(a.shape[0] for a in job[0]) for job in jobs]
    outs = 2 if direct else 1

    def joined(refs):
        parts = [r[...] for r in refs]
        return parts[0] if len(parts) == 1 else jnp.concatenate(parts, 0)

    def body(place_ref, *refs):
        lefts, rights = [], []
        refs = refs[0 if into is None else 1 :]
        for left, right in jobs:
            lefts.append(refs[: len(left)])
            rights.append(refs[len(left) : len(left) + len(right)])
            refs = refs[len(left) + len(right) :]
        out_refs, sums_ref, turned = refs[:outs], refs[outs], refs[outs + 1 :]
        r, i = pl.program_id(0), pl.program_id(1)

        for k in range(len(jobs)):

            @pl.when(i == k)
            def _(k=k):
                @pl.when(r == 0)
                def _():
                    turned[k][...] = joined(lefts[k]).T

                value = joined(rights[k])
                if k == 0:
                    sums_ref[...] = jnp.sum(value.astype(F32), axis=0, keepdims=True)
                out = dot_nn(turned[k][...], value).astype(BF)
                start = 0 if even else starts[k]
                cut = slice(start, start + halves_[k])
                if not direct:
                    out_refs[0][0, :, cut] = out
                    return
                core = place_ref[3]
                for zz in range(z.depth):
                    for xx in range(2):
                        at = [z.block * ((zz * 2 + cc) * 2 + xx) for cc in range(2)]
                        first, second = [out[a : a + z.block] for a in at]
                        x, depth = xx ^ place_ref[1], zz ^ place_ref[4]
                        out_refs[0][0, x, depth, :, cut] = jnp.where(core == 0, first, second)
                        out_refs[1][0, x, depth, :, cut] = jnp.where(core == 0, second, first)

    def right_spec(k, a):
        def index(r, i, place_ref):
            return (0, r ^ place_ref[2] if direct else r)

        return pl.BlockSpec((a.shape[0], halves_[k]), index)

    in_specs, args = ([], []) if into is None else ([HBM], [into])
    for k, (left, right) in enumerate(jobs):
        in_specs += [whole(a.shape) for a in left] + [right_spec(k, a) for a in right]
        args += [*left, *right]
    block = halves_[0] if even else width
    first = start_at // block
    if direct:
        part = (2, z.depth, z.block)
        out_specs = [
            pl.BlockSpec((1,) + part + (block,), lambda r, i, p: (r, 0, 0, 0, i if even else 0))
        ] * 2
        out_shape = [shaped((z.cols,) + part + (width,), BF)] * 2
    else:
        out_specs = [pl.BlockSpec((1, D, block), lambda r, i, p: (r, 0, first + (i if even else 0)))]
        out_shape = [shaped((z.cols, D, width + room) if into is None else into.shape, BF)]
    out_specs.append(right_spec(0, shaped((1, total), F32)))
    out_shape.append(shaped((1, total), F32))
    flops = sum(2 * n * D * h * z.cols for n, h in zip(rows, halves_))
    moved = sum(a.size * a.dtype.itemsize for a in args + out_shape)
    scratch = [pltpu.VMEM((D, n), BF) for n in rows]
    limit = vmem_bytes([*in_specs, *out_specs], [*args, *out_shape], scratch)
    *parts, sums = pl.pallas_call(
        body,
        name=name,
        grid_spec=pltpu.PrefetchScalarGridSpec(
            num_scalar_prefetch=1,
            grid=(z.cols, len(jobs)),
            in_specs=in_specs,
            out_specs=out_specs,
            scratch_shapes=scratch,
        ),
        out_shape=out_shape,
        input_output_aliases={} if into is None else {1: 0},
        compiler_params=pltpu.CompilerParams(
            vmem_limit_bytes=limit, dimension_semantics=("arbitrary",) * 2
        ),
        cost_estimate=pl.CostEstimate(flops=int(flops), bytes_accessed=int(moved), transcendentals=0),
    )(place, *args)
    return parts, sums


def swap(value, axis, apart):
    pairs = [(at, at ^ apart) for at in range(lax.axis_size(axis))]
    return lax.ppermute(value, axis, pairs)


def add_terms(terms):
    total = terms[0].astype(F32)
    for term in terms[1:]:
        total = total + term.astype(F32)
    return total


def add_low(terms):
    return add_terms(terms).astype(BF)


def reduce_whole(z, part):
    flat_rows = part.reshape(z.cols * D, -1)
    own = lax.psum_scatter(flat_rows, ROWS_AXES, scatter_dimension=0, tiled=True)
    return own.astype(F32)


def reduce_steps(z, keep, send):
    (got,) = yield [(send, "dp", 1)]
    terms = [keep, got]
    half = z.depth // 2

    def of(*at):
        return [term[at] for term in terms]

    low, high = slice(0, half), slice(half, None)
    over_x, over_y = yield [
        (add_low(of(slice(None), 1, low)), "row", 1),
        (add_low(of(1, slice(None), high)), "col", 1),
    ]
    x_high, y_low = yield [
        (add_low(of(0, 1, high) + [over_y[1]]), "row", 1),
        (add_low(of(1, 0, low) + [over_x[1]]), "col", 1),
    ]
    lows = of(0, 0, low) + [over_x[0], y_low]
    highs = of(0, 0, high) + [x_high, over_y[0]]
    apart = z.depth
    while True:
        (got,) = yield [(add_low(highs), "dp", apart)]
        lows = lows + [got]
        if half == 1:
            return add_terms([term[0] for term in lows])
        half //= 2
        apart //= 2
        highs = [term[half:] for term in lows]
        lows = [term[:half] for term in lows]


class Mover:
    def __init__(self):
        self.flying = []

    def launch(self, value, started):
        moves = [list(next_moves) for _, next_moves, _ in started]
        operands = [[move[0] for move in group] for group in moves]
        value, operands = lax.optimization_barrier((value, operands))
        for (steps, _, done), group, held in zip(started, moves, operands):
            arrived = [swap(v, axis, apart) for v, (_, axis, apart) in zip(held, group)]
            self.flying.append((steps, arrived, done))
        return value

    def add(self, value, steps, done):
        return self.launch(value, [(steps, next(steps), done)])

    def tick(self, value):
        flying, self.flying = self.flying, []
        if not flying:
            return value
        value, landed = lax.optimization_barrier((value, [f[1] for f in flying]))
        started = []
        for (steps, _, done), arrived in zip(flying, landed):
            try:
                started.append((steps, steps.send(arrived), done))
            except StopIteration as stop:
                done(stop.value)
        return self.launch(value, started) if started else value


def sum_everywhere(value):
    for axis in ALL_AXES:
        apart = 1
        while apart < lax.axis_size(axis):
            value = value + swap(value, axis, apart)
            apart *= 2
    return value


def clip_swap(value, apart):
    count = lax.axis_size("row") * lax.axis_size("col")
    return lax.ppermute(value, CLIP_AXES, [(at, at ^ apart) for at in range(count)])


def swap_pieces(pieces):
    return [pieces[0]] + [clip_swap(pieces[apart], apart) for apart in range(1, len(pieces))]


def flat(pieces):
    return [p.reshape(-1, D) for p in pieces]


def pad_frames(z, rows):
    grid = rows.reshape(z.frames, PATCHES, D)
    return jnp.pad(grid, ((0, 0), (0, FRAME_PAD - PATCHES), (0, 0)))


def cut_frames(z, grid):
    return grid[:, :PATCHES].reshape(z.frames * PATCHES, D)


def layer_forward(z, place, hidden, w, small):
    gains, shifts, bias_qkv, bias_out, bias_up, bias_down = small
    x0, qkv0, mixed0, h1, *send = spatial_forward(
        z, place, hidden, w["qkv0"], w["out0"], bias_qkv[0], bias_out, gains, shifts
    )
    pieces = swap_pieces(send)
    qkv1, *back = temporal_forward(z, pieces, w["qkv1"], bias_qkv[1])
    mixed1 = swap_pieces(back)
    h2, x2, act, slope, h3 = hidden_forward(
        z, place, mixed1, h1, w["out1"], w["up"], w["down"], bias_out, bias_up, bias_down, gains, shifts
    )
    return h3, (hidden, x0, qkv0, mixed0, h1, pieces, qkv1, mixed1, h2, x2, act, slope)


def group_rows(z, pieces):
    stacked = jnp.stack(pieces, axis=1)
    return stacked.reshape(z.patch_rows, D)


def partial_set(owned, name):
    return lambda value: owned.__setitem__(name, value)


def after(value, other):
    return lax.optimization_barrier((value, other))[0]


def layer_backward(z, place, grad, record, w, small, owned, mover, direct, carry):
    gains, *_ = small
    hidden, x0, qkv0, mixed0, h1, pieces, qkv1, mixed1, h2, x2, act, slope = record
    di, gb, g2, sums_h, *send = hidden_backward(z, place, grad, h2, slope, w["up"], w["down"], gains)
    got = swap_pieces(send)
    jobs = [([x2], [di]), ([gb], [act])]
    part = 4 * z.half
    if carry is None:
        parts, up_b = weight_grads(z, place, "hidden_grads", jobs, False)
        owned["hidden"] = reduce_whole(z, parts[0])
    else:
        parts, up_b = weight_grads(
            z, place, "hidden_grads", jobs, False, into=carry[0], start_at=2 * part
        )
        whole_rows = reduce_whole(z, parts[0])
        carry[1]["temporal"] = whole_rows[:, :part]
        carry[1]["spatial"] = whole_rows[:, part : 2 * part]
        owned["hidden"] = whole_rows[:, 2 * part :]
    got[0] = after(got[0], up_b)
    d1, *back = temporal_backward(z, got, qkv1, w["qkv1"], w["out1"])
    dx = swap_pieces(back)
    jobs = [([group_rows(z, pieces)], [d1]), (flat(send), flat(mixed1))]
    room = 0 if direct else part + 2 * z.units
    parts, qkv1_b = weight_grads(z, place, "temporal_grads", jobs, direct, room)
    dx[0] = after(dx[0], qkv1_b)
    if direct:
        g2 = mover.add(g2, reduce_steps(z, *parts), partial_set(owned, "temporal"))
    gb, d0, g1, sums_s = spatial_backward(z, place, dx, g2, h1, qkv0, w["out0"], gains)
    jobs = [([x0.reshape(z.rows, D)], [d0]), ([gb], [mixed0.reshape(z.rows, D)])]
    if direct:
        d0 = mover.tick(d0)
        jobs[0] = (jobs[0][0], [d0])
        parts, qkv0_b = weight_grads(z, place, "spatial_grads", jobs, True)
        g1 = mover.tick(g1)
        g1 = mover.add(g1, reduce_steps(z, *parts), partial_set(owned, "spatial"))
    else:
        parts, qkv0_b = weight_grads(
            z, place, "spatial_grads", jobs, False, into=parts[0], start_at=part
        )
    g0, sums_i = input_backward(z, d0, g1, hidden, w["qkv0"], gains)

    def qv(sums):
        parts = sums.reshape(z.cols, 3, z.half)
        return jnp.stack([parts[:, 0].reshape(D), parts[:, 2].reshape(D)])

    gain = jnp.stack([sums_i[0], sums_s[0], sums_h[1]])
    shift = jnp.stack([sums_i[1], sums_s[1], sums_h[2]])
    qv_g = jnp.concatenate([qv(qkv0_b), qv(qkv1_b)])
    out_g = jnp.stack([sums_s[2], sums_h[3]])
    small_g = jnp.concatenate([gain, shift, qv_g, out_g, sums_h[0:1], up_b.reshape(-1, D)])
    return g0, small_g, (parts[0], owned)


def own_parts(qkv_weight, out_weight, up_weight, down_weight, at):
    rows = up_weight.shape[1]
    return {
        "qkv0": qkv_weight[at, 0].reshape(rows, -1),
        "out0": out_weight[at, 0].T,
        "qkv1": qkv_weight[at, 1].reshape(rows, -1),
        "out1": out_weight[at, 1].T,
        "up": up_weight[at],
        "down": down_weight[at].T,
    }


ATTENTION_PARTS = ("qkv0", "qkv1", "out0", "out1")
HIDDEN_PARTS = ("up", "down")


def fetch(parts, cols, batches):
    result = {}
    for names in batches:
        packed = jnp.concatenate([parts[name] for name in names], axis=1)
        full = lax.all_gather(packed, ROWS_AXES, axis=0, tiled=True).reshape(cols, D, -1)
        at = 0
        for name in names:
            width = parts[name].shape[1]
            result[name] = Weight(full, at, width)
            at += width
    return result


def over_cols(value):
    if lax.axis_size("col") != 2:
        return lax.all_gather(value, "col", axis=0)
    other = swap(value, "col", 1)
    first = lax.axis_index("col") == 0
    return jnp.where(first, jnp.stack([value, other]), jnp.stack([other, value]))


def shards(
    hidden_in,
    qkv_weight,
    out_weight,
    up_weight,
    down_weight,
    qv_bias,
    out_bias,
    up_bias,
    down_bias,
    norm_gain,
    norm_shift,
    cotangent,
):
    layers = qkv_weight.shape[0]
    cols = lax.axis_size("col")
    z = Sizes(
        hidden_in.shape[0], up_weight.shape[1], lax.axis_size("dp") // 2, lax.axis_size("row"), cols
    )
    row_at, col_at, dp_at = lax.axis_index("row"), lax.axis_index("col"), lax.axis_index("dp")
    place = [(row_at * cols + col_at) % z.members, row_at, col_at, dp_at % 2, dp_at // 2]
    place = jnp.stack(place).astype(jnp.int32)
    biases = over_cols(jnp.concatenate([qv_bias.reshape(layers, -1), up_bias], axis=1))
    qv_all = biases[:, :, : 4 * z.half].reshape(cols, layers, 2, 2, 1, z.half)
    qv_all = jnp.moveaxis(qv_all, 0, 2)
    up_all = jnp.moveaxis(biases[:, :, 4 * z.half :], 0, 1).reshape(layers, FF)
    zero = jnp.zeros_like(qv_all[:, :, :, 0])
    bias_qkv = jnp.concatenate([qv_all[:, :, :, 0], zero, qv_all[:, :, :, 1]], axis=-1)
    hidden = pad_frames(z, hidden_in)
    kept = []
    for at in range(layers):
        parts = own_parts(qkv_weight, out_weight, up_weight, down_weight, at)
        batches = (ATTENTION_PARTS + HIDDEN_PARTS,) if at == 0 else (ATTENTION_PARTS, HIDDEN_PARTS)
        w = fetch(parts, cols, batches)
        small = (
            norm_gain[at],
            norm_shift[at],
            bias_qkv[at],
            out_bias[at],
            up_all[at][None],
            down_bias[at][None],
        )
        hidden, record = layer_forward(z, place, hidden, w, small)
        kept.append((w, small, record))
    grad = pad_frames(z, cotangent)
    owned = [{} for _ in range(layers)]
    smalls = [None] * layers
    mover, carry = Mover(), None
    for at in reversed(range(layers)):
        w, small, record = kept[at]
        direct = z.direct and at == 0
        grad, small_g, carry = layer_backward(
            z, place, grad, record, w, small, owned[at], mover, direct, carry
        )
        smalls[at] = sum_everywhere(small_g)
    if not z.direct:
        part = 4 * z.half
        last = reduce_whole(z, carry[0][:, :, : 2 * part])
        owned[0]["temporal"], owned[0]["spatial"] = last[:, :part], last[:, part:]
    while mover.flying:
        grad = mover.tick(grad)
    rows, units = z.block, z.units
    qkv_cols = 3 * z.half

    def attention_parts(make):
        return jnp.stack(
            [jnp.stack([make(o["spatial"]), make(o["temporal"])]) for o in owned]
        )

    grad_qkv = attention_parts(lambda a: a[:, :qkv_cols].reshape(rows, 3, z.half))
    grad_out = attention_parts(lambda a: a[:, qkv_cols:].T)
    grad_up = jnp.stack([o["hidden"][:, :units] for o in owned])
    grad_down = jnp.stack([o["hidden"][:, units:].T for o in owned])
    terms = jnp.stack(smalls)
    gain, shift = terms[:, 0:3], terms[:, 3:6]
    qv = terms[:, 6:10].reshape(layers, 2, 2, D)
    outb, downb, upb = terms[:, 10:12], terms[:, 12], terms[:, 13:].reshape(layers, FF)
    qv = lax.dynamic_slice_in_dim(qv, col_at * z.half, z.half, 3)
    upb = lax.dynamic_slice_in_dim(upb, col_at * z.units, z.units, 1)
    return (
        cut_frames(z, hidden),
        cut_frames(z, grad),
        grad_qkv,
        grad_out,
        grad_up,
        grad_down,
        qv,
        outb,
        upb,
        downb,
        gain,
        shift,
    )


def solution(mesh):
    return jax.shard_map(
        shards,
        mesh=mesh,
        in_specs=(
            P(("dp", "row", "col"), None),
            P(None, None, ("dp", "row"), None, "col"),
            P(None, None, "col", ("dp", "row")),
            P(None, ("dp", "row"), "col"),
            P(None, "col", ("dp", "row")),
            P(None, None, None, "col"),
            P(),
            P(None, "col"),
            P(),
            P(),
            P(),
            P(("dp", "row", "col"), None),
        ),
        out_specs=(
            P(("dp", "row", "col"), None),
            P(("dp", "row", "col"), None),
            P(None, None, ("dp", "row"), None, "col"),
            P(None, None, "col", ("dp", "row")),
            P(None, ("dp", "row"), "col"),
            P(None, "col", ("dp", "row")),
            P(None, None, None, "col"),
            P(),
            P(None, "col"),
            P(),
            P(),
            P(),
        ),
        check_vma=False,
    )
```

time: 1320 us -> 801 us (0.61)
  waiting for transfers between devices: 705 us -> 302 us
  Pallas kernels: 431 us -> 294 us
  starting transfers between devices: 28.7 us -> 52.8 us
  local copies, waits for them, and re-layouts: 116 us -> 92.8 us
  other arithmetic: 11.9 us -> 33.6 us
    reduce_scatter x2, waiting for transfers between devices: 416 us -> 0.04 us  [reduce_whole(): lax.psum_scatter(flat_rows, ROWS_AXES, scatter_dimension=0, tiled=True)]
    pallas_call x26 -> x14, Pallas kernels: 431 us -> 228 us  [call(): pl.pallas_call(body, name=name, grid=grid, in_specs=in_specs, out_specs=o...]
    psum x1 -> x0, waiting for transfers between devices: 78.1 us -> none  [shards(): gain, shift, qv, outb, upb, downb = lax.psum(tuple(terms), ALL_AXES)]
    ppermute x0 -> x25, waiting for transfers between devices: none -> 70.5 us  [swap(): return lax.ppermute(value, axis, pairs)]
    ppermute x24, waiting for transfers between devices: 38.5 us -> 108 us  [clip_swap(): lax.ppermute(value, CLIP_AXES, [(at, at ^ apart) for at in range(count)])]
    pallas_call x0 -> x6, Pallas kernels: none -> 66.3 us  [weight_grads(): pl.pallas_call(body, name=name, grid_spec=pltpu.PrefetchScalarGridSpec(nu...]
    all_gather x2 -> x3, waiting for transfers between devices: 171 us -> 124 us  [fetch(): lax.all_gather(packed, ROWS_AXES, axis=0, tiled=True).reshape(cols, D, -1)]
    slice x15 -> x9, local copies, waits for them, and re-layouts: 42.3 us -> 0.12 us  [the longest x3 0.07 us: shards(): a[:, :qkv_cols].reshape(rows, 3, z.half)]
  transfers between devices with their start and end apart: 29 -> 54, of which waited for: 13 -> 32; matrix products, arithmetic and copies ran while one was open for 8% -> 7% of each run, Pallas kernels for 10% -> 30%
where the time goes in v3:
time: 801 us; the launch traced here: 791 us
  waiting for transfers between devices  302 us (38%)
  Pallas kernels  294 us (37%)
  local copies, waits for them, and re-layouts  92.8 us (12%)
  starting transfers between devices  52.8 us (7%)
  other arithmetic  33.6 us (4%)
  between operations  15.8 us (2%)
    pallas_call x14, Pallas kernels, call(): pl.pallas_call(body, name=name, grid=grid, in_specs=in_specs, out_specs=o...  228 us
    all_gather x3, waiting for transfers between devices, fetch(): lax.all_gather(packed, ROWS_AXES, axis=0, tiled=True).reshape(cols, D, -1)  124 us
    ppermute x24, waiting for transfers between devices, clip_swap(): lax.ppermute(value, CLIP_AXES, [(at, at ^ apart) for at in range(count)])  108 us
    ppermute x25, waiting for transfers between devices, swap(): return lax.ppermute(value, axis, pairs)  70.5 us
    pallas_call x6, Pallas kernels, weight_grads(): pl.pallas_call(body, name=name, grid_spec=pltpu.PrefetchScalarGridSpec(nu...  66.3 us
    unnamed x235, local copies, waits for them, and re-layouts  64.1 us
    ppermute x24, starting transfers between devices, clip_swap(): lax.ppermute(value, CLIP_AXES, [(at, at ^ apart) for at in range(count)])  28.5 us
    ppermute x25, starting transfers between devices, swap(): return lax.ppermute(value, axis, pairs)  24.1 us
  transfers between devices with their start and end apart: 54, of which 32 were waited for; matrix products, arithmetic and copies ran while one was open for 7% of the time, Pallas kernels for 30%

profile of v3, /device:TPU:0, one launch (start us, length us, event | category | flops | bytes accessed | tf_op | source)
XLA Modules:
  0.0 791.3 jit_solution(274016995349071413)
XLA Ops:
  11.6 3.0 collective-permute-start
  14.8 2.9 reshape.342
  17.7 3.5 pad.7.h_ref
  21.4 117.5 %all-gather.4.cloned.1.call-done = bf16[1536,6144]{1,0:T(8,128)(2,1)} async-done(((bf16[48,6144]{1,0:T(8,128)(2,1)}), bf16[1536,6144]{1,0:T(8,128)(2,1)}) %all-gather.4.cloned.1.call-update) | async-done | bytes 18874384 | tf_op jit(solution)/shard_map/all_gather | solution.py:1057
  138.9 15.6 %spatial_forward.2 = (bf16[4,208,768]{2,1,0:T(8,128)(2,1)S(1)}, bf16[4,208,2304]{2,1,0:T(8,128)(2,1)}, bf16[4,208,768]{2,1,0:T(8,128)(2,1)S(1)}, f32[4,208,768]{...) custom-call(s32[5]{0:T(128)S(1)} %stack.136.place_ref, ...), custom_call_target="tpu_custom_call" | custom-call | flops 4580179968 | bytes 50660372 | tf_op jit(solution)/shard_map/spatial_forward/pallas_call | solution.py:252
  161.6 6.7 collective-permute-done.1.refs_1_
  168.3 2.9 collective-permute-done.2.refs_2_
  171.3 12.8 %collective-permute-done.3.refs_3_ = bf16[7,32,768]{2,1,0:T(8,128)(2,1)S(1)} collective-permute-done((bf16[7,32,768]{2,1,0:T(8,128)(2,1)S(1)}, bf16[7,32,768]{2,1,0:T(8,128)(2,1)S(1)}, u32[]{:S(2)}, u32[]{:S(2)}) %collective-permute-start.3) | collective-permute-done | bytes 344096 | tf_op jit(solution)/shard_map/ppermute | solution.py:937
  184.1 6.6 copy-done
  190.6 10.4 %temporal_forward.2 = (bf16[7,128,2304]{2,1,0:T(8,128)(2,1)S(1)}, bf16[7,32,768]{2,1,0:T(8,128)(2,1)S(1)}, bf16[7,32,768]{2,1,0:T(8,128)(2,1)S(1)}, bf16[7,32,76...) custom-call(bf16[7,32,768]{2,1,0:T(8,128)(2,1)S(1)} %get-tuple-element.147.refs_0_, ...), custom_call_target="tpu_custom_call" | custom-call | flops 3523215360 | bytes 25764864 | tf_op jit(solution)/shard_map/temporal_forward/pallas_call | solution.py:252
  203.1 2.4 collective-permute-start.4
  206.9 14.4 %collective-permute-done.4.refs_1_ = bf16[7,32,768]{2,1,0:T(8,128)(2,1)S(1)} collective-permute-done((bf16[7,32,768]{2,1,0:T(8,128)(2,1)S(1)}, bf16[7,32,768]{2,1,0:T(8,128)(2,1)S(1)}, u32[]{:S(2)}, u32[]{:S(2)}) %collective-permute-start.4) | collective-permute-done | bytes 344096 | tf_op jit(solution)/shard_map/ppermute | solution.py:937
  221.3 2.3 collective-permute-done.5.refs_2_
  223.6 7.1 collective-permute-done.6.refs_3_
  230.7 24.4 %hidden_forward.2 = (f32[4,208,768]{2,1,0:T(8,128)S(1)}, bf16[832,768]{1,0:T(8,128)(2,1)S(1)}, bf16[832,3072]{1,0:T(8,128)(2,1)}, f32[832,3072]{1,0:T(8,128)}, f32[4,208,768]{2,1,0:T(8,128)}) custom-call(s32[5]{0:T(128)S(1)} %stack.136.place_ref, bf16[7,32,768]{2,1,0:T(8,128)(2,1)S(1)} %get-tuple-element.151.refs_0_, ...), custom_call_target="tpu_custom_call" | custom-call | flops 8833204224 | bytes 82320400 | tf_op jit(solution)/shard_map/hidden_forward/pallas_call | solution.py:252
  260.6 16.0 %spatial_forward.3 = (bf16[4,208,768]{2,1,0:T(8,128)(2,1)S(1)}, bf16[4,208,2304]{2,1,0:T(8,128)(2,1)}, bf16[4,208,768]{2,1,0:T(8,128)(2,1)S(1)}, f32[4,208,768]{...) custom-call(s32[5]{0:T(128)S(1)} %stack.136.place_ref, ...), custom_call_target="tpu_custom_call" | custom-call | flops 4580179968 | bytes 31786004 | tf_op jit(solution)/shard_map/spatial_forward/pallas_call | solution.py:252
  280.3 5.6 collective-permute-done.7.refs_1_
  285.8 3.7 collective-permute-done.8.refs_2_
  289.5 7.5 collective-permute-done.9.refs_3_
  297.0 11.5 %temporal_forward.3 = (bf16[7,128,2304]{2,1,0:T(8,128)(2,1)S(1)}, bf16[7,32,768]{2,1,0:T(8,128)(2,1)S(1)}, bf16[7,32,768]{2,1,0:T(8,128)(2,1)}, bf16[7,32,768]{2,1,0:T(8,128)(2,1)}, bf16[7,32,768]{2,1,0:T(8,128)(2,1)}) custom-call(bf16[7,32,768]{2,1,0:T(8,128)(2,1)S(1)} %get-tuple-element.157.refs_0_, ...), custom_call_target="tpu_custom_call" | custom-call | flops 3523215360 | bytes 16327680 | tf_op jit(solution)/shard_map/temporal_forward/pallas_call | solution.py:252
  312.1 2.6 collective-permute-start.12
  314.8 3.0 reshape.349
  317.8 3.4 pad.8.g_ref
  321.2 6.6 all-gather.8.cloned.1.call-done
  330.7 24.2 %hidden_forward.3 = (f32[4,208,768]{2,1,0:T(8,128)S(1)}, bf16[832,768]{1,0:T(8,128)(2,1)S(1)}, bf16[832,3072]{1,0:T(8,128)(2,1)}, f32[832,3072]{1,0:T(8,128)}, f32[4,208,768]{2,1,0:T(8,128)}) custom-call(s32[5]{0:T(128)S(1)} %stack.136.place_ref, bf16[7,32,768]{2,1,0:T(8,128)(2,1)S(1)} %copy-done.87, ...), custom_call_target="tpu_custom_call" | custom-call | flops 8833204224 | bytes 54008852 | tf_op jit(solution)/shard_map/hidden_forward/pallas_call | solution.py:252
  356.4 19.4 %hidden_backward.2 = (bf16[832,3072]{1,0:T(8,128)(2,1)}, bf16[832,768]{1,0:T(8,128)(2,1)S(1)}, f32[4,208,768]{2,1,0:T(8,128)S(1)}, f32[4,768]{1,0:T(4,128)S(1)},...) custom-call(s32[5]{0:T(128)S(1)} %stack.136.place_ref, ...), custom_call_target="tpu_custom_call" | custom-call | flops 7851737088 | bytes 44553236 | tf_op jit(solution)/shard_map/hidden_backward/pallas_call | solution.py:252
  375.9 3.7 copy-done.65
  379.6 14.2 %hidden_grads.2 = (bf16[2,768,3072]{2,1,0:T(8,128)(2,1)}, f32[1,3072]{1,0:T(1,128)S(1)}) custom-call(s32[5]{0:T(128)S(1)} %stack.136.place_ref, bf16[832,768]{1,0:T(8,128)(2,1)S(1)} %get-tuple-element.170.refs_0_, bf16[832,3072]{1,0:T(8,128)(2,1)S(1)} %copy-done.65, bf16[832,768]{1,0:T(8,128)(2,1)S(1)} %get-tuple-element.172.refs_2_, ...), custom_call_target="tpu_custom_call" | custom-call | flops 7851737088 | bytes 22228992 | tf_op jit(solution)/shard_map/hidden_grads/pallas_call | solution.py:823
  395.0 2.3 collective-permute-start.15
  397.7 5.5 collective-permute-done.13.refs_1_
  403.1 2.5 collective-permute-done.14.refs_2_
  405.6 6.0 collective-permute-done.15.refs_3_
  411.7 17.7 %temporal_backward.2 = (bf16[896,2304]{1,0:T(8,128)(2,1)S(1)}, bf16[7,32,768]{2,1,0:T(8,128)(2,1)S(1)}, bf16[7,32,768]{2,1,0:T(8,128)(2,1)S(1)}, bf16[7,32,768]{2,1,0:T(8,128)(2,1)S(1)}, bf16[7,32,768]{2,1,0:T(8,128)(2,1)S(1)}) custom-call(bf16[7,32,768]{2,1,0:T(8,128)(2,1)S(1)} %get-tuple-element.175.refs_0_, ...), custom_call_target="tpu_custom_call" | custom-call | flops 5108662272 | bytes 29884416 | tf_op jit(solution)/shard_map/temporal_backward/pallas_call | solution.py:252
  432.9 9.6 %temporal_grads.2 = (bf16[2,768,6144]{2,1,0:T(8,128)(2,1)}, f32[1,2304]{1,0:T(1,128)S(1)}) custom-call(s32[5]{0:T(128)S(1)} %stack.136.place_ref, bf16[896,768]{1,0:T(8,128)(2,1)S(1)} %bitcast.275, bf16[896,2304]{1,0:T(8,128)(2,1)S(1)} %get-tuple-element.181.refs_1_, bf16[224,768]{1,0:T(8,128)(2,1)S(1)} %bitcast.287, bf16[224,768]{1,0:T(8,128)(2,1)S(1)} %bitcast.296, ...), custom_call_target="tpu_custom_call" | custom-call | flops 4227858432 | bytes 27141120 | tf_op jit(solution)/shard_map/temporal_grads/pallas_call | solution.py:823
  444.6 2.3 collective-permute-done.18.refs_3_
  451.0 19.3 %spatial_backward.2 = (bf16[832,768]{1,0:T(8,128)(2,1)S(1)}, bf16[832,2304]{1,0:T(8,128)(2,1)}, f32[4,208,768]{2,1,0:T(8,128)S(1)}, f32[3,768]{1,0:T(4,128)S(1)}) custom-call(s32[5]{0:T(128)S(1)} %stack.136.place_ref, bf16[7,32,768]{2,1,0:T(8,128)(2,1)S(1)} %get-tuple-element.183.refs_0_, bf16[7,32,768]{2,1,0:T(8,128)(2,1)S(1)} %copy-done.48, ...), custom_call_target="tpu_custom_call" | custom-call | flops 2617245696 | bytes 27445268 | tf_op jit(solution)/shard_map/spatial_backward/pallas_call | solution.py:252
  475.9 5.2 input_backward.2
  481.2 9.5 %spatial_grads.2 = (bf16[2,768,6144]{2,1,0:T(8,128)(2,1)}, f32[1,2304]{1,0:T(1,128)S(1)}) custom-call(s32[5]{0:T(128)S(1)} %stack.136.place_ref, bf16[2,768,6144]{2,1,0:T(8,128)(2,1)} %get-tuple-element.195.refs_0_, bf16[832,768]{1,0:T(8,128)(2,1)S(1)} %bitcast.277, bf16[832,2304]{1,0:T(8,128)(2,1)S(1)} %copy-done.3, ...), custom_call_target="tpu_custom_call", output_to_operand_aliasing={{0}: (1, {})} | custom-call | flops 3925868544 | bytes 45425664 | tf_op jit(solution)/shard_map/spatial_grads/pallas_call | solution.py:823
  491.3 19.5 %hidden_backward.3 = (bf16[832,3072]{1,0:T(8,128)(2,1)}, bf16[832,768]{1,0:T(8,128)(2,1)S(1)}, f32[4,208,768]{2,1,0:T(8,128)S(1)}, f32[4,768]{1,0:T(4,128)S(1)},...) custom-call(s32[5]{0:T(128)S(1)} %stack.136.place_ref, ...), custom_call_target="tpu_custom_call" | custom-call | flops 7851737088 | bytes 63427604 | tf_op jit(solution)/shard_map/hidden_backward/pallas_call | solution.py:252
  514.1 2.6 copy-done.6
  518.0 14.2 %hidden_grads.3 = (bf16[2,768,6144]{2,1,0:T(8,128)(2,1)}, f32[1,3072]{1,0:T(1,128)S(1)}) custom-call(s32[5]{0:T(128)S(1)} %stack.136.place_ref, bf16[2,768,6144]{2,1,0:T(8,128)(2,1)} %get-tuple-element.199.refs_0_, bf16[832,768]{1,0:T(8,128)(2,1)S(1)} %copy-done.36, bf16[832,3072]{1,0:T(8,128)(2,1)S(1)} %copy-done.6, ...), custom_call_target="tpu_custom_call", output_to_operand_aliasing={{0}: (1, {})} | custom-call | flops 7851737088 | bytes 50540544 | tf_op jit(solution)/shard_map/hidden_grads/pallas_call | solution.py:823
  532.7 2.6 collective-permute-start.20
  537.3 5.2 collective-permute-done.19.refs_1_
  544.4 4.8 collective-permute-done.21.refs_3_
  549.3 18.8 %temporal_backward.3 = (bf16[896,2304]{1,0:T(8,128)(2,1)S(1)}, bf16[7,32,768]{2,1,0:T(8,128)(2,1)S(1)}, bf16[7,32,768]{2,1,0:T(8,128)(2,1)}, bf16[7,32,768]{2,1,0:T(8,128)(2,1)}, bf16[7,32,768]{2,1,0:T(8,128)(2,1)}) custom-call(bf16[7,32,768]{2,1,0:T(8,128)(2,1)S(1)} %copy-done.54, bf16[7,32,768]{2,1,0:T(8,128)(2,1)S(1)} %collective-permute-done.19.refs_1_, ...), custom_call_target="tpu_custom_call" | custom-call | flops 5108662272 | bytes 48758784 | tf_op jit(solution)/shard_map/temporal_backward/pallas_call | solution.py:252
  568.2 9.5 %temporal_grads.3 = (bf16[2,2,4,48,1536]{4,3,2,1,0:T(8,128)(2,1)S(1)}, bf16[2,2,4,48,1536]{4,3,2,1,0:T(8,128)(2,1)}, f32[1,2304]{1,0:T(1,128)S(1)}) custom-call(s32[5]{0:T(128)S(1)} %stack.136.place_ref, bf16[896,768]{1,0:T(8,128)(2,1)S(1)} %bitcast.276, bf16[896,2304]{1,0:T(8,128)(2,1)S(1)} %get-tuple-element.211.refs_1_, bf16[224,768]{1,0:T(8,128)(2,1)S(1)} %bitcast.288, ...), custom_call_target="tpu_custom_call" | custom-call | flops 4227858432 | bytes 12985344 | tf_op jit(solution)/shard_map/temporal_grads/pallas_call | solution.py:823
  583.9 5.9 collective-permute-done.22.refs_1_
  591.3 7.2 collective-permute-done.24.refs_3_
  599.4 18.9 %spatial_backward.3 = (bf16[832,768]{1,0:T(8,128)(2,1)S(1)}, bf16[832,2304]{1,0:T(8,128)(2,1)}, f32[4,208,768]{2,1,0:T(8,128)S(1)}, f32[3,768]{1,0:T(4,128)S(1)}) custom-call(s32[5]{0:T(128)S(1)} %stack.136.place_ref, bf16[7,32,768]{2,1,0:T(8,128)(2,1)S(1)} %copy-done.56, bf16[7,32,768]{2,1,0:T(8,128)(2,1)S(1)} %collective-permute-done.22.refs_1_, ...), custom_call_target="tpu_custom_call" | custom-call | flops 2617245696 | bytes 36882452 | tf_op jit(solution)/shard_map/spatial_backward/pallas_call | solution.py:252
  619.8 2.5 fusion
  630.8 9.3 %spatial_grads.3 = (bf16[2,2,4,48,1536]{4,3,2,1,0:T(8,128)(2,1)S(1)}, bf16[2,2,4,48,1536]{4,3,2,1,0:T(8,128)(2,1)}, f32[1,2304]{1,0:T(1,128)S(1)}) custom-call(s32[5]{0:T(128)S(1)} %stack.136.place_ref, bf16[832,768]{1,0:T(8,128)(2,1)S(1)} %bitcast.291, bf16[832,2304]{1,0:T(8,128)(2,1)S(1)} %copy-done.11, bf16[832,768]{1,0:T(8,128)(2,1)S(1)} %copy-done.71, ...), custom_call_target="tpu_custom_call" | custom-call | flops 3925868544 | bytes 12395520 | tf_op jit(solution)/shard_map/spatial_grads/pallas_call | solution.py:823
  643.7 2.5 fusion.8
  647.7 3.1 collective-permute-done.44
  655.9 6.7 input_backward.3
  668.5 4.0 collective-permute-done.46
  679.1 3.2 slice.453
  682.3 3.4 reshape.348
  687.6 4.1 collective-permute-done.42
  700.1 23.6 %collective-permute-done.31 = bf16[2,48,1536]{2,1,0:T(8,128)(2,1)S(1)} collective-permute-done((bf16[2,48,1536]{2,1,0:T(8,128)(2,1)S(1)}, bf16[2,48,1536]{2,1,0:T(8,128)(2,1)S(1)}, u32[]{:S(2)}, u32[]{:S(2)}) %collective-permute-start.31) | collective-permute-done | bytes 294944 | tf_op jit(solution)/shard_map/ppermute | solution.py:845
  723.8 2.3 fusion.15
  733.4 3.0 collective-permute-done.34
  740.1 25.0 %collective-permute-done.37 = bf16[2,48,1536]{2,1,0:T(8,128)(2,1)} collective-permute-done((bf16[2,48,1536]{2,1,0:T(8,128)(2,1)}, bf16[2,48,1536]{2,1,0:T(8,128)(2,1)}, u32[]{:S(2)}, u32[]{:S(2)}) %collective-permute-start.37) | collective-permute-done | bytes 294944 | tf_op jit(solution)/shard_map/ppermute | solution.py:845
  766.5 5.1 collective-permute-done.38
  773.3 2.8 reshape.372
  (424 shorter events, 131.9 us)
Async XLA Ops:
  7.2 131.7 %all-gather.4.cloned.1.call-start = ((), (), s32[]{:S(2)}) async-start(), calls=%async_computation.2 | async-start | bytes 19464192 | tf_op jit(solution)/shard_map/all_gather | solution.py:1057
  9.7 251.0 %all-gather.6.cloned.1.call-start = ((), (), s32[]{:S(2)}) async-start(), calls=%async_computation.3 | async-start | bytes 9732096 | tf_op jit(solution)/shard_map/all_gather | solution.py:1057
  10.7 317.1 %all-gather.8.cloned.1.call-start = ((), (), s32[]{:S(2)}) async-start(), calls=%async_computation.4 | async-start | bytes 9732096 | tf_op jit(solution)/shard_map/all_gather | solution.py:1057
  11.5 766.3 %reduce-scatter.5.cloned.1.call-start = ((), (), s32[]{:S(2)}) async-start(), calls=%async_computation.6 | async-start | bytes 9732096 | tf_op jit(solution)/shard_map/reduce_scatter | solution.py:861
  11.6 9.6 %collective-permute-start = (f32[2,3072]{1,0:T(2,128)S(1)}, f32[2,3072]{1,0:T(2,128)S(1)}, u32[]{:S(2)}, u32[]{:S(2)}) collective-permute-start(f32[2,3072]{1,0:T(2,128)S(1)} %constant_dynamic-update-slice_fusion.2), channel_id=1, source_target_pairs={{0,1},{1,0},{2,3},{3,2},{4,5},{5,4},{6,7},{7,6},{8,9},{9,8},{10,11... | collective-permute-start | bytes 73736 | tf_op jit(solution)/shard_map/ppermute | solution.py:845
  158.1 10.2 %collective-permute-start.1 = (bf16[7,32,768]{2,1,0:T(8,128)(2,1)S(1)}, bf16[7,32,768]{2,1,0:T(8,128)(2,1)S(1)}, u32[]{:S(2)}, u32[]{:S(2)}) collective-permute-start(bf16[7,32,768]{2,1,0:T(8,128)(2,1)S(1)} %get-tuple-element.148), channel_id=1, source_target_pairs={{0,1},{1,0},{2,3},{3,2},{4,5},{5,4},{6,7},{7,6},{8,9},{9,8},{10,11... | collective-permute-start | bytes 1032200 | tf_op jit(solution)/shard_map/ppermute | solution.py:937
  159.6 11.7 %collective-permute-start.2 = (bf16[7,32,768]{2,1,0:T(8,128)(2,1)S(1)}, bf16[7,32,768]{2,1,0:T(8,128)(2,1)S(1)}, u32[]{:S(2)}, u32[]{:S(2)}) collective-permute-start(bf16[7,32,768]{2,1,0:T(8,128)(2,1)S(1)} %get-tuple-element.149), channel_id=1, source_target_pairs={{0,2},{1,3},{2,0},{3,1},{4,6},{5,7},{6,4},{7,5},{8,10},{9,11},{10,... | collective-permute-start | bytes 1032200 | tf_op jit(solution)/shard_map/ppermute | solution.py:937
  160.1 24.0 %collective-permute-start.3 = (bf16[7,32,768]{2,1,0:T(8,128)(2,1)S(1)}, bf16[7,32,768]{2,1,0:T(8,128)(2,1)S(1)}, u32[]{:S(2)}, u32[]{:S(2)}) collective-permute-start(bf16[7,32,768]{2,1,0:T(8,128)(2,1)S(1)} %get-tuple-element.150), channel_id=1, source_target_pairs={{0,3},{1,2},{2,1},{3,0},{4,7},{5,6},{6,5},{7,4},{8,11},{9,10},{10,... | collective-permute-start | bytes 1032200 | tf_op jit(solution)/shard_map/ppermute | solution.py:937
  171.3 29.8 %copy-start.29 = (bf16[7,32,768]{2,1,0:T(8,128)(2,1)}, bf16[7,32,768]{2,1,0:T(8,128)(2,1)S(1)}, u32[]{:S(2)}) copy-start(bf16[7,32,768]{2,1,0:T(8,128)(2,1)S(1)} %collective-permute-done.2.refs_2_) | copy-start | bytes 1032196
  203.1 18.2 %collective-permute-start.4 = (bf16[7,32,768]{2,1,0:T(8,128)(2,1)S(1)}, bf16[7,32,768]{2,1,0:T(8,128)(2,1)S(1)}, u32[]{:S(2)}, u32[]{:S(2)}) collective-permute-start(bf16[7,32,768]{2,1,0:T(8,128)(2,1)S(1)} %get-tuple-element.152), channel_id=1, source_target_pairs={{0,1},{1,0},{2,3},{3,2},{4,5},{5,4},{6,7},{7,6},{8,9},{9,8},{10,11... | collective-permute-start | bytes 1032200 | tf_op jit(solution)/shard_map/ppermute | solution.py:937
  205.4 18.2 %collective-permute-start.5 = (bf16[7,32,768]{2,1,0:T(8,128)(2,1)S(1)}, bf16[7,32,768]{2,1,0:T(8,128)(2,1)S(1)}, u32[]{:S(2)}, u32[]{:S(2)}) collective-permute-start(bf16[7,32,768]{2,1,0:T(8,128)(2,1)S(1)} %get-tuple-element.153), channel_id=1, source_target_pairs={{0,2},{1,3},{2,0},{3,1},{4,6},{5,7},{6,4},{7,5},{8,10},{9,11},{10,... | collective-permute-start | bytes 1032200 | tf_op jit(solution)/shard_map/ppermute | solution.py:937
  206.3 24.5 %collective-permute-start.6 = (bf16[7,32,768]{2,1,0:T(8,128)(2,1)S(1)}, bf16[7,32,768]{2,1,0:T(8,128)(2,1)S(1)}, u32[]{:S(2)}, u32[]{:S(2)}) collective-permute-start(bf16[7,32,768]{2,1,0:T(8,128)(2,1)S(1)} %get-tuple-element.154), channel_id=1, source_target_pairs={{0,3},{1,2},{2,1},{3,0},{4,7},{5,6},{6,5},{7,4},{8,11},{9,10},{10,... | collective-permute-start | bytes 1032200 | tf_op jit(solution)/shard_map/ppermute | solution.py:937
  260.6 36.3 %copy-start.1 = (bf16[1536,3072]{1,0:T(8,128)(2,1)S(1)}, bf16[1536,3072]{1,0:T(8,128)(2,1)}, u32[]{:S(2)}) copy-start(bf16[1536,3072]{1,0:T(8,128)(2,1)} %all-gather.6.cloned.1.call-done) | copy-start | bytes 28311556
  276.7 31.8 %copy-start.15 = (f32[4,208,768]{2,1,0:T(8,128)}, f32[4,208,768]{2,1,0:T(8,128)S(1)}, u32[]{:S(2)}) copy-start(f32[4,208,768]{2,1,0:T(8,128)S(1)} %get-tuple-element.165.refs_4_.refs_5_) | copy-start | bytes 7667716
  276.7 31.8 %copy-start.31 = (bf16[4,208,768]{2,1,0:T(8,128)(2,1)}, bf16[4,208,768]{2,1,0:T(8,128)(2,1)S(1)}, u32[]{:S(2)}) copy-start(bf16[4,208,768]{2,1,0:T(8,128)(2,1)S(1)} %get-tuple-element.196) | copy-start | bytes 3833860
  276.7 31.8 %copy-start.33 = (bf16[4,208,768]{2,1,0:T(8,128)(2,1)}, bf16[4,208,768]{2,1,0:T(8,128)(2,1)S(1)}, u32[]{:S(2)}) copy-start(bf16[4,208,768]{2,1,0:T(8,128)(2,1)S(1)} %get-tuple-element.198) | copy-start | bytes 3833860
  276.7 9.1 %collective-permute-start.7 = (bf16[7,32,768]{2,1,0:T(8,128)(2,1)}, bf16[7,32,768]{2,1,0:T(8,128)(2,1)S(1)}, u32[]{:S(2)}, u32[]{:S(2)}) collective-permute-start(bf16[7,32,768]{2,1,0:T(8,128)(2,1)} %get-tuple-element.158), channel_id=1, source_target_pairs={{0,1},{1,0},{2,3},{3,2},{4,5},{5,4},{6,7},{7,6},{8,9},{9,8},{10,11... | collective-permute-start | bytes 1032200 | tf_op jit(solution)/shard_map/ppermute | solution.py:937
  277.4 12.2 %collective-permute-start.8 = (bf16[7,32,768]{2,1,0:T(8,128)(2,1)S(1)}, bf16[7,32,768]{2,1,0:T(8,128)(2,1)S(1)}, u32[]{:S(2)}, u32[]{:S(2)}) collective-permute-start(bf16[7,32,768]{2,1,0:T(8,128)(2,1)S(1)} %get-tuple-element.159), channel_id=1, source_target_pairs={{0,2},{1,3},{2,0},{3,1},{4,6},{5,7},{6,4},{7,5},{8,10},{9,11},{10,... | collective-permute-start | bytes 1032200 | tf_op jit(solution)/shard_map/ppermute | solution.py:937
  278.0 18.9 %collective-permute-start.9 = (bf16[7,32,768]{2,1,0:T(8,128)(2,1)S(1)}, bf16[7,32,768]{2,1,0:T(8,128)(2,1)S(1)}, u32[]{:S(2)}, u32[]{:S(2)}) collective-permute-start(bf16[7,32,768]{2,1,0:T(8,128)(2,1)S(1)} %get-tuple-element.160), channel_id=1, source_target_pairs={{0,3},{1,2},{2,1},{3,0},{4,7},{5,6},{6,5},{7,4},{8,11},{9,10},{10,... | collective-permute-start | bytes 1032200 | tf_op jit(solution)/shard_map/ppermute | solution.py:937
  311.3 16.5 %collective-permute-start.10 = (bf16[7,32,768]{2,1,0:T(8,128)(2,1)}, bf16[7,32,768]{2,1,0:T(8,128)(2,1)S(1)}, u32[]{:S(2)}, u32[]{:S(2)}) collective-permute-start(bf16[7,32,768]{2,1,0:T(8,128)(2,1)} %get-tuple-element.162), channel_id=1, source_target_pairs={{0,1},{1,0},{2,3},{3,2},{4,5},{5,4},{6,7},{7,6},{8,9},{9,8},{10,11... | collective-permute-start | bytes 1032200 | tf_op jit(solution)/shard_map/ppermute | solution.py:937
  311.8 16.0 %collective-permute-start.11 = (bf16[7,32,768]{2,1,0:T(8,128)(2,1)}, bf16[7,32,768]{2,1,0:T(8,128)(2,1)S(1)}, u32[]{:S(2)}, u32[]{:S(2)}) collective-permute-start(bf16[7,32,768]{2,1,0:T(8,128)(2,1)} %get-tuple-element.163), channel_id=1, source_target_pairs={{0,2},{1,3},{2,0},{3,1},{4,6},{5,7},{6,4},{7,5},{8,10},{9,11},{10,... | collective-permute-start | bytes 1032200 | tf_op jit(solution)/shard_map/ppermute | solution.py:937
  312.1 17.5 %collective-permute-start.12 = (bf16[7,32,768]{2,1,0:T(8,128)(2,1)}, bf16[7,32,768]{2,1,0:T(8,128)(2,1)S(1)}, u32[]{:S(2)}, u32[]{:S(2)}) collective-permute-start(bf16[7,32,768]{2,1,0:T(8,128)(2,1)} %get-tuple-element.164), channel_id=1, source_target_pairs={{0,3},{1,2},{2,1},{3,0},{4,7},{5,6},{6,5},{7,4},{8,11},{9,10},{10,... | collective-permute-start | bytes 1032200 | tf_op jit(solution)/shard_map/ppermute | solution.py:937
  329.6 25.3 %copy-start.72 = (bf16[7,32,768]{2,1,0:T(8,128)(2,1)}, bf16[7,32,768]{2,1,0:T(8,128)(2,1)S(1)}, u32[]{:S(2)}) copy-start(bf16[7,32,768]{2,1,0:T(8,128)(2,1)S(1)} %collective-permute-done.12.refs_3_) | copy-start | bytes 1032196
  393.8 385.1 %reduce-scatter.3.cloned.1.call-start = ((), (), s32[]{:S(2)}) async-start(), calls=%async_computation.5 | async-start | bytes 19464192 | tf_op jit(solution)/shard_map/reduce_scatter | solution.py:861
  393.8 9.3 %collective-permute-start.13 = (bf16[7,32,768]{2,1,0:T(8,128)(2,1)}, bf16[7,32,768]{2,1,0:T(8,128)(2,1)S(1)}, u32[]{:S(2)}, u32[]{:S(2)}) collective-permute-start(bf16[7,32,768]{2,1,0:T(8,128)(2,1)} %copy-done.74), channel_id=1, source_target_pairs={{0,1},{1,0},{2,3},{3,2},{4,5},{5,4},{6,7},{7,6},{8,9},{9,8},{10,11... | collective-permute-start | bytes 1032200 | tf_op jit(solution)/shard_map/ppermute | solution.py:937
  394.4 11.2 %collective-permute-start.14 = (bf16[7,32,768]{2,1,0:T(8,128)(2,1)}, bf16[7,32,768]{2,1,0:T(8,128)(2,1)S(1)}, u32[]{:S(2)}, u32[]{:S(2)}) collective-permute-start(bf16[7,32,768]{2,1,0:T(8,128)(2,1)} %copy-done.76), channel_id=1, source_target_pairs={{0,2},{1,3},{2,0},{3,1},{4,6},{5,7},{6,4},{7,5},{8,10},{9,11},{10,... | collective-permute-start | bytes 1032200 | tf_op jit(solution)/shard_map/ppermute | solution.py:937
  395.0 16.6 %collective-permute-start.15 = (bf16[7,32,768]{2,1,0:T(8,128)(2,1)}, bf16[7,32,768]{2,1,0:T(8,128)(2,1)S(1)}, u32[]{:S(2)}, u32[]{:S(2)}) collective-permute-start(bf16[7,32,768]{2,1,0:T(8,128)(2,1)} %copy-done.78), channel_id=1, source_target_pairs={{0,3},{1,2},{2,1},{3,0},{4,7},{5,6},{6,5},{7,4},{8,11},{9,10},{10,... | collective-permute-start | bytes 1032200 | tf_op jit(solution)/shard_map/ppermute | solution.py:937
  429.4 13.8 %collective-permute-start.16 = (bf16[7,32,768]{2,1,0:T(8,128)(2,1)S(1)}, bf16[7,32,768]{2,1,0:T(8,128)(2,1)S(1)}, u32[]{:S(2)}, u32[]{:S(2)}) collective-permute-start(bf16[7,32,768]{2,1,0:T(8,128)(2,1)S(1)} %get-tuple-element.184), channel_id=1, source_target_pairs={{0,1},{1,0},{2,3},{3,2},{4,5},{5,4},{6,7},{7,6},{8,9},{9,8},{10,11... | collective-permute-start | bytes 1032200 | tf_op jit(solution)/shard_map/ppermute | solution.py:937
  430.3 13.6 %collective-permute-start.17 = (bf16[7,32,768]{2,1,0:T(8,128)(2,1)S(1)}, bf16[7,32,768]{2,1,0:T(8,128)(2,1)S(1)}, u32[]{:S(2)}, u32[]{:S(2)}) collective-permute-start(bf16[7,32,768]{2,1,0:T(8,128)(2,1)S(1)} %get-tuple-element.185), channel_id=1, source_target_pairs={{0,2},{1,3},{2,0},{3,1},{4,6},{5,7},{6,4},{7,5},{8,10},{9,11},{10,... | collective-permute-start | bytes 1032200 | tf_op jit(solution)/shard_map/ppermute | solution.py:937
  431.7 15.2 %collective-permute-start.18 = (bf16[7,32,768]{2,1,0:T(8,128)(2,1)S(1)}, bf16[7,32,768]{2,1,0:T(8,128)(2,1)S(1)}, u32[]{:S(2)}, u32[]{:S(2)}) collective-permute-start(bf16[7,32,768]{2,1,0:T(8,128)(2,1)S(1)} %get-tuple-element.186), channel_id=1, source_target_pairs={{0,3},{1,2},{2,1},{3,0},{4,7},{5,6},{6,5},{7,4},{8,11},{9,10},{10,... | collective-permute-start | bytes 1032200 | tf_op jit(solution)/shard_map/ppermute | solution.py:937
  447.7 24.1 %slice-start = ((s8[9437184]{0:T(1024)(128)(4,1)}), s8[4194304]{0:T(1024)(128)(4,1)S(1)}, s32[]{:S(2)}) async-start(s8[9437184]{0:T(1024)(128)(4,1)} %bitcast.266), calls=%async_computation.7 | async-start | bytes 8388608
  491.3 22.7 %copy-start.36 = (bf16[832,768]{1,0:T(8,128)(2,1)S(1)}, bf16[832,768]{1,0:T(8,128)(2,1)}, u32[]{:S(2)}) copy-start(bf16[832,768]{1,0:T(8,128)(2,1)} %copy-done.35) | copy-start | bytes 3833860
  532.2 10.3 %collective-permute-start.19 = (bf16[7,32,768]{2,1,0:T(8,128)(2,1)}, bf16[7,32,768]{2,1,0:T(8,128)(2,1)S(1)}, u32[]{:S(2)}, u32[]{:S(2)}) collective-permute-start(bf16[7,32,768]{2,1,0:T(8,128)(2,1)} %copy-done.80), channel_id=1, source_target_pairs={{0,1},{1,0},{2,3},{3,2},{4,5},{5,4},{6,7},{7,6},{8,9},{9,8},{10,11... | collective-permute-start | bytes 1032200 | tf_op jit(solution)/shard_map/ppermute | solution.py:937
  532.7 11.8 %collective-permute-start.20 = (bf16[7,32,768]{2,1,0:T(8,128)(2,1)}, bf16[7,32,768]{2,1,0:T(8,128)(2,1)S(1)}, u32[]{:S(2)}, u32[]{:S(2)}) collective-permute-start(bf16[7,32,768]{2,1,0:T(8,128)(2,1)} %copy-done.82), channel_id=1, source_target_pairs={{0,2},{1,3},{2,0},{3,1},{4,6},{5,7},{6,4},{7,5},{8,10},{9,11},{10,... | collective-permute-start | bytes 1032200 | tf_op jit(solution)/shard_map/ppermute | solution.py:937
  535.3 14.0 %collective-permute-start.21 = (bf16[7,32,768]{2,1,0:T(8,128)(2,1)}, bf16[7,32,768]{2,1,0:T(8,128)(2,1)S(1)}, u32[]{:S(2)}, u32[]{:S(2)}) collective-permute-start(bf16[7,32,768]{2,1,0:T(8,128)(2,1)} %copy-done.84), channel_id=1, source_target_pairs={{0,3},{1,2},{2,1},{3,0},{4,7},{5,6},{6,5},{7,4},{8,11},{9,10},{10,... | collective-permute-start | bytes 1032200 | tf_op jit(solution)/shard_map/ppermute | solution.py:937
  579.1 40.7 %collective-permute-start.25 = (bf16[2,2,4,48,1536]{4,3,2,1,0:T(8,128)(2,1)}, bf16[2,2,4,48,1536]{4,3,2,1,0:T(8,128)(2,1)}, u32[]{:S(2)}, u32[]{:S(2)}) collective-permute-start(bf16[2,2,4,48,1536]{4,3,2,1,0:T(8,128)(2,1)} %get-tuple-element.222), channel_id=1, source_target_pairs={{0,4},{4,0},{8,12},{12,8},{16,20},{20,16},{24,28},{28,24},{1,5},{5... | collective-permute-start | bytes 7077896 | tf_op jit(solution)/shard_map/ppermute | solution.py:845
  579.1 10.7 %collective-permute-start.22 = (bf16[7,32,768]{2,1,0:T(8,128)(2,1)}, bf16[7,32,768]{2,1,0:T(8,128)(2,1)S(1)}, u32[]{:S(2)}, u32[]{:S(2)}) collective-permute-start(bf16[7,32,768]{2,1,0:T(8,128)(2,1)} %get-tuple-element.214), channel_id=1, source_target_pairs={{0,1},{1,0},{2,3},{3,2},{4,5},{5,4},{6,7},{7,6},{8,9},{9,8},{10,11... | collective-permute-start | bytes 1032200 | tf_op jit(solution)/shard_map/ppermute | solution.py:937
  580.2 11.1 %collective-permute-start.23 = (bf16[7,32,768]{2,1,0:T(8,128)(2,1)}, bf16[7,32,768]{2,1,0:T(8,128)(2,1)S(1)}, u32[]{:S(2)}, u32[]{:S(2)}) collective-permute-start(bf16[7,32,768]{2,1,0:T(8,128)(2,1)} %get-tuple-element.215), channel_id=1, source_target_pairs={{0,2},{1,3},{2,0},{3,1},{4,6},{5,7},{6,4},{7,5},{8,10},{9,11},{10,... | collective-permute-start | bytes 1032200 | tf_op jit(solution)/shard_map/ppermute | solution.py:937
  581.9 16.5 %collective-permute-start.24 = (bf16[7,32,768]{2,1,0:T(8,128)(2,1)}, bf16[7,32,768]{2,1,0:T(8,128)(2,1)}, u32[]{:S(2)}, u32[]{:S(2)}) collective-permute-start(bf16[7,32,768]{2,1,0:T(8,128)(2,1)} %get-tuple-element.216), channel_id=1, source_target_pairs={{0,3},{1,2},{2,1},{3,0},{4,7},{5,6},{6,5},{7,4},{8,11},{9,10},{10,... | collective-permute-start | bytes 1032200 | tf_op jit(solution)/shard_map/ppermute | solution.py:937
  624.4 19.1 %collective-permute-start.26 = (bf16[2,2,48,1536]{3,2,1,0:T(8,128)(2,1)}, bf16[2,2,48,1536]{3,2,1,0:T(8,128)(2,1)S(1)}, u32[]{:S(2)}, u32[]{:S(2)}) collective-permute-start(bf16[2,2,48,1536]{3,2,1,0:T(8,128)(2,1)} %fusion), channel_id=1, source_target_pairs={{0,2},{2,0},{1,3},{3,1},{4,6},{6,4},{5,7},{7,5},{8,10},{10,8},{9,1... | collective-permute-start | bytes 1769480 | tf_op jit(solution)/shard_map/ppermute | solution.py:845
  626.3 17.4 %collective-permute-start.27 = (bf16[2,2,48,1536]{3,2,1,0:T(8,128)(2,1)}, bf16[2,2,48,1536]{3,2,1,0:T(8,128)(2,1)}, u32[]{:S(2)}, u32[]{:S(2)}) collective-permute-start(bf16[2,2,48,1536]{3,2,1,0:T(8,128)(2,1)} %fusion.1), channel_id=1, source_target_pairs={{0,1},{1,0},{2,3},{3,2},{4,5},{5,4},{6,7},{7,6},{8,9},{9,8},{10,11... | collective-permute-start | bytes 1769480 | tf_op jit(solution)/shard_map/ppermute | solution.py:845
  643.5 80.2 %copy-start.92 = (bf16[2,2,48,1536]{3,2,1,0:T(8,128)(2,1)}, bf16[2,2,48,1536]{3,2,1,0:T(8,128)(2,1)S(1)}, u32[]{:S(2)}) copy-start(bf16[2,2,48,1536]{3,2,1,0:T(8,128)(2,1)S(1)} %collective-permute-done.26) | copy-start | bytes 1769476
  646.1 46.1 %collective-permute-start.30 = (bf16[2,2,4,48,1536]{4,3,2,1,0:T(8,128)(2,1)}, bf16[2,2,4,48,1536]{4,3,2,1,0:T(8,128)(2,1)}, u32[]{:S(2)}, u32[]{:S(2)}) collective-permute-start(bf16[2,2,4,48,1536]{4,3,2,1,0:T(8,128)(2,1)} %get-tuple-element.242), channel_id=1, source_target_pairs={{0,4},{4,0},{8,12},{12,8},{16,20},{20,16},{24,28},{28,24},{1,5},{5... | collective-permute-start | bytes 7077896 | tf_op jit(solution)/shard_map/ppermute | solution.py:845
  646.4 4.4 collective-permute-start.44
  651.4 12.9 %collective-permute-start.45 = (f32[17,768]{1,0:T(8,128)}, f32[17,768]{1,0:T(8,128)}, u32[]{:S(2)}, u32[]{:S(2)}) collective-permute-start(f32[17,768]{1,0:T(8,128)} %add.283), channel_id=1, source_target_pairs={{0,8},{4,12},{8,0},{12,4},{16,24},{20,28},{24,16},{28,20},{1,9},{5... | collective-permute-start | bytes 156680 | tf_op jit(solution)/shard_map/ppermute | solution.py:845
  664.3 3.0 collective-permute-start.39
  665.3 7.2 collective-permute-start.46
  667.3 8.6 %collective-permute-start.40 = (f32[17,768]{1,0:T(8,128)S(1)}, f32[17,768]{1,0:T(8,128)S(1)}, u32[]{:S(2)}, u32[]{:S(2)}) collective-permute-start(f32[17,768]{1,0:T(8,128)S(1)} %add.278), channel_id=1, source_target_pairs={{0,8},{4,12},{8,0},{12,4},{16,24},{20,28},{24,16},{28,20},{1,9},{5... | collective-permute-start | bytes 156680 | tf_op jit(solution)/shard_map/ppermute | solution.py:845
  672.5 5.2 collective-permute-start.47
  674.0 18.3 %collective-permute-start.28 = (bf16[2,48,1536]{2,1,0:T(8,128)(2,1)}, bf16[2,48,1536]{2,1,0:T(8,128)(2,1)}, u32[]{:S(2)}, u32[]{:S(2)}) collective-permute-start(bf16[2,48,1536]{2,1,0:T(8,128)(2,1)} %get-tuple-element.240), channel_id=1, source_target_pairs={{0,2},{2,0},{1,3},{3,1},{4,6},{6,4},{5,7},{7,5},{8,10},{10,8},{9,1... | collective-permute-start | bytes 884744 | tf_op jit(solution)/shard_map/ppermute | solution.py:845
  674.6 17.7 %collective-permute-start.29 = (bf16[2,48,1536]{2,1,0:T(8,128)(2,1)S(1)}, bf16[2,48,1536]{2,1,0:T(8,128)(2,1)}, u32[]{:S(2)}, u32[]{:S(2)}) collective-permute-start(bf16[2,48,1536]{2,1,0:T(8,128)(2,1)S(1)} %copy-done.95), channel_id=1, source_target_pairs={{0,1},{1,0},{2,3},{3,2},{4,5},{5,4},{6,7},{7,6},{8,9},{9,8},{10,11... | collective-permute-start | bytes 884744 | tf_op jit(solution)/shard_map/ppermute | solution.py:845
  675.9 9.8 %collective-permute-start.41 = (f32[17,768]{1,0:T(8,128)S(1)}, f32[17,768]{1,0:T(8,128)S(1)}, u32[]{:S(2)}, u32[]{:S(2)}) collective-permute-start(f32[17,768]{1,0:T(8,128)S(1)} %add.279), channel_id=1, source_target_pairs={{0,16},{4,20},{8,24},{12,28},{16,0},{20,4},{24,8},{28,12},{1,17},{... | collective-permute-start | bytes 156680 | tf_op jit(solution)/shard_map/ppermute | solution.py:845
  677.7 9.0 %collective-permute-start.48 = (f32[17,768]{1,0:T(8,128)S(1)}, f32[17,768]{1,0:T(8,128)}, u32[]{:S(2)}, u32[]{:S(2)}) collective-permute-start(f32[17,768]{1,0:T(8,128)S(1)} %add.286), channel_id=1, source_target_pairs={{0,1},{1,0},{2,3},{3,2},{4,5},{5,4},{6,7},{7,6},{8,9},{9,8},{10,11... | collective-permute-start | bytes 156680 | tf_op jit(solution)/shard_map/ppermute | solution.py:845
  685.7 6.0 collective-permute-start.42
  691.7 6.9 collective-permute-start.43
  696.1 27.6 %collective-permute-start.32 = (bf16[2,2,48,1536]{3,2,1,0:T(8,128)(2,1)S(1)}, bf16[2,2,48,1536]{3,2,1,0:T(8,128)(2,1)S(1)}, u32[]{:S(2)}, u32[]{:S(2)}) collective-permute-start(bf16[2,2,48,1536]{3,2,1,0:T(8,128)(2,1)S(1)} %fusion.2), channel_id=1, source_target_pairs={{0,2},{2,0},{1,3},{3,1},{4,6},{6,4},{5,7},{7,5},{8,10},{10,8},{9,1... | collective-permute-start | bytes 1769480 | tf_op jit(solution)/shard_map/ppermute | solution.py:845
  697.6 26.1 %collective-permute-start.33 = (bf16[2,2,48,1536]{3,2,1,0:T(8,128)(2,1)S(1)}, bf16[2,2,48,1536]{3,2,1,0:T(8,128)(2,1)S(1)}, u32[]{:S(2)}, u32[]{:S(2)}) collective-permute-start(bf16[2,2,48,1536]{3,2,1,0:T(8,128)(2,1)S(1)} %fusion.3), channel_id=1, source_target_pairs={{0,1},{1,0},{2,3},{3,2},{4,5},{5,4},{6,7},{7,6},{8,9},{9,8},{10,11... | collective-permute-start | bytes 1769480 | tf_op jit(solution)/shard_map/ppermute | solution.py:845
  698.7 25.0 %collective-permute-start.31 = (bf16[2,48,1536]{2,1,0:T(8,128)(2,1)S(1)}, bf16[2,48,1536]{2,1,0:T(8,128)(2,1)S(1)}, u32[]{:S(2)}, u32[]{:S(2)}) collective-permute-start(bf16[2,48,1536]{2,1,0:T(8,128)(2,1)S(1)} %fusion.7), channel_id=1, source_target_pairs={{0,16},{4,20},{8,24},{12,28},{16,0},{20,4},{24,8},{28,12},{1,17},{... | collective-permute-start | bytes 884744 | tf_op jit(solution)/shard_map/ppermute | solution.py:845
  727.3 9.1 %collective-permute-start.35 = (bf16[2,48,1536]{2,1,0:T(8,128)(2,1)S(1)}, bf16[2,48,1536]{2,1,0:T(8,128)(2,1)}, u32[]{:S(2)}, u32[]{:S(2)}) collective-permute-start(bf16[2,48,1536]{2,1,0:T(8,128)(2,1)S(1)} %get-tuple-element.258), channel_id=1, source_target_pairs={{0,2},{2,0},{1,3},{3,1},{4,6},{6,4},{5,7},{7,5},{8,10},{10,8},{9,1... | collective-permute-start | bytes 884744 | tf_op jit(solution)/shard_map/ppermute | solution.py:845
  728.8 7.5 collective-permute-start.36
  730.9 5.5 collective-permute-start.34
  732.2 39.5 %copy-start.24 = (f32[4,208,768]{2,1,0:T(8,128)S(1)}, f32[4,208,768]{2,1,0:T(8,128)}, u32[]{:S(2)}) copy-start(f32[4,208,768]{2,1,0:T(8,128)} %copy-done.23) | copy-start | bytes 7667716
  738.4 26.7 %collective-permute-start.37 = (bf16[2,48,1536]{2,1,0:T(8,128)(2,1)}, bf16[2,48,1536]{2,1,0:T(8,128)(2,1)}, u32[]{:S(2)}, u32[]{:S(2)}) collective-permute-start(bf16[2,48,1536]{2,1,0:T(8,128)(2,1)} %fusion.4), channel_id=1, source_target_pairs={{0,16},{4,20},{8,24},{12,28},{16,0},{20,4},{24,8},{28,12},{1,17},{... | collective-permute-start | bytes 884744 | tf_op jit(solution)/shard_map/ppermute | solution.py:845
  766.4 5.2 collective-permute-start.38
  (100 other events, 837.5 us)
Sparse Core Ops, SparseCore 0:
  11.5 127.3 all-gather.3
  142.4 97.5 all-gather.5
  242.9 84.8 all-gather.7
  393.9 134.7 reduce-scatter.4
  536.0 230.1 reduce-scatter.2
